TPU v7x, 512 devices: a whole 4x8x8 slice. The times are simulated.
512 devices in a mesh: row: 8 (over z), au: 8 (over y), vert: 8 (over x, core).
Axes of the slice: x: 4, y: 8, z: 8, core: 2. Of those that a mesh axis runs over, the one named last changes fastest.
Arguments:
- velocity: float32 [32, 128, 2048], P('row', 'au', 'vert'), may hold values from -6 to 6
- log_visc: float32 [32, 128, 2048], P('row', 'au', 'vert'), may hold values from -3.45 to 3.45
- labels: int32 [128, 2048], P('au', 'vert'), may hold values from 0 to 511
- seg_dir: float32 [512], replicated, may hold values from -5 to 5
- layer_dir: float32 [32], P('row'), may hold values from -5 to 5
Outputs:
- increment: float32 [32, 128, 2048], P('row', 'au', 'vert')
- adjoint: float32 [32, 128, 2048], P('row', 'au', 'vert')
- hv_segments: float32 [512], replicated
- hv_layers: float32 [32], P('row')
All inputs are finite; a program needn't handle non-finite values.
Results may differ from a plain program's by a relative error of at most 0.000022.
Values sent between devices are 32-bit elements; how exact they have to be, the bound alone decides.
No kernel may reach another device: no remote copies, remote signals or barrier semaphores. Data moves between devices by JAX's collectives and lax.ppermute only.
A program may use at most 64 MiB of HBM per device.

v0:
```python
import jax
import jax.numpy as jnp
from jax import lax
from jax.sharding import PartitionSpec as P

NSEG = 512
SWEEPS = 2
COARSE_SWEEPS = 4


DAMPING = 0.7
COARSE_FACTOR = 0.25
DIRECTIONS = ((0, -1), (0, 1), (1, -1), (1, 1), (2, -1), (2, 1))


def extended(cells, sides, width):
    for axis, dim in sides:
        count = lax.axis_size(axis)
        ends = count - 1
        head = lax.slice_in_dim(cells, 0, width, axis=dim)
        tail = lax.slice_in_dim(cells, cells.shape[dim] - width, cells.shape[dim], axis=dim)
        cells = jnp.concatenate(
            [
                lax.ppermute(tail, axis, [(i, (i + 1) % count) for i in range(ends)]),
                cells,
                lax.ppermute(head, axis, [((i + 1) % count, i) for i in range(ends)]),
            ],
            axis=dim,
        )
    return cells


def neighbor(padded, dim_no, offset):
    slicers = [slice(1, -1), slice(1, -1), slice(1, -1)]
    slicers[dim_no] = slice(1 + offset, padded.shape[dim_no] - 1 + offset)
    return padded[tuple(slicers)]


def centre(padded):
    return padded[1:-1, 1:-1, 1:-1]


def inside_masks(extent, starts, totals):
    result = []
    for dim_no, offset in DIRECTIONS:
        global_at = starts[dim_no] + jnp.arange(extent[dim_no], dtype=jnp.int32) + offset
        inside = (global_at >= 0) & (global_at < totals[dim_no])
        layout = [1, 1, 1]
        layout[dim_no] = extent[dim_no]
        result.append(jnp.broadcast_to(inside.reshape(layout), tuple(extent)))
    return result


def face_weights(log_padded, masks_list, factor):
    middle = centre(log_padded)
    weights = []
    for number in range(6):
        dim_no, offset = DIRECTIONS[number]
        beside = neighbor(log_padded, dim_no, offset)
        weights.append(
            factor
            * jnp.where(masks_list[number], jnp.exp(0.5 * (middle + beside)), jnp.exp(middle))
        )
    return weights


def diagonal_of(weights):
    result = weights[0]
    for number in range(1, 6):
        result = result + weights[number]
    return result


def apply_operator(padded, weights):
    middle = centre(padded)
    result = weights[0] * (middle - neighbor(padded, 0, -1))
    for number in range(1, 6):
        dim_no, offset = DIRECTIONS[number]
        result = result + weights[number] * (middle - neighbor(padded, dim_no, offset))
    return result


def restrict(values):
    shaped = values.reshape(
        values.shape[0] // 2, 2, values.shape[1] // 2, 2, values.shape[2] // 2, 2
    )
    return jnp.sum(shaped, axis=(1, 3, 5)) * 0.125


def prolong(values):
    return jnp.repeat(jnp.repeat(jnp.repeat(values, 2, axis=0), 2, axis=1), 2, axis=2)


def jacobi(iterate, source, level):
    weights, diag_sum, pad_fn = level
    applied = apply_operator(pad_fn(iterate), weights)
    return iterate + DAMPING * (source - applied) / diag_sum


def depth_weight(row_ids, total_rows):
    return jnp.exp(-(total_rows - 1 - row_ids).astype(jnp.float32) / (total_rows / 4.0))


def forcing_term(vel_padded, step_padded, weights, masks_list):
    middle = centre(vel_padded)
    step_mid = centre(step_padded)
    result = jnp.zeros_like(middle)
    for number in range(6):
        dim_no, offset = DIRECTIONS[number]
        step_face = jnp.where(
            masks_list[number], 0.5 * (step_mid + neighbor(step_padded, dim_no, offset)), step_mid
        )
        result = result - weights[number] * step_face * (
            middle - neighbor(vel_padded, dim_no, offset)
        )
    return result


def density_term(vel_padded, adj_padded, weights, masks_list):
    vel_mid = centre(vel_padded)
    adj_mid = centre(adj_padded)
    result = jnp.zeros_like(vel_mid)
    for number in range(6):
        dim_no, offset = DIRECTIONS[number]
        halves = jnp.where(masks_list[number], 0.5, 1.0)
        result = result + halves * weights[number] * (
            neighbor(adj_padded, dim_no, offset) - adj_mid
        ) * (neighbor(vel_padded, dim_no, offset) - vel_mid)
    return result


def sweep_pad(values):
    return extended(values, (("row", 0), ("au", 1), ("vert", 2)), 1)


def residual_pad(values):
    return extended(values, (("row", 0), ("au", 1), ("vert", 2)), 1)


def coarse_pad(values):
    return extended(values, (("row", 0), ("au", 1), ("vert", 2)), 1)


def shards(velocity, log_visc, labels, seg_dir, layer_dir):
    rows_dev, across_dev, along_dev = velocity.shape
    total_rows = rows_dev * lax.axis_size("row")
    total_across = across_dev * lax.axis_size("au")
    total_along = along_dev * lax.axis_size("vert")
    row_start = lax.axis_index("row") * rows_dev
    across_start = lax.axis_index("au") * across_dev
    along_start = lax.axis_index("vert") * along_dev
    row_ids = row_start + jnp.arange(rows_dev, dtype=jnp.int32)
    depth_scale = depth_weight(row_ids, total_rows)
    log_step = seg_dir[labels][None, :, :] * depth_scale[:, None, None] + layer_dir[:, None, None]
    stacked = jnp.stack([velocity, log_visc, log_step])
    extent = velocity.shape
    starts = (row_start, across_start, along_start)
    totals = (total_rows, total_across, total_along)
    masks_list = inside_masks(extent, starts, totals)
    padded_all = extended(stacked, (("row", 1), ("au", 2), ("vert", 3)), 1)
    weights = face_weights(padded_all[1], masks_list, 1.0)
    fine_level = (weights, diagonal_of(weights), sweep_pad)

    def smooth_first(source):
        iterate = jnp.zeros_like(source)
        for sweep_no in range(SWEEPS):
            iterate = jacobi(iterate, source, fine_level)
        return (iterate, source)

    def smooth_last(iterate, source):
        for sweep_no in range(SWEEPS):
            iterate = jacobi(iterate, source, fine_level)
        return iterate

    vel_padded = padded_all[0]
    step_padded = padded_all[2]
    coarse_log = restrict(log_visc)
    coarse_starts = (row_start // 2, across_start // 2, along_start // 2)
    coarse_totals = (total_rows // 2, total_across // 2, total_along // 2)
    coarse_masks = inside_masks(coarse_log.shape, coarse_starts, coarse_totals)
    coarse_weights = face_weights(coarse_pad(coarse_log), coarse_masks, COARSE_FACTOR)
    coarse_level = (coarse_weights, diagonal_of(coarse_weights), coarse_pad)

    def vcycle(source):
        iterate, source_ext = smooth_first(source)
        leftover = source - apply_operator(residual_pad(iterate), weights)
        coarse_source = restrict(leftover)
        correction = jnp.zeros_like(coarse_source)
        for sweep_no in range(COARSE_SWEEPS):
            correction = jacobi(correction, coarse_source, coarse_level)
        iterate = iterate + prolong(correction)
        return smooth_last(iterate, source)

    source = forcing_term(vel_padded, step_padded, weights, masks_list)
    increment = vcycle(source)
    adjoint = vcycle(-increment)
    adj_padded = extended(adjoint, (("row", 0), ("au", 1), ("vert", 2)), 1)
    density = density_term(vel_padded, adj_padded, weights, masks_list)
    column = jnp.sum(depth_scale[:, None, None] * density, axis=0)
    seg_part = jax.ops.segment_sum(column.reshape(-1), labels.reshape(-1), num_segments=NSEG)
    layer_part = jnp.sum(density, axis=(1, 2))
    seg_total = lax.psum(seg_part, ("row", "au", "vert"))
    layer_total = lax.psum(layer_part, ("au", "vert"))
    seg_scale = 1.0 / (total_rows * total_across * total_along / NSEG) ** 0.5
    layer_scale = 1.0 / (total_across * total_along) ** 0.5
    return (increment, adjoint, seg_total * seg_scale, layer_total * layer_scale)


def solution(mesh):
    in_specs = (P("row", "au", "vert"), P("row", "au", "vert"), P("au", "vert"), P(), P("row"))
    out_specs = (P("row", "au", "vert"), P("row", "au", "vert"), P(), P("row"))
    return jax.shard_map(shards, mesh=mesh, in_specs=in_specs, out_specs=out_specs, check_vma=False)
```

profile of v0, /device:TPU:1, one launch (start us, length us, event | category | flops | bytes accessed | tf_op | source)
XLA Modules:
  0.0 767.0 jit_solution(4808202452328450242)
XLA Ops:
  0.7 4.8 collective-permute-start.6
  6.8 4.6 collective-permute-start.25
  13.6 25.8 %gather_fusion = f32[4096]{0:T(1024)S(1)} fusion(f32[512]{0:T(512)S(1)} %copy-done, s32[4096]{0:T(1024)S(1)} %broadcast_clamp_fusion), kind=kCustom, calls=%fused_computation | custom fusion | bytes 49152 | tf_op jit(solution)/shard_map/gather | solution.py:154
  39.5 4.6 collective-permute-start
  44.3 5.6 reshape.150
  53.8 5.8 collective-permute-start.24
  64.2 4.0 collective-permute-start.2
  72.9 6.8 collective-permute-start.4
  82.6 4.4 collective-permute-start.10
  93.2 4.9 collective-permute-start.12
  99.4 3.5 collective-permute-start.28
  104.2 5.5 collective-permute-start.14
  111.1 5.5 collective-permute-start.29
  118.0 3.5 collective-permute-start.16
  123.5 3.7 collective-permute-done.17
  127.3 5.5 collective-permute-start.18
  138.8 4.3 collective-permute-start.20
  144.4 3.3 collective-permute-done.21
  147.9 4.3 collective-permute-start.22
  154.2 3.6 collective-permute-start.33
  159.9 5.6 reshape.149
  168.2 5.5 collective-permute-start.36
  175.0 4.5 collective-permute-done.37
  179.5 4.0 collective-permute-start.38
  184.9 4.6 collective-permute-done.39
  189.5 5.9 collective-permute-start.40
  197.4 3.3 collective-permute-done.41
  200.8 4.8 collective-permute-start.42
  206.9 4.5 collective-permute-done.43
  211.5 4.8 collective-permute-start.44
  217.6 3.3 collective-permute-done.45
  221.0 4.2 collective-permute-start.46
  227.2 3.3 collective-permute-done.47
  230.6 4.8 collective-permute-start.48
  236.7 3.3 collective-permute-done.49
  240.1 3.6 collective-permute-start.50
  248.2 4.4 collective-permute-start.52
  254.6 3.3 collective-permute-done.53
  258.5 3.6 collective-permute-start.54
  270.8 3.4 collective-permute-done.57
  274.3 4.5 collective-permute-start.58
  280.7 3.7 collective-permute-done.59
  299.3 4.7 collective-permute-start.64
  305.9 3.7 collective-permute-done.65
  324.6 4.7 collective-permute-start.70
  331.3 3.7 collective-permute-done.71
  349.9 4.7 collective-permute-start.76
  356.5 3.7 collective-permute-done.77
  360.4 5.6 reshape.154
  383.1 4.7 collective-permute-start.82
  389.7 3.3 collective-permute-done.83
  407.6 4.8 collective-permute-start.88
  414.3 3.3 collective-permute-done.89
  432.2 4.8 collective-permute-start.94
  454.4 3.4 collective-permute-done.99
  457.8 4.5 collective-permute-start.100
  464.2 3.7 collective-permute-done.101
  482.8 4.7 collective-permute-start.106
  489.5 3.7 collective-permute-done.107
  508.1 4.7 collective-permute-start.112
  514.8 3.7 collective-permute-done.113
  518.9 28.8 %scatter_custom_fusion = f32[512]{0:T(512)S(1)} fusion(s32[4096]{0:T(1024)S(1)} %bitcast.38, f32[4096]{0:T(1024)S(1)} %bitcast.39, f32[]{:T(128)} %constant.28.clone.1), kind=kCustom, calls=%fused_computation.873 | custom fusion | flops 4096 | bytes 2052 | tf_op jit(solution)/shard_map/scatter-add | solution.py:200
  547.7 94.2 %psum.14 = f32[512]{0:T(512)S(1)} all-reduce(f32[512]{0:T(512)S(1)} %scatter_custom_fusion), channel_id=1, replica_groups=mesh['row'=8,'au'=8,'vert'=8] {'row','au','vert'}, use_global_device_ids=true, to_apply=%region_5.6 | all-reduce | flops 512 | bytes 4096 | tf_op jit(solution)/shard_map/psum | solution.py:202
  642.4 124.1 %psum.15 = f32[4]{0:T(128)S(1)} all-reduce(f32[4]{0:T(128)S(1)} %get-tuple-element.24), channel_id=1, replica_groups=mesh['row'=8,'au'=8,'vert'=8] {'au','vert'}, use_global_device_ids=true, to_apply=%region_7.8 | all-reduce | flops 4 | bytes 32 | tf_op jit(solution)/shard_map/psum | solution.py:203
  (318 shorter events, 229.8 us)
Async XLA Ops:
  0.7 51.8 %collective-permute-start.6 = (f32[1,16,256]{2,1,0:T(8,128)S(1)}, f32[1,16,256]{2,1,0:T(8,128)S(1)}, u32[]{:S(2)}, u32[]{:S(2)}) collective-permute-start(f32[1,16,256]{2,1,0:T(8,128)S(1)} %broadcast.369), channel_id=1, source_target_pairs={{0,64},{64,128},{128,192},{192,256},{256,320},{320,384},{384,448},... | collective-permute-start | bytes 49160 | tf_op jit(solution)/shard_map/ppermute | solution.py:24
  5.5 48.3 %collective-permute-start.7 = (f32[1,16,256]{2,1,0:T(8,128)S(1)}, f32[1,16,256]{2,1,0:T(8,128)S(1)}, u32[]{:S(2)}, u32[]{:S(2)}) collective-permute-start(f32[1,16,256]{2,1,0:T(8,128)S(1)} %broadcast.369), channel_id=1, source_target_pairs={{64,0},{128,64},{192,128},{256,192},{320,256},{384,320},{448,384},... | collective-permute-start | bytes 49160 | tf_op jit(solution)/shard_map/ppermute | solution.py:26
  6.8 102.9 %collective-permute-start.25 = (f32[1,8,128]{2,1,0:T(8,128)S(1)}, f32[1,8,128]{2,1,0:T(8,128)S(1)}, u32[]{:S(2)}, u32[]{:S(2)}) collective-permute-start(f32[1,8,128]{2,1,0:T(8,128)S(1)} %broadcast.378), channel_id=1, source_target_pairs={{0,64},{64,128},{128,192},{192,256},{256,320},{320,384},{384,448},... | collective-permute-start | bytes 12296 | tf_op jit(solution)/shard_map/ppermute | solution.py:24
  11.4 99.6 %collective-permute-start.27 = (f32[1,8,128]{2,1,0:T(8,128)S(1)}, f32[1,8,128]{2,1,0:T(8,128)S(1)}, u32[]{:S(2)}, u32[]{:S(2)}) collective-permute-start(f32[1,8,128]{2,1,0:T(8,128)S(1)} %broadcast.378), channel_id=1, source_target_pairs={{64,0},{128,64},{192,128},{256,192},{320,256},{384,320},{448,384},... | collective-permute-start | bytes 12296 | tf_op jit(solution)/shard_map/ppermute | solution.py:26
  39.5 20.1 %collective-permute-start = (f32[3,1,16,256]{3,2,1,0:T(8,128)S(1)}, f32[3,1,16,256]{3,2,1,0:T(8,128)S(1)}, u32[]{:S(2)}, u32[]{:S(2)}) collective-permute-start(f32[3,1,16,256]{3,2,1,0:T(8,128)S(1)} %get-tuple-element.51), channel_id=1, source_target_pairs={{0,64},{64,128},{128,192},{192,256},{256,320},{320,384},{384,448},... | collective-permute-start | bytes 147464 | tf_op jit(solution)/shard_map/ppermute | solution.py:24
  52.5 10.4 %collective-permute-start.1 = (f32[3,1,16,256]{3,2,1,0:T(8,128)S(1)}, f32[3,1,16,256]{3,2,1,0:T(8,128)S(1)}, u32[]{:S(2)}, u32[]{:S(2)}) collective-permute-start(f32[3,1,16,256]{3,2,1,0:T(8,128)S(1)} %get-tuple-element.52), channel_id=1, source_target_pairs={{64,0},{128,64},{192,128},{256,192},{320,256},{384,320},{448,384},... | collective-permute-start | bytes 147464 | tf_op jit(solution)/shard_map/ppermute | solution.py:26
  53.8 44.2 %collective-permute-start.24 = (f32[1,8,128]{2,1,0:T(8,128)S(1)}, f32[1,8,128]{2,1,0:T(8,128)S(1)}, u32[]{:S(2)}, u32[]{:S(2)}) collective-permute-start(f32[1,8,128]{2,1,0:T(8,128)S(1)} %get-tuple-element.155), channel_id=1, source_target_pairs={{0,64},{64,128},{128,192},{192,256},{256,320},{320,384},{384,448},... | collective-permute-start | bytes 12296 | tf_op jit(solution)/shard_map/ppermute | solution.py:24
  62.9 5.3 collective-permute-start.9
  64.2 5.3 collective-permute-start.2
  72.9 9.7 %collective-permute-start.4 = (f32[3,6,18,1]{3,2,1,0:T(8,128)S(1)}, f32[3,6,18,1]{3,2,1,0:T(8,128)S(1)}, u32[]{:S(2)}, u32[]{:S(2)}) collective-permute-start(f32[3,6,18,1]{3,2,1,0:T(8,128)S(1)} %get-tuple-element.47), channel_id=1, source_target_pairs={{0,1},{1,2},{2,3},{3,4},{4,5},{5,6},{6,7},{8,9},{9,10},{10,11},{11... | collective-permute-start | bytes 3896 | tf_op jit(solution)/shard_map/ppermute | solution.py:24
  79.7 7.3 collective-permute-start.5
  82.6 6.8 collective-permute-start.10
  87.0 5.7 collective-permute-start.11
  89.4 9.9 %collective-permute-start.26 = (f32[1,8,128]{2,1,0:T(8,128)S(1)}, f32[1,8,128]{2,1,0:T(8,128)S(1)}, u32[]{:S(2)}, u32[]{:S(2)}) collective-permute-start(f32[1,8,128]{2,1,0:T(8,128)S(1)} %get-tuple-element.156), channel_id=1, source_target_pairs={{64,0},{128,64},{192,128},{256,192},{320,256},{384,320},{448,384},... | collective-permute-start | bytes 12296 | tf_op jit(solution)/shard_map/ppermute | solution.py:26
  93.2 9.8 %collective-permute-start.12 = (f32[1,16,256]{2,1,0:T(8,128)S(1)}, f32[1,16,256]{2,1,0:T(8,128)S(1)}, u32[]{:S(2)}, u32[]{:S(2)}) collective-permute-start(f32[1,16,256]{2,1,0:T(8,128)S(1)} %get-tuple-element.109), channel_id=1, source_target_pairs={{0,64},{64,128},{128,192},{192,256},{256,320},{320,384},{384,448},... | collective-permute-start | bytes 49160 | tf_op jit(solution)/shard_map/ppermute | solution.py:24
  98.0 6.2 collective-permute-start.13
  99.4 22.1 %collective-permute-start.28 = (f32[4,1,128]{2,1,0:T(1,128)S(1)}, f32[4,1,128]{2,1,0:T(1,128)S(1)}, u32[]{:S(2)}, u32[]{:S(2)}) collective-permute-start(f32[4,1,128]{2,1,0:T(1,128)S(1)} %get-tuple-element.140), channel_id=1, source_target_pairs={{0,8},{8,16},{16,24},{24,32},{32,40},{40,48},{48,56},{1,9},{9,17},... | collective-permute-start | bytes 6152 | tf_op jit(solution)/shard_map/ppermute | solution.py:24
  102.9 20.5 %collective-permute-start.30 = (f32[4,1,128]{2,1,0:T(1,128)S(1)}, f32[4,1,128]{2,1,0:T(1,128)S(1)}, u32[]{:S(2)}, u32[]{:S(2)}) collective-permute-start(f32[4,1,128]{2,1,0:T(1,128)S(1)} %get-tuple-element.139), channel_id=1, source_target_pairs={{8,0},{16,8},{24,16},{32,24},{40,32},{48,40},{56,48},{9,1},{17,9},... | collective-permute-start | bytes 6152 | tf_op jit(solution)/shard_map/ppermute | solution.py:26
  104.2 12.3 %collective-permute-start.14 = (f32[6,1,256]{2,1,0:T(1,128)S(1)}, f32[6,1,256]{2,1,0:T(1,128)S(1)}, u32[]{:S(2)}, u32[]{:S(2)}) collective-permute-start(f32[6,1,256]{2,1,0:T(1,128)S(1)} %get-tuple-element.89), channel_id=1, source_target_pairs={{0,8},{8,16},{16,24},{24,32},{32,40},{40,48},{48,56},{1,9},{9,17},... | collective-permute-start | bytes 18440 | tf_op jit(solution)/shard_map/ppermute | solution.py:24
  109.7 8.1 %collective-permute-start.15 = (f32[6,1,256]{2,1,0:T(1,128)S(1)}, f32[6,1,256]{2,1,0:T(1,128)S(1)}, u32[]{:S(2)}, u32[]{:S(2)}) collective-permute-start(f32[6,1,256]{2,1,0:T(1,128)S(1)} %get-tuple-element.90), channel_id=1, source_target_pairs={{8,0},{16,8},{24,16},{32,24},{40,32},{48,40},{56,48},{9,1},{17,9},... | collective-permute-start | bytes 18440 | tf_op jit(solution)/shard_map/ppermute | solution.py:26
  111.1 32.0 %collective-permute-start.29 = (f32[4,1,128]{2,1,0:T(1,128)S(1)}, f32[4,1,128]{2,1,0:T(1,128)S(1)}, u32[]{:S(2)}, u32[]{:S(2)}) collective-permute-start(f32[4,1,128]{2,1,0:T(1,128)S(1)} %get-tuple-element.141), channel_id=1, source_target_pairs={{0,8},{8,16},{16,24},{24,32},{32,40},{40,48},{48,56},{1,9},{9,17},... | collective-permute-start | bytes 6152 | tf_op jit(solution)/shard_map/ppermute | solution.py:24
  116.6 27.8 %collective-permute-start.31 = (f32[4,1,128]{2,1,0:T(1,128)S(1)}, f32[4,1,128]{2,1,0:T(1,128)S(1)}, u32[]{:S(2)}, u32[]{:S(2)}) collective-permute-start(f32[4,1,128]{2,1,0:T(1,128)S(1)} %get-tuple-element.142), channel_id=1, source_target_pairs={{8,0},{16,8},{24,16},{32,24},{40,32},{48,40},{56,48},{9,1},{17,9},... | collective-permute-start | bytes 6152 | tf_op jit(solution)/shard_map/ppermute | solution.py:26
  118.0 5.4 collective-permute-start.16
  121.5 5.7 collective-permute-start.17
  127.3 9.0 %collective-permute-start.18 = (f32[1,16,256]{2,1,0:T(8,128)S(1)}, f32[1,16,256]{2,1,0:T(8,128)S(1)}, u32[]{:S(2)}, u32[]{:S(2)}) collective-permute-start(f32[1,16,256]{2,1,0:T(8,128)S(1)} %get-tuple-element.107), channel_id=1, source_target_pairs={{0,64},{64,128},{128,192},{192,256},{256,320},{320,384},{384,448},... | collective-permute-start | bytes 49160 | tf_op jit(solution)/shard_map/ppermute | solution.py:24
  132.8 6.0 collective-permute-start.19
  134.2 33.9 %collective-permute-start.32 = (f32[4,10,1]{2,1,0:T(8,128)S(1)}, f32[4,10,1]{2,1,0:T(8,128)S(1)}, u32[]{:S(2)}, u32[]{:S(2)}) collective-permute-start(f32[4,10,1]{2,1,0:T(8,128)S(1)} %get-tuple-element.124), channel_id=1, source_target_pairs={{0,1},{1,2},{2,3},{3,4},{4,5},{5,6},{6,7},{8,9},{9,10},{10,11},{11... | collective-permute-start | bytes 488 | tf_op jit(solution)/shard_map/ppermute | solution.py:24
  136.3 31.7 %collective-permute-start.34 = (f32[4,10,1]{2,1,0:T(8,128)S(1)}, f32[4,10,1]{2,1,0:T(8,128)S(1)}, u32[]{:S(2)}, u32[]{:S(2)}) collective-permute-start(f32[4,10,1]{2,1,0:T(8,128)S(1)} %get-tuple-element.123), channel_id=1, source_target_pairs={{1,0},{2,1},{3,2},{4,3},{5,4},{6,5},{7,6},{9,8},{10,9},{11,10},{12... | collective-permute-start | bytes 488 | tf_op jit(solution)/shard_map/ppermute | solution.py:26
  138.8 5.6 collective-permute-start.20
  147.9 10.0 %collective-permute-start.22 = (f32[6,18,1]{2,1,0:T(8,128)S(1)}, f32[6,18,1]{2,1,0:T(8,128)S(1)}, u32[]{:S(2)}, u32[]{:S(2)}) collective-permute-start(f32[6,18,1]{2,1,0:T(8,128)S(1)} %get-tuple-element.67), channel_id=1, source_target_pairs={{0,1},{1,2},{2,3},{3,4},{4,5},{5,6},{6,7},{8,9},{9,10},{10,11},{11... | collective-permute-start | bytes 1304 | tf_op jit(solution)/shard_map/ppermute | solution.py:24
  152.2 7.6 collective-permute-start.23
  154.2 13.9 %collective-permute-start.33 = (f32[4,10,1]{2,1,0:T(8,128)S(1)}, f32[4,10,1]{2,1,0:T(8,128)S(1)}, u32[]{:S(2)}, u32[]{:S(2)}) collective-permute-start(f32[4,10,1]{2,1,0:T(8,128)S(1)} %get-tuple-element.125), channel_id=1, source_target_pairs={{0,1},{1,2},{2,3},{3,4},{4,5},{5,6},{6,7},{8,9},{9,10},{10,11},{11... | collective-permute-start | bytes 488 | tf_op jit(solution)/shard_map/ppermute | solution.py:24
  157.8 10.2 %collective-permute-start.35 = (f32[4,10,1]{2,1,0:T(8,128)S(1)}, f32[4,10,1]{2,1,0:T(8,128)S(1)}, u32[]{:S(2)}, u32[]{:S(2)}) collective-permute-start(f32[4,10,1]{2,1,0:T(8,128)S(1)} %get-tuple-element.126), channel_id=1, source_target_pairs={{1,0},{2,1},{3,2},{4,3},{5,4},{6,5},{7,6},{9,8},{10,9},{11,10},{12... | collective-permute-start | bytes 488 | tf_op jit(solution)/shard_map/ppermute | solution.py:26
  168.2 6.8 collective-permute-start.36
  173.7 5.8 collective-permute-start.37
  179.5 5.4 collective-permute-start.38
  183.6 5.9 collective-permute-start.39
  189.5 7.8 %collective-permute-start.40 = (f32[4,10,1]{2,1,0:T(8,128)S(1)}, f32[4,10,1]{2,1,0:T(8,128)S(1)}, u32[]{:S(2)}, u32[]{:S(2)}) collective-permute-start(f32[4,10,1]{2,1,0:T(8,128)S(1)} %get-tuple-element.121), channel_id=1, source_target_pairs={{0,1},{1,2},{2,3},{3,4},{4,5},{5,6},{6,7},{8,9},{9,10},{10,11},{11... | collective-permute-start | bytes 488 | tf_op jit(solution)/shard_map/ppermute | solution.py:24
  195.4 5.2 collective-permute-start.41
  200.8 6.2 collective-permute-start.42
  205.6 5.8 collective-permute-start.43
  211.5 6.1 collective-permute-start.44
  221.0 6.1 collective-permute-start.46
  225.2 5.2 collective-permute-start.47
  230.6 6.2 collective-permute-start.48
  248.2 6.4 collective-permute-start.52
  252.6 5.2 collective-permute-start.53
  274.3 6.4 collective-permute-start.58
  278.7 5.7 collective-permute-start.59
  299.3 6.7 collective-permute-start.64
  304.0 5.7 collective-permute-start.65
  324.6 6.7 collective-permute-start.70
  329.3 5.7 collective-permute-start.71
  349.9 6.7 collective-permute-start.76
  354.6 5.7 collective-permute-start.77
  383.1 6.6 collective-permute-start.82
  407.6 6.7 collective-permute-start.88
  432.2 6.7 collective-permute-start.94
  457.8 6.4 collective-permute-start.100
  462.3 5.7 collective-permute-start.101
  482.8 6.7 collective-permute-start.106
  487.6 5.7 collective-permute-start.107
  508.1 6.7 collective-permute-start.112
  512.8 5.7 collective-permute-start.113
  (57 other events, 914.8 us)
where the time goes:
time: 770 us; the launch traced here: 767 us
  starting transfers between devices  314 us (41%)
  blocking collectives  218 us (28%)
  waiting for transfers between devices  145 us (19%)
  local copies, waits for them, and re-layouts  45.3 us (6%)
  other arithmetic  42.1 us (5%)
    ppermute x57, starting transfers between devices, extended(): lax.ppermute(tail, axis, [(i, (i + 1) % count) for i in range(ends)])  228 us
    ppermute x57, waiting for transfers between devices, extended(): lax.ppermute(head, axis, [((i + 1) % count, i) for i in range(ends)])  144 us
    psum x1, blocking collectives, shards(): layer_total = lax.psum(layer_part, ('au', 'vert'))  124 us
    psum x1, blocking collectives, shards(): seg_total = lax.psum(seg_part, ('row', 'au', 'vert'))  94.2 us
    ppermute x57, starting transfers between devices, extended(): lax.ppermute(head, axis, [((i + 1) % count, i) for i in range(ends)])  86 us
    scatter-add x1, other arithmetic, shards(): jax.ops.segment_sum(column.reshape(-1), labels.reshape(-1), num_segments=...  28.8 us
    gather x2, local copies, waits for them, and re-layouts, shards(): seg_dir[labels][None, :, :] * depth_scale[:, None, None]  25.9 us
    reshape x3, local copies, waits for them, and re-layouts, restrict(): values.reshape(values.shape[0] // 2, 2, values.shape[1] // 2, 2, values.s...  16.8 us
  transfers between devices with their start and end apart: 114, of which 45 were waited for; matrix products, arithmetic and copies ran while one was open for 6% of the time, Pallas kernels for 0%

commit v1 on v0

v1 whole, which is shorter than its diff:
```python
import jax
import jax.numpy as jnp
from jax import lax
from jax.experimental import pallas as pl
from jax.experimental.pallas import tpu as pltpu
from jax.sharding import PartitionSpec as P

NSEG = 512
DAMPING = 0.7
KEEP = 1.0 - DAMPING
COARSE_FACTOR = 0.25

LAYERS = 32
OWN = 16
HALO = 12
WINDOW = OWN + 2 * HALO
PART = 32
MARGIN = 24
SPAN = PART + 2 * MARGIN
LANES = 128
TOP = 8
PAD_ROWS = WINDOW + 2 * TOP
TILES = 40
F32 = jnp.float32
VMEM_LIMIT = 48 * 1024 * 1024


def lanes_of(shape):
    return lax.broadcasted_iota(jnp.int32, shape, len(shape) - 1)


def turn(values, amount):
    return pltpu.roll(values, amount % LANES, values.ndim - 1)


def call(kernel, outs, scratch=()):
    return pl.pallas_call(
        kernel,
        out_shape=outs,
        scratch_shapes=list(scratch),
        compiler_params=pltpu.CompilerParams(vmem_limit_bytes=VMEM_LIMIT),
    )


def sds(*shape):
    return jax.ShapeDtypeStruct(shape, F32)


def edge_kernel(vel, log, lab, seg, left, right, plate):
    for top in (0, 8):
        for half in range(2):
            labels = lab[top : top + 8, half * LANES : (half + 1) * LANES]
            low = labels & 127
            high = labels >> 7
            value = jnp.zeros((8, LANES), F32)
            for part in range(4):
                table = jnp.broadcast_to(seg[part : part + 1, :], (8, LANES))
                got = jnp.take_along_axis(table, low, axis=1, mode="promise_in_bounds")
                value = jnp.where(high == part, got, value)
            plate[top : top + 8, half * LANES : (half + 1) * LANES] = value
    slot = lanes_of((OWN, LANES)) // PART
    for group, field in enumerate((vel, log)):
        first = field[0, :, 0:LANES]
        last = turn(field[0, :, LANES : 2 * LANES], MARGIN)
        for row in range(1, 4):
            first = jnp.where(slot == row, turn(field[row, :, 0:LANES], PART * row), first)
            last = jnp.where(slot == row, turn(field[row, :, LANES : 2 * LANES], PART * row + MARGIN), last)
        left[group] = first
        right[group] = last
    left[2] = plate[:, 0:LANES]
    right[2] = turn(plate[:, LANES : 2 * LANES], MARGIN)


def stretched(first, second, before, after, row):
    lane = lanes_of(first.shape)
    head = lane < MARGIN
    first = turn(first, MARGIN)
    second = turn(second, MARGIN)
    return (
        jnp.where(head, turn(before, -PART * row), first),
        jnp.where(head, first, second),
        jnp.where(head, second, turn(after, MARGIN - PART * row)),
    )


def window_kernel(vel, log, lab, plate, before, after, layer, send, plate_window, label_window):
    lane = lanes_of((OWN, LANES))
    for group, field in enumerate((vel, log)):
        for row in range(4):
            slab = group * 4 + row
            tiles = stretched(
                field[row, :, 0:LANES], field[row, :, LANES : 2 * LANES], before[group], after[group], row
            )
            for part in range(8):
                base, shift = part // 4, PART * (part % 4)
                if shift:
                    wide = jnp.where(
                        lane < LANES - shift, turn(tiles[base], -shift), turn(tiles[base + 1], -shift)
                    )
                else:
                    wide = tiles[base]
                if group == 0:
                    wide = jnp.where(lane == SPAN - 1, layer[row], wide)
                start = 64 * (slab % 2)
                send[part, slab // 2, :, start : start + 64] = wide[:, 0:64]
                send[part, 4, :, 16 * slab : 16 * slab + 16] = wide[:, 64:80]
    part = lax.axis_index("row")
    shift = PART * (part % 4)
    tiles = stretched(plate[:, 0:LANES], plate[:, LANES : 2 * LANES], before[2], after[2], 0)
    late = part >= 4
    here = jnp.where(late, tiles[1], tiles[0])
    there = jnp.where(late, tiles[2], tiles[1])
    back = (LANES - shift) % LANES
    plate_window[...] = jnp.where(lane < LANES - shift, pltpu.roll(here, back, 1), pltpu.roll(there, back, 1))
    labels = jnp.where(late, lab[:, LANES : 2 * LANES], lab[:, 0:LANES])
    label_window[...] = pltpu.roll(labels, (LANES + MARGIN - shift) % LANES, 1)


def rows_kernel(got, plate_window, up, down):
    def tile(index):
        if index < TILES:
            return got[index // 5, index % 5]
        return plate_window[...]

    for index in range(TILES + 1):
        values = tile(index)
        at = TILES + 1 + index // 2
        half = 4 * (index % 2)
        up[index] = values[8:16]
        down[index] = values[0:8]
        up[at, half : half + 4, :] = values[4:8]
        down[at, half : half + 4, :] = values[8:12]


def rows_of(index, up, down, total):
    at = total + index // 2
    half = 4 * (index % 2)
    return up[at, half : half + 4, :], up[index], down[index], down[at, half : half + 4, :]


def places():
    row_at = lax.broadcasted_iota(jnp.int32, (WINDOW, LANES), 0)
    lane = lanes_of((WINDOW, LANES))
    across = row_at + (lax.axis_index("au") * OWN - HALO)
    along = lane + (lax.axis_index("vert") * (8 * PART) + lax.axis_index("row") * PART - MARGIN)
    across_end = lax.axis_size("au") * OWN
    along_end = lax.axis_size("vert") * 8 * PART
    domain = (across >= 0) & (across < across_end) & (along >= 0) & (along < along_end) & (lane < SPAN)
    return row_at, lane, across, along, across_end, along_end, domain


def middle(ref, at):
    return ref[at, TOP : TOP + WINDOW, :]


def four(ref, at, reach=1):
    centre = middle(ref, at)
    return (
        centre,
        ref[at, TOP - reach : TOP - reach + WINDOW, :],
        ref[at, TOP + reach : TOP + reach + WINDOW, :],
        turn(centre, reach),
        turn(centre, -reach),
    )


def around(ref, at, reach=1):
    centre, low, high, left, right = four(ref, at, reach)
    total = (low + high) + (left + right)
    return centre, total + (middle(ref, at - 1) + middle(ref, at + 1))


def pair_sum(values, even_row, even_lane):
    shaped = values.reshape(WINDOW // 8, 8, LANES)
    partner = jnp.where(even_row, pltpu.roll(shaped, 7, 1), pltpu.roll(shaped, 1, 1))
    shaped = shaped + partner
    partner = jnp.where(even_lane, turn(shaped, -1), turn(shaped, 1))
    return (shaped + partner).reshape(WINDOW, LANES)


def parities():
    shape = (WINDOW // 8, 8, LANES)
    return lax.broadcasted_iota(jnp.int32, shape, 1) % 2 == 0, lanes_of(shape) % 2 == 0


def clear_edges(refs):
    for ref in refs:
        last = ref.shape[0] - 1
        zero = jnp.zeros((TOP, LANES), F32)
        zeros = jnp.zeros((PAD_ROWS, LANES), F32)
        ref[0] = zeros
        ref[last] = zeros

        def clear(at, _, ref=ref, zero=zero):
            ref[at, 0:TOP, :] = zero
            ref[at, TOP + WINDOW : PAD_ROWS, :] = zero
            return 0

        lax.fori_loop(1, last, clear, 0)


def loop(count, body, unroll=2):
    def step(at, _):
        body(at)
        return 0

    lax.fori_loop(0, count, step, 0, unroll=unroll)


def smooth(out, values, source, factor, count, reach, first=False):
    def body(at):
        centre, total = around(values, at + 1, reach)
        if first:
            out[at + 1, TOP : TOP + WINDOW, :] = (1.0 + KEEP) * centre + factor[at] * total
        else:
            out[at + 1, TOP : TOP + WINDOW, :] = (
                KEEP * centre + middle(source, at + 1) + factor[at] * total
            )

    loop(count, body)


def vcycle(f, one, two, zf, za, zb, g, c, big, cc, kc, ginv):
    even_row, even_lane = parities()
    smooth(two, f, None, c, LAYERS, 1, first=True)

    def leftover(at):
        centre, total = around(two, at + 1)
        return big[at] * ((middle(f, at + 1) - DAMPING * centre) + c[at] * total)

    def down(at):
        total = leftover(2 * at) + leftover(2 * at + 1)
        zf[at + 1, TOP : TOP + WINDOW, :] = kc[at] * pair_sum(total, even_row, even_lane)

    loop(LAYERS // 2, down, 1)
    smooth(za, zf, None, cc, LAYERS // 2, 2, first=True)
    smooth(zb, za, zf, cc, LAYERS // 2, 2)
    smooth(za, zb, zf, cc, LAYERS // 2, 2)

    def up(at):
        value = middle(za, at + 1) * ginv[at]
        for row in range(2):
            one[2 * at + row + 1, TOP : TOP + WINDOW, :] = (
                middle(two, 2 * at + row + 1) + middle(g, 2 * at + row + 1) * value
            )

    loop(LAYERS // 2, up)
    smooth(two, one, f, c, LAYERS, 1)
    smooth(one, two, f, c, LAYERS, 1)


def depth_at(at):
    place = jnp.zeros((8, LANES), jnp.int32) + at
    return jnp.exp(-(LAYERS - 1 - place).astype(F32) / (LAYERS / 4.0))


def tall(values):
    return jnp.concatenate([values] * (WINDOW // 8), axis=0)


def first_kernel(
    got, plate_window, from_low, from_high,
    g, c, big, cc, kc, ginv, vel, f_own, f_up, f_down, inc,
    packed, f, one, two, zf, za, zb, layer, gc,
):
    row_at, lane, across, along, across_end, along_end, domain = places()
    clear_edges((f, one, two, zf, za, zb, vel, g, gc))
    for index in range(TILES + 1):
        a, b, d, e = rows_of(index, from_low, from_high, TILES + 1)
        packed[index, 0:4, :] = a
        packed[index, 4:12, :] = b
        packed[index, 12:28, :] = got[index // 5, index % 5] if index < TILES else plate_window[...]
        packed[index, 28:36, :] = d
        packed[index, 36:40, :] = e

    short, span = lane < 64, lane < SPAN

    def slab_of(source, slab):
        head = packed[source * 5 + slab // 2]
        if slab % 2:
            head = turn(head, 64)
        tail = turn(packed[source * 5 + 4], 64 - 16 * slab)
        return jnp.where(short, head, jnp.where(span, tail, 0.0))

    def unpack(source):
        for row in range(4):
            at = source * 4 + row + 1
            speed = slab_of(source, row)
            layer[at] = jnp.broadcast_to(speed[16:24, SPAN - 1 : SPAN], (8, LANES))
            vel[at, TOP : TOP + WINDOW, :] = jnp.where(domain, speed, 0.0)
            one[at, TOP : TOP + WINDOW, :] = slab_of(source, 4 + row)

    loop(8, unpack, 1)
    layer[0] = layer[1]
    layer[LAYERS + 1] = layer[LAYERS]

    def replicated(ref, at, reach):
        centre, low, high, left, right = four(ref, at, reach)
        centre = jnp.where((across >= -reach) & (across < 0), high, centre)
        centre = jnp.where((across >= across_end) & (across < across_end + reach), low, centre)
        centre = jnp.where((along >= -reach) & (along < 0), right, centre)
        return jnp.where((along >= along_end) & (along < along_end + reach), left, centre)

    even_row, even_lane = parities()

    def coarse_log(at):
        total = middle(one, 2 * at + 1) + middle(one, 2 * at + 2)
        zb[at + 1, TOP : TOP + WINDOW, :] = pair_sum(total, even_row, even_lane) * 0.125
        for row in range(2):
            g[2 * at + row + 1, TOP : TOP + WINDOW, :] = jnp.exp(0.5 * replicated(one, 2 * at + row + 1, 1))

    loop(LAYERS // 2, coarse_log, 1)

    def coarse_g(at):
        gc[at + 1, TOP : TOP + WINDOW, :] = jnp.exp(0.5 * replicated(zb, at + 1, 2))

    loop(LAYERS // 2, coarse_g)
    g[0] = g[1]
    g[LAYERS + 1] = g[LAYERS]
    gc[0] = gc[1]
    gc[LAYERS // 2 + 1] = gc[LAYERS // 2]

    def coarse_factors(at):
        centre, total = around(gc, at + 1, 2)
        per = 1.0 / total
        cc[at] = jnp.where(domain, DAMPING * centre * per, 0.0)
        kc[at] = jnp.where(domain, (DAMPING / COARSE_FACTOR * 0.125) * per, 0.0)
        ginv[at] = 1.0 / centre

    loop(LAYERS // 2, coarse_factors)

    one[1, TOP : TOP + WINDOW, :] = packed[TILES]
    one[1, TOP : TOP + WINDOW, :] = replicated(one, 1, 1)
    plate, *beside = four(one, 1)
    beside = [plate + other for other in beside]

    def forcing(at):
        g_mid, *g_four = four(g, at + 1)
        v_mid, *v_four = four(vel, at + 1)
        depth = depth_at(at)
        level = layer[at + 1]
        depth_tall, twice = tall(depth), tall(2.0 * level)
        total_g = (g_four[0] + g_four[1]) + (g_four[2] + g_four[3])
        total = jnp.zeros((WINDOW, LANES), F32)
        for g_n, v_n, s_n in zip(g_four, v_four, beside):
            total = total + g_n * (depth_tall * s_n + twice) * (v_mid - v_n)
        for other in (at, at + 2):
            place = jnp.clip(other - 1, 0, LAYERS - 1)
            g_n = middle(g, other)
            total_g = total_g + g_n
            scale = tall(depth + depth_at(place)) * plate + tall(level + layer[other])
            total = total + g_n * scale * (v_mid - middle(vel, other))
        per = jnp.where(domain, DAMPING / total_g, 0.0)
        c[at] = g_mid * per
        big[at] = total_g * (1.0 / DAMPING)
        f[at + 1, TOP : TOP + WINDOW, :] = -0.5 * g_mid * total * per

    loop(LAYERS, forcing, 1)
    vcycle(f, one, two, zf, za, zb, g, c, big, cc, kc, ginv)

    own_lane = lanes_of((OWN, LANES))
    slot = own_lane // PART

    def finish(part):
        tile = jnp.zeros((OWN, LANES), F32)
        sent = []
        for row in range(4):
            at = 4 * part + row
            y = one[at + 1, TOP + HALO : TOP + HALO + OWN, :]
            x = y / g[at + 1, TOP + HALO : TOP + HALO + OWN, :]
            tile = jnp.where(slot == row, turn(x, PART * row - MARGIN), tile)
            nxt = -x / big[at, HALO : HALO + OWN, :]
            f_own[at] = nxt
            sent.append(nxt)
        inc[part] = tile
        for pair in range(2):
            both = jnp.where(own_lane < 64, turn(sent[2 * pair], -8), turn(sent[2 * pair + 1], 56))
            index = 2 * part + pair
            f_up[index] = both[8:16]
            f_down[index] = both[0:8]
            f_up[16 + part, 4 * pair : 4 * pair + 4, :] = both[4:8]
            f_down[16 + part, 4 * pair : 4 * pair + 4, :] = both[8:12]

    loop(8, finish, 1)


def second_kernel(
    g, c, big, cc, kc, ginv, vel, f_own, from_low, from_high, inc, label_window,
    send,
    f, one, two, zf, za, zb, rows, column, layers,
):
    row_at, lane, across, along, across_end, along_end, domain = places()
    clear_edges((f, one, two, zf, za, zb))
    half = lane < 64

    def unpack(part):
        for pair in range(2):
            index = 2 * part + pair
            rows[0:4, :] = from_low[16 + part, 4 * pair : 4 * pair + 4, :]
            rows[4:12, :] = from_low[index]
            rows[28:36, :] = from_high[index]
            rows[36:40, :] = from_high[16 + part, 4 * pair : 4 * pair + 4, :]
            both = rows[...]
            for row, shift in ((0, 8), (1, 72)):
                at = 4 * part + 2 * pair + row
                here = turn(both, shift)
                here = jnp.where(domain, here, 0.0)
                f[at + 1, TOP : TOP + WINDOW, :] = here
                f[at + 1, TOP + HALO : TOP + HALO + OWN, :] = f_own[at]

    rows[...] = jnp.zeros((WINDOW, LANES), F32)
    loop(8, unpack, 1)
    vcycle(f, one, two, zf, za, zb, g, c, big, cc, kc, ginv)

    def adjoint(at):
        two[at + 1, TOP : TOP + WINDOW, :] = middle(one, at + 1) / middle(g, at + 1)

    loop(LAYERS, adjoint)
    own = (row_at >= HALO) & (row_at < HALO + OWN) & (lane >= MARGIN) & (lane < MARGIN + PART)
    a_low = jnp.where(across == 0, 1.0, 0.5)
    a_high = jnp.where(across == across_end - 1, 1.0, 0.5)
    v_low = jnp.where(along == 0, 1.0, 0.5)
    v_high = jnp.where(along == along_end - 1, 1.0, 0.5)
    column[...] = jnp.zeros((WINDOW, LANES), F32)

    def density(at):
        g_mid, *g_four = four(g, at + 1)
        v_mid, *v_four = four(vel, at + 1)
        x_mid, *x_four = four(two, at + 1)
        total = jnp.zeros((WINDOW, LANES), F32)
        for h, g_n, v_n, x_n in zip((a_low, a_high, v_low, v_high), g_four, v_four, x_four):
            total = total + h * g_n * (x_n - x_mid) * (v_n - v_mid)
        for other, end in ((at, 0), (at + 2, LAYERS + 1)):
            h = jnp.where(other == end, 1.0, 0.5)
            total = total + h * middle(g, other) * (middle(two, other) - x_mid) * (middle(vel, other) - v_mid)
        total = jnp.where(own, g_mid * total, 0.0)
        column[...] += tall(depth_at(at)) * total
        folded = jnp.sum(total.reshape(WINDOW // 8, 8, LANES), axis=0)
        layers[pl.ds(at, 1), :] = jnp.sum(folded, axis=0, keepdims=True)

    loop(LAYERS, density, 1)

    labels = label_window[...]
    high, low = labels >> 7, labels & 127
    sums = column[HALO : HALO + OWN, :]
    kind = lax.broadcasted_iota(jnp.int32, (4, LANES), 0)
    place = lax.broadcasted_iota(jnp.int32, (LANES, LANES), 0)
    left, right = [], []
    for at in range(OWN):
        value = jnp.where(high[at : at + 1, :] == kind, sums[at : at + 1, :], 0.0)
        top = value.astype(jnp.bfloat16).astype(F32)
        rest = value - top
        mid = rest.astype(jnp.bfloat16).astype(F32)
        left.append(jnp.concatenate([top, mid, rest - mid, jnp.zeros_like(top)], axis=0).astype(jnp.bfloat16))
        right.append(jnp.where(low[at : at + 1, :] == place, 1.0, 0.0).astype(jnp.bfloat16))
    product = lax.dot_general(
        jnp.concatenate(left, axis=1),
        jnp.concatenate(right, axis=1),
        (((1,), (1,)), ((), ())),
        preferred_element_type=F32,
    )
    segments = (product[0:4] + product[4:8]) + product[8:12]

    slot = lanes_of((OWN, LANES)) // PART

    def pack(part):
        tile = jnp.zeros((OWN, LANES), F32)
        for row in range(4):
            x = two[4 * part + row + 1, TOP + HALO : TOP + HALO + OWN, :]
            tile = jnp.where(slot == row, turn(x, PART * row - MARGIN), tile)
        send[part, 0:16, :] = inc[part]
        send[part, 16:32, :] = tile
        send[part, 32:36, :] = segments
        send[part, 36:40, :] = layers[pl.ds(4 * part, 4), :]

    loop(8, pack, 1)


def place_kernel(got, inc, adj, spread):
    lane = lanes_of((OWN, LANES))
    slot = lane // PART
    for out, start in ((inc, 0), (adj, 16)):
        for row in range(4):
            for half in range(2):
                tile = jnp.zeros((OWN, LANES), F32)
                for source in range(4):
                    piece = got[4 * half + source, start : start + 16, :]
                    tile = jnp.where(slot == source, turn(piece, PART * (source - row)), tile)
                out[row, :, half * LANES : (half + 1) * LANES] = tile
    total = got[0, 32:40, :]
    for source in range(1, 8):
        total = total + got[source, 32:40, :]
    for other in range(64):
        spread[other] = total


def shards(velocity, log_visc, labels, seg_dir, layer_dir):
    vert = lax.axis_size("vert")
    across = lax.axis_size("au")
    ahead = [(i, (i + 1) % vert) for i in range(vert)]
    back = [((i + 1) % vert, i) for i in range(vert)]
    upward = [(i, (i + 1) % across) for i in range(across)]
    downward = [((i + 1) % across, i) for i in range(across)]

    left, right, plate = call(edge_kernel, (sds(3, OWN, LANES), sds(3, OWN, LANES), sds(OWN, 2 * LANES)))(
        velocity, log_visc, labels, seg_dir.reshape(4, LANES)
    )
    before = lax.ppermute(right, "vert", ahead)
    after = lax.ppermute(left, "vert", back)
    vmem = pl.BlockSpec(memory_space=pltpu.VMEM)
    send, plate_window, label_window = pl.pallas_call(
        window_kernel,
        out_shape=(sds(8, 5, OWN, LANES), sds(OWN, LANES), jax.ShapeDtypeStruct((OWN, LANES), jnp.int32)),
        in_specs=[vmem] * 6 + [pl.BlockSpec(memory_space=pltpu.SMEM)],
        compiler_params=pltpu.CompilerParams(vmem_limit_bytes=VMEM_LIMIT),
    )(velocity, log_visc, labels, plate, before, after, layer_dir)
    got = lax.all_to_all(send, "row", 0, 0, tiled=True)
    up, down = call(rows_kernel, (sds(62, 8, LANES), sds(62, 8, LANES)))(got, plate_window)
    from_low = lax.ppermute(up, "au", upward)
    from_high = lax.ppermute(down, "au", downward)
    fine = sds(LAYERS, WINDOW, LANES)
    fine_padded = sds(LAYERS + 2, PAD_ROWS, LANES)
    coarse = sds(LAYERS // 2, WINDOW, LANES)
    fine_scratch = pltpu.VMEM((LAYERS + 2, PAD_ROWS, LANES), F32)
    coarse_scratch = pltpu.VMEM((LAYERS // 2 + 2, PAD_ROWS, LANES), F32)
    window_scratch = pltpu.VMEM((WINDOW, LANES), F32)
    *factors, f_own, f_up, f_down, inc = call(
        first_kernel,
        (fine_padded, fine, fine, coarse, coarse, coarse, fine_padded)
        + (sds(LAYERS, OWN, LANES), sds(24, 8, LANES), sds(24, 8, LANES), sds(8, OWN, LANES)),
        [pltpu.VMEM((TILES + 1, WINDOW, LANES), F32)]
        + [fine_scratch] * 3
        + [coarse_scratch] * 3
        + [pltpu.VMEM((LAYERS + 2, 8, LANES), F32), coarse_scratch],
    )(got, plate_window, from_low, from_high)
    from_low = lax.ppermute(f_up, "au", upward)
    from_high = lax.ppermute(f_down, "au", downward)
    send = call(
        second_kernel,
        sds(8, 40, LANES),
        [fine_scratch] * 3
        + [coarse_scratch] * 3
        + [window_scratch, window_scratch, pltpu.VMEM((LAYERS, LANES), F32)],
    )(*factors, f_own, from_low, from_high, inc, label_window)
    got = lax.all_to_all(send, "row", 0, 0, tiled=True)
    field = sds(4, OWN, 8 * PART)
    increment, adjoint, spread = call(place_kernel, (field, field, sds(64, 8, LANES)))(got)
    parts = lax.all_to_all(spread, ("au", "vert"), 0, 0, tiled=True)
    total = jnp.sum(parts, axis=0)
    total_rows = LAYERS
    total_across = across * OWN
    total_along = vert * 8 * PART
    seg_scale = 1.0 / (total_rows * total_across * total_along / NSEG) ** 0.5
    layer_scale = 1.0 / (total_across * total_along) ** 0.5
    hv_segments = total[0:4].reshape(NSEG) * seg_scale
    hv_layers = jnp.sum(total[4:8], axis=1) * layer_scale
    return increment, adjoint, hv_segments, hv_layers


def solution(mesh):
    in_specs = (P("row", "au", "vert"), P("row", "au", "vert"), P("au", "vert"), P(), P("row"))
    out_specs = (P("row", "au", "vert"), P("row", "au", "vert"), P(), P("row"))
    return jax.shard_map(shards, mesh=mesh, in_specs=in_specs, out_specs=out_specs, check_vma=False)
```

time: 770 us -> 132 us (0.17)
  starting transfers between devices: 314 us -> 21.2 us
  blocking collectives: 218 us -> 58.7 us
  waiting for transfers between devices: 145 us -> 7.72 us
  local copies, waits for them, and re-layouts: 45.3 us -> 3.07 us
  other arithmetic: 42.1 us -> 1.28 us
  Pallas kernels: 0 us -> 39 us
    ppermute x114 -> x6, starting transfers between devices: 314 us -> 21.2 us  [the longest x1 4.3 us: shards(): after = lax.ppermute(left, 'vert', back)]
    psum x2 -> x0, blocking collectives: 218 us -> none  [the longest x1 124 us: shards(): layer_total = lax.psum(layer_part, ('au', 'vert'))]
    ppermute x114 -> x6, waiting for transfers between devices: 145 us -> 7.72 us  [the longest x1 3.41 us: shards(): from_low = lax.ppermute(up, 'au', upward)]
    all_to_all x0 -> x3, blocking collectives: none -> 58.7 us  [the longest x2 31.7 us: shards(): got = lax.all_to_all(send, 'row', 0, 0, tiled=True)]
    pallas_call x0 -> x6, Pallas kernels: none -> 39 us  [the longest x1 19.6 us: shards(): call(first_kernel, (fine_padded, fine, fine, coarse, coarse, coarse, fine...]
    scatter-add x1 -> x0, other arithmetic: 28.8 us -> none  [shards(): jax.ops.segment_sum(column.reshape(-1), labels.reshape(-1), num_segments=...]
    gather x2 -> x0, local copies, waits for them, and re-layouts: 25.9 us -> none  [shards(): seg_dir[labels][None, :, :] * depth_scale[:, None, None]]
    reshape x7 -> x0, local copies, waits for them, and re-layouts: 17.3 us -> none  [the longest x3 16.8 us: restrict(): values.reshape(values.shape[0] // 2, 2, values.shape[1] // 2, 2, values.s...]
  transfers between devices with their start and end apart: 114 -> 6, of which waited for: 45 -> 6; matrix products, arithmetic and copies ran while one was open for 6% -> 0% of each run, Pallas kernels for 0% -> 0%
where the time goes in v1:
time: 132 us
  blocking collectives  58.7 us (44%)
  Pallas kernels  39 us (30%)
  starting transfers between devices  21.2 us (16%)
  waiting for transfers between devices  7.72 us (6%)
  local copies, waits for them, and re-layouts  3.07 us (2%)
    all_to_all x2, blocking collectives, shards(): got = lax.all_to_all(send, 'row', 0, 0, tiled=True)  31.7 us
    all_to_all x1, blocking collectives, shards(): parts = lax.all_to_all(spread, ('au', 'vert'), 0, 0, tiled=True)  26.9 us
    pallas_call x1, Pallas kernels, shards(): call(first_kernel, (fine_padded, fine, fine, coarse, coarse, coarse, fine...  19.6 us
    pallas_call x1, Pallas kernels, shards(): call(second_kernel, sds(8, 40, LANES), [fine_scratch] * 3 + [coarse_scrat...  15.8 us
    ppermute x1, starting transfers between devices, shards(): after = lax.ppermute(left, 'vert', back)  4.3 us
    ppermute x1, starting transfers between devices, shards(): from_high = lax.ppermute(f_down, 'au', downward)  4.02 us
    ppermute x1, starting transfers between devices, shards(): from_high = lax.ppermute(down, 'au', downward)  3.81 us
    ppermute x1, waiting for transfers between devices, shards(): from_low = lax.ppermute(up, 'au', upward)  3.41 us
  transfers between devices with their start and end apart: 6, of which 6 were waited for; matrix products, arithmetic and copies ran while one was open for 0% of the time, Pallas kernels for 0%

profile of v1, /device:TPU:1, one launch (start us, length us, event | category | flops | bytes accessed | tf_op | source)
XLA Modules:
  0.0 131.6 jit_solution(10559886678024787356)
XLA Ops:
  0.6 0.0 copy-start
  0.6 0.8 copy-done
  1.5 0.0 copy-start.1
  1.5 0.8 copy-done.1
  2.3 0.0 copy-start.2
  2.3 0.7 copy-done.2
  3.0 0.0 copy-start.3
  3.0 0.7 copy-done.3
  3.7 0.1 shard_map.84
  3.9 2.6 %collective-permute-start = (f32[3,16,128]{2,1,0:T(8,128)S(1)}, f32[3,16,128]{2,1,0:T(8,128)S(1)}, u32[]{:S(2)}, u32[]{:S(2)}) collective-permute-start(f32[3,16,128]{2,1,0:T(8,128)S(1)} %get-tuple-element.27), channel_id=1, source_target_pairs={{0,1},{1,2},{2,3},{3,4},{4,5},{5,6},{6,7},{7,0},{8,9},{9,10},{10,1... | collective-permute-start | bytes 73736 | tf_op jit(solution)/shard_map/ppermute | solution.py:508
  6.5 0.0 copy-start.4
  6.5 4.3 %collective-permute-start.1 = (f32[3,16,128]{2,1,0:T(8,128)S(1)}, f32[3,16,128]{2,1,0:T(8,128)S(1)}, u32[]{:S(2)}, u32[]{:S(2)}) collective-permute-start(f32[3,16,128]{2,1,0:T(8,128)S(1)} %get-tuple-element.28), channel_id=1, source_target_pairs={{1,0},{2,1},{3,2},{4,3},{5,4},{6,5},{7,6},{0,7},{9,8},{10,9},{11,1... | collective-permute-start | bytes 73736 | tf_op jit(solution)/shard_map/ppermute | solution.py:509
  10.8 0.7 collective-permute-done.before
  11.4 0.2 collective-permute-done.1.after
  11.6 0.0 copy-done.4
  11.6 2.6 %shard_map.85 = (f32[8,5,16,128]{3,2,1,0:T(8,128)S(1)}, f32[16,128]{1,0:T(8,128)S(1)}, s32[16,128]{1,0:T(8,128)S(1)}) custom-call(f32[4,16,256]{2,1,0:T(8,128)S(1)} %copy-done, f32[4,16,256]{2,1,0:T(8,128)S(1)} %copy-done.1, s32[16,256]{1,0:T(8,128)S(1)} %copy-done.2, f32[16,256]{1,0:T(8,128)S(1)} %get-tuple-element.26.plate, ...), custom_call_target="tpu_custom_call" | custom-call | tf_op jit(solution)/shard_map/pallas_call | solution.py:511
  14.2 21.1 %all_to_all.15.got = f32[8,5,16,128]{3,2,1,0:T(8,128)S(1)} all-to-all(f32[8,5,16,128]{3,2,1,0:T(8,128)S(1)} %get-tuple-element.29), channel_id=1, replica_groups=mesh['row'=8,'au'=8,'vert'=8] {'row'}, dimensions={0} | all-to-all | bytes 655360 | tf_op jit(solution)/shard_map/all_to_all | solution.py:517
  35.4 3.2 %collective-permute-start.2 = (f32[62,8,128]{2,1,0:T(8,128)S(1)}, f32[62,8,128]{2,1,0:T(8,128)S(1)}, u32[]{:S(2)}, u32[]{:S(2)}) collective-permute-start(f32[62,8,128]{2,1,0:T(8,128)S(1)} %get-tuple-element.31), channel_id=1, source_target_pairs={{0,8},{8,16},{16,24},{24,32},{32,40},{40,48},{48,56},{56,0},{1,9},... | collective-permute-start | bytes 761864 | tf_op jit(solution)/shard_map/ppermute | solution.py:519
  38.6 3.8 %collective-permute-start.3 = (f32[62,8,128]{2,1,0:T(8,128)S(1)}, f32[62,8,128]{2,1,0:T(8,128)S(1)}, u32[]{:S(2)}, u32[]{:S(2)}) collective-permute-start(f32[62,8,128]{2,1,0:T(8,128)S(1)} %get-tuple-element.32), channel_id=1, source_target_pairs={{8,0},{16,8},{24,16},{32,24},{40,32},{48,40},{56,48},{0,56},{9,1},... | collective-permute-start | bytes 761864 | tf_op jit(solution)/shard_map/ppermute | solution.py:520
  42.4 3.4 %collective-permute-done.2.from_low = f32[62,8,128]{2,1,0:T(8,128)S(1)} collective-permute-done((f32[62,8,128]{2,1,0:T(8,128)S(1)}, f32[62,8,128]{2,1,0:T(8,128)S(1)}, u32[]{:S(2)}, u32[]{:S(2)}) %collective-permute-start.2) | collective-permute-done | bytes 253984 | tf_op jit(solution)/shard_map/ppermute | solution.py:519
  45.8 0.9 collective-permute-done.3.from_high
  46.7 19.6 %shard_map.87 = (f32[34,56,128]{2,1,0:T(8,128)S(1)}, f32[32,40,128]{2,1,0:T(8,128)S(1)}, f32[32,40,128]{2,1,0:T(8,128)S(1)}, f32[16,40,128]{2,1,0:T(8,128)S(1)},...) custom-call(f32[8,5,16,128]{3,2,1,0:T(8,128)S(1)} %all_to_all.15.got, ...), custom_call_target="tpu_custom_call" | custom-call | tf_op jit(solution)/shard_map/pallas_call | solution.py:527
  66.3 3.2 %collective-permute-start.4 = (f32[24,8,128]{2,1,0:T(8,128)S(1)}, f32[24,8,128]{2,1,0:T(8,128)S(1)}, u32[]{:S(2)}, u32[]{:S(2)}) collective-permute-start(f32[24,8,128]{2,1,0:T(8,128)S(1)} %get-tuple-element.41), channel_id=1, source_target_pairs={{0,8},{8,16},{16,24},{24,32},{32,40},{40,48},{48,56},{56,0},{1,9},... | collective-permute-start | bytes 294920 | tf_op jit(solution)/shard_map/ppermute | solution.py:536
  69.6 4.0 %collective-permute-start.5 = (f32[24,8,128]{2,1,0:T(8,128)S(1)}, f32[24,8,128]{2,1,0:T(8,128)S(1)}, u32[]{:S(2)}, u32[]{:S(2)}) collective-permute-start(f32[24,8,128]{2,1,0:T(8,128)S(1)} %get-tuple-element.42), channel_id=1, source_target_pairs={{8,0},{16,8},{24,16},{32,24},{40,32},{48,40},{56,48},{0,56},{9,1},... | collective-permute-start | bytes 294920 | tf_op jit(solution)/shard_map/ppermute | solution.py:537
  73.6 0.1 collective-permute-done.4.from_low
  73.6 2.5 %collective-permute-done.5.from_high = f32[24,8,128]{2,1,0:T(8,128)S(1)} collective-permute-done((f32[24,8,128]{2,1,0:T(8,128)S(1)}, f32[24,8,128]{2,1,0:T(8,128)S(1)}, u32[]{:S(2)}, u32[]{:S(2)}) %collective-permute-start.5) | collective-permute-done | bytes 98336 | tf_op jit(solution)/shard_map/ppermute | solution.py:537
  76.2 15.8 %shard_map.88 = f32[8,40,128]{2,1,0:T(8,128)S(1)} custom-call(f32[34,56,128]{2,1,0:T(8,128)S(1)} %get-tuple-element.33.g, f32[32,40,128]{2,1,0:T(8,128)S(1)} %get-tuple-element.34.c, f32[32,40,128]{2,1,0:T(8,128)S(1)} %get-tuple-element.35.big, f32[16,40,128]{2,1,0:T(8,128)S(1)} %get-tuple-element.36.cc, f32[16,40,128]{2,1,0:T(8,128)S(1)} %get-tuple-element.37.kc, ...), custom_call_target="tpu_custom_call" | custom-call | tf_op jit(solution)/shard_map/pallas_call | solution.py:538
  91.9 10.7 %all_to_all.16.got = f32[8,40,128]{2,1,0:T(8,128)S(1)} all-to-all(f32[8,40,128]{2,1,0:T(8,128)S(1)} %shard_map.88), channel_id=1, replica_groups=mesh['row'=8,'au'=8,'vert'=8] {'row'}, dimensions={0} | all-to-all | bytes 327680 | tf_op jit(solution)/shard_map/all_to_all | solution.py:545
  102.6 0.8 shard_map.89
  103.4 26.9 %all_to_all.17 = f32[64,8,128]{2,1,0:T(8,128)S(1)} all-to-all(f32[64,8,128]{2,1,0:T(8,128)S(1)} %get-tuple-element.47), channel_id=1, replica_groups=mesh['row'=8,'au'=8,'vert'=8] {'au','vert'}, dimensions={0} | all-to-all | bytes 524288 | tf_op jit(solution)/shard_map/all_to_all | solution.py:548
  130.3 0.1 reduce_sum.18
  130.4 0.7 slice_reduce_fusion
  131.1 0.5 broadcast_multiply_fusion
  (1 shorter events, 0.0 us)
Async XLA Ops:
  0.6 0.8 copy-start
  1.5 0.8 copy-start.1
  2.3 0.7 copy-start.2
  3.0 0.7 copy-start.3
  3.9 7.6 %collective-permute-start = (f32[3,16,128]{2,1,0:T(8,128)S(1)}, f32[3,16,128]{2,1,0:T(8,128)S(1)}, u32[]{:S(2)}, u32[]{:S(2)}) collective-permute-start(f32[3,16,128]{2,1,0:T(8,128)S(1)} %get-tuple-element.27), channel_id=1, source_target_pairs={{0,1},{1,2},{2,3},{3,4},{4,5},{5,6},{6,7},{7,0},{8,9},{9,10},{10,1... | collective-permute-start | bytes 73736 | tf_op jit(solution)/shard_map/ppermute | solution.py:508
  6.5 5.2 %copy-start.4 = (f32[4]{0:T(128)S(1)}, f32[4]{0:T(128)}, u32[]{:S(2)}) copy-start(f32[4]{0:T(128)} %layer.1) | copy-start | bytes 52
  6.5 5.2 %collective-permute-start.1 = (f32[3,16,128]{2,1,0:T(8,128)S(1)}, f32[3,16,128]{2,1,0:T(8,128)S(1)}, u32[]{:S(2)}, u32[]{:S(2)}) collective-permute-start(f32[3,16,128]{2,1,0:T(8,128)S(1)} %get-tuple-element.28), channel_id=1, source_target_pairs={{1,0},{2,1},{3,2},{4,3},{5,4},{6,5},{7,6},{0,7},{9,8},{10,9},{11,1... | collective-permute-start | bytes 73736 | tf_op jit(solution)/shard_map/ppermute | solution.py:509
  35.4 10.4 %collective-permute-start.2 = (f32[62,8,128]{2,1,0:T(8,128)S(1)}, f32[62,8,128]{2,1,0:T(8,128)S(1)}, u32[]{:S(2)}, u32[]{:S(2)}) collective-permute-start(f32[62,8,128]{2,1,0:T(8,128)S(1)} %get-tuple-element.31), channel_id=1, source_target_pairs={{0,8},{8,16},{16,24},{24,32},{32,40},{40,48},{48,56},{56,0},{1,9},... | collective-permute-start | bytes 761864 | tf_op jit(solution)/shard_map/ppermute | solution.py:519
  38.6 8.1 %collective-permute-start.3 = (f32[62,8,128]{2,1,0:T(8,128)S(1)}, f32[62,8,128]{2,1,0:T(8,128)S(1)}, u32[]{:S(2)}, u32[]{:S(2)}) collective-permute-start(f32[62,8,128]{2,1,0:T(8,128)S(1)} %get-tuple-element.32), channel_id=1, source_target_pairs={{8,0},{16,8},{24,16},{32,24},{40,32},{48,40},{56,48},{0,56},{9,1},... | collective-permute-start | bytes 761864 | tf_op jit(solution)/shard_map/ppermute | solution.py:520
  66.3 7.3 %collective-permute-start.4 = (f32[24,8,128]{2,1,0:T(8,128)S(1)}, f32[24,8,128]{2,1,0:T(8,128)S(1)}, u32[]{:S(2)}, u32[]{:S(2)}) collective-permute-start(f32[24,8,128]{2,1,0:T(8,128)S(1)} %get-tuple-element.41), channel_id=1, source_target_pairs={{0,8},{8,16},{16,24},{24,32},{32,40},{40,48},{48,56},{56,0},{1,9},... | collective-permute-start | bytes 294920 | tf_op jit(solution)/shard_map/ppermute | solution.py:536
  69.6 6.6 %collective-permute-start.5 = (f32[24,8,128]{2,1,0:T(8,128)S(1)}, f32[24,8,128]{2,1,0:T(8,128)S(1)}, u32[]{:S(2)}, u32[]{:S(2)}) collective-permute-start(f32[24,8,128]{2,1,0:T(8,128)S(1)} %get-tuple-element.42), channel_id=1, source_target_pairs={{8,0},{16,8},{24,16},{32,24},{40,32},{48,40},{56,48},{0,56},{9,1},... | collective-permute-start | bytes 294920 | tf_op jit(solution)/shard_map/ppermute | solution.py:537

commit v2 on v1

v2 whole, which is shorter than its diff:
```python
import jax
import jax.numpy as jnp
from jax import lax
from jax.experimental import pallas as pl
from jax.experimental.pallas import tpu as pltpu
from jax.sharding import PartitionSpec as P

NSEG = 512
DAMPING = 0.7
KEEP = 1.0 - DAMPING
COARSE_FACTOR = 0.25

LAYERS = 32
OWN = 16
HALO = 12
WINDOW = OWN + 2 * HALO
PART = 32
MARGIN = 24
SPAN = PART + 2 * MARGIN
LANES = 128
TOP = 8
HALF = WINDOW // 2
HALF_ROWS = 40
PAD_ROWS = WINDOW + 2 * TOP
TILES = 40
F32 = jnp.float32
VMEM_LIMIT = 48 * 1024 * 1024


def lanes_of(shape):
    return lax.broadcasted_iota(jnp.int32, shape, len(shape) - 1)


def turn(values, amount):
    return pltpu.roll(values, amount % LANES, values.ndim - 1)


def call(kernel, outs, scratch=(), **more):
    return pl.pallas_call(
        kernel,
        out_shape=outs,
        **more,
        scratch_shapes=list(scratch),
        compiler_params=pltpu.CompilerParams(vmem_limit_bytes=VMEM_LIMIT),
    )


def sds(*shape):
    return jax.ShapeDtypeStruct(shape, F32)


def edge_kernel(vel_in, log_in, lab_in, seg_in, left, right, plate, vel, log, lab, seg, sems):
    copies = [
        pltpu.make_async_copy(source, target, sems.at[number])
        for number, (source, target) in enumerate(((vel_in, vel), (log_in, log), (lab_in, lab), (seg_in, seg)))
    ]
    for copy in copies:
        copy.start()
    for copy in copies:
        copy.wait()
    for top in (0, 8):
        for half in range(2):
            labels = lab[top : top + 8, half * LANES : (half + 1) * LANES]
            low = labels & 127
            high = labels >> 7
            value = jnp.zeros((8, LANES), F32)
            for part in range(4):
                table = jnp.broadcast_to(seg[part : part + 1, :], (8, LANES))
                got = jnp.take_along_axis(table, low, axis=1, mode="promise_in_bounds")
                value = jnp.where(high == part, got, value)
            plate[top : top + 8, half * LANES : (half + 1) * LANES] = value
    slot = lanes_of((OWN, LANES)) // PART
    for group, field in enumerate((vel, log)):
        first = field[0, :, 0:LANES]
        last = turn(field[0, :, LANES : 2 * LANES], MARGIN)
        for row in range(1, 4):
            first = jnp.where(slot == row, turn(field[row, :, 0:LANES], PART * row), first)
            last = jnp.where(slot == row, turn(field[row, :, LANES : 2 * LANES], PART * row + MARGIN), last)
        left[group] = first
        right[group] = last
    left[2] = plate[:, 0:LANES]
    right[2] = turn(plate[:, LANES : 2 * LANES], MARGIN)


PIECES = (
    ((0, 0, 0, 80),),
    ((1, 0, 0, 80),),
    ((2, 0, 0, 80),),
    ((3, 0, 0, 80),),
    ((4, 0, 0, 80),),
    ((0, 80, 0, 48), (1, 80, 48, 32)),
    ((1, 112, 0, 16), (2, 80, 16, 48), (3, 80, 64, 16)),
    ((3, 96, 0, 32), (4, 80, 32, 48)),
)


def window_kernel(vel, log, layer, send):
    lane = lanes_of((OWN, LANES))
    turned = {}

    def at(slab, half, amount):
        key = (slab, half, amount % LANES)
        if key not in turned:
            field = (vel, log)[slab // 4]
            turned[key] = turn(field[slab % 4, :, half * LANES : (half + 1) * LANES], amount)
        return turned[key]

    for part in range(8):
        tiles = [None] * 5
        for slab, pieces in enumerate(PIECES):
            for tile, start, first, count in pieces:
                shift = start - first
                amount = MARGIN - PART * part + shift
                edge = LANES + MARGIN - PART * part + shift
                if edge >= start + count:
                    wide = at(slab, 0, amount)
                elif edge <= start:
                    wide = at(slab, 1, amount)
                else:
                    wide = jnp.where(lane < edge, at(slab, 0, amount), at(slab, 1, amount))
                if slab < 4:
                    wide = jnp.where(lane == SPAN - 1, layer[slab], wide)
                if tiles[tile] is None:
                    tiles[tile] = wide
                else:
                    tiles[tile] = jnp.where((lane >= start) & (lane < start + count), wide, tiles[tile])
        for tile in range(5):
            send[part, tile] = tiles[tile]


def patch_kernel(sent, plate, lab, left, right, from_left, from_right, send, plate_window, label_window):
    lane = lanes_of((OWN, LANES))
    place = lane % PART
    first = lax.axis_index("vert") == 0
    last = lax.axis_index("vert") == lax.axis_size("vert") - 1
    before, after = [], []
    for group in range(3):
        low, high = from_left[group], from_right[group]
        if group == 0:
            low_inner = jnp.where(place >= MARGIN - 2, 0.0, low)
            high_inner = jnp.where(place < 2, 0.0, high)
        else:
            low_inner = jnp.where(place == MARGIN - 1, turn(left[group], MARGIN - 1), low)
            low_inner = jnp.where(place == MARGIN - 2, turn(left[group], MARGIN - 3), low_inner)
            high_inner = jnp.where(place == 0, turn(right[group], 1 - MARGIN), high)
            high_inner = jnp.where(place == 1, turn(right[group], 3 - MARGIN), high_inner)
        before.append(jnp.where(first, low_inner, low))
        after.append(jnp.where(last, high_inner, high))
    for part in range(1, 7):
        send[part] = sent[part]
    for part, edges, begin, stop in ((0, before, 0, MARGIN), (7, after, SPAN - MARGIN, SPAN)):
        tiles = [sent[part, tile] for tile in range(5)]
        for slab, pieces in enumerate(PIECES):
            group, row = slab // 4, slab % 4
            end = SPAN - 1 if group == 0 and stop == SPAN else stop
            for tile, start, head, count in pieces:
                low, high = max(begin, head), min(end, head + count)
                if low >= high:
                    continue
                shift = start - head
                moved = turn(edges[group], shift + begin - PART * row)
                tiles[tile] = jnp.where((lane >= low + shift) & (lane < high + shift), moved, tiles[tile])
        for tile in range(5):
            send[part, tile] = tiles[tile]
    part = lax.axis_index("row")
    shift = PART * (part % 4)
    one, two = turn(plate[:, 0:LANES], MARGIN), turn(plate[:, LANES : 2 * LANES], MARGIN)
    head = lane < MARGIN
    tiles = (
        jnp.where(head, before[2], one),
        jnp.where(head, one, two),
        jnp.where(head, two, turn(after[2], MARGIN)),
    )
    late = part >= 4
    here = jnp.where(late, tiles[1], tiles[0])
    there = jnp.where(late, tiles[2], tiles[1])
    back = (LANES - shift) % LANES
    plate_window[...] = jnp.where(lane < LANES - shift, pltpu.roll(here, back, 1), pltpu.roll(there, back, 1))
    labels = jnp.where(late, lab[:, LANES : 2 * LANES], lab[:, 0:LANES])
    label_window[...] = pltpu.roll(labels, (LANES + MARGIN - shift) % LANES, 1)


def rows_kernel(got, plate_window, up, down):
    def tile(index):
        if index < TILES:
            return got[index // 5, index % 5]
        return plate_window[...]

    for index in range(TILES + 1):
        values = tile(index)
        at = TILES + 1 + index // 2
        half = 4 * (index % 2)
        up[index] = values[8:16]
        down[index] = values[0:8]
        up[at, half : half + 4, :] = values[4:8]
        down[at, half : half + 4, :] = values[8:12]


def rows_of(index, up, down, total):
    at = total + index // 2
    half = 4 * (index % 2)
    return up[at, half : half + 4, :], up[index], down[index], down[at, half : half + 4, :]


def places(rows=WINDOW):
    step = WINDOW // rows
    row_at = lax.broadcasted_iota(jnp.int32, (rows, LANES), 0)
    lane = lanes_of((rows, LANES))
    across = step * row_at + (lax.axis_index("au") * OWN - HALO)
    along = lane + (lax.axis_index("vert") * (8 * PART) + lax.axis_index("row") * PART - MARGIN)
    across_end = lax.axis_size("au") * OWN
    along_end = lax.axis_size("vert") * 8 * PART
    domain = (across >= 0) & (across < across_end) & (along >= 0) & (along < along_end) & (lane < SPAN)
    return row_at, lane, across, along, across_end, along_end, domain


def middle(ref, at, rows=WINDOW, top=TOP):
    return ref[at, top : top + rows, :]


def four(ref, at, rows=WINDOW, reach=1, top=TOP):
    centre = middle(ref, at, rows, top)
    return (
        centre,
        ref[at, top - 1 : top - 1 + rows, :],
        ref[at, top + 1 : top + 1 + rows, :],
        turn(centre, reach),
        turn(centre, -reach),
    )


def around(ref, at, rows=WINDOW, reach=1):
    centre, low, high, left, right = four(ref, at, rows, reach)
    total = (low + high) + (left + right)
    return centre, total + (middle(ref, at - 1, rows) + middle(ref, at + 1, rows))


def pair_sum(values, spare, even_lane):
    spare[...] = values
    total = spare[pl.ds(0, HALF, 2), :] + spare[pl.ds(1, HALF, 2), :]
    return total + jnp.where(even_lane, turn(total, -1), turn(total, 1))


def clear_edges(refs, rows=WINDOW):
    row = jnp.zeros((1, LANES), F32)
    slab = jnp.zeros((rows, LANES), F32)
    for ref in refs:
        last = ref.shape[0] - 1
        for at in range(1, last):
            ref[at, TOP - 1 : TOP, :] = row
            ref[at, TOP + rows : TOP + rows + 1, :] = row
        ref[0, TOP : TOP + rows, :] = slab
        ref[last, TOP : TOP + rows, :] = slab


def smooth(out, values, source, factor, count, rows=WINDOW, reach=1):
    for at in range(count):
        centre, total = around(values, at + 1, rows, reach)
        if source is None:
            result = (1.0 + KEEP) * centre + factor[at] * total
        else:
            result = (KEEP * centre + middle(source, at + 1, rows)) + factor[at] * total
        out[at + 1, TOP : TOP + rows, :] = result


def vcycle(f, one, two, zf, za, zb, spare, g, c, big, cc, kc, ginv):
    even_lane = lanes_of((HALF, LANES)) % 2 == 0
    coarse = (LAYERS // 2, HALF, 2)
    smooth(two, f, None, c, LAYERS)

    def leftover(at):
        centre, total = around(two, at + 1)
        return big[at] * ((middle(f, at + 1) - DAMPING * centre) + c[at] * total)

    for at in range(LAYERS // 2):
        total = leftover(2 * at) + leftover(2 * at + 1)
        zf[at + 1, TOP : TOP + HALF, :] = kc[at] * pair_sum(total, spare.at[at], even_lane)
    smooth(za, zf, None, cc, *coarse)
    smooth(zb, za, zf, cc, *coarse)
    smooth(za, zb, zf, cc, *coarse)
    for at in range(LAYERS // 2):
        value = middle(za, at + 1, HALF) * ginv[at]
        spare[at, pl.ds(0, HALF, 2), :] = value
        spare[at, pl.ds(1, HALF, 2), :] = value
        value = spare[at]
        for row in (2 * at + 1, 2 * at + 2):
            one[row, TOP : TOP + WINDOW, :] = middle(two, row) + middle(g, row) * value
    smooth(two, one, f, c, LAYERS)
    smooth(one, two, f, c, LAYERS)


def depth_at(at):
    place = jnp.full((8, LANES), at, jnp.int32)
    return jnp.exp(-(LAYERS - 1 - place).astype(F32) / (LAYERS / 4.0))


def tall(values, rows=WINDOW):
    return jnp.concatenate([values] * (rows // 8), axis=0)


def first_kernel(
    got, plate_window, from_low, from_high,
    g, c, big, cc, kc, ginv, vel, x_own, f_own, f_up, f_down,
    packed, f, one, two, zf, za, zb, spare, layer, gc,
):
    domain = places()[-1]
    coarse_domain = places(HALF)[-1]
    clear_edges((f, one, two, vel, g))
    clear_edges((zf, za, zb, gc), HALF)
    for index in range(TILES + 1):
        a, b, d, e = rows_of(index, from_low, from_high, TILES + 1)
        packed[index, 0:4, :] = a
        packed[index, 4:12, :] = b
        packed[index, 12:28, :] = got[index // 5, index % 5] if index < TILES else plate_window[...]
        packed[index, 28:36, :] = d
        packed[index, 36:40, :] = e

    def mirror(pairs):
        speed = lanes_of((1, LANES)) < SPAN
        for index in range(TILES + 1):
            for target, source in pairs:
                value = packed[index, source : source + 1, :]
                if index < TILES and index % 5 < 4:
                    value = jnp.where(speed, 0.0, value)
                packed[index, target : target + 1, :] = value

    @pl.when(lax.axis_index("au") == 0)
    def _():
        mirror(((HALO - 1, HALO), (HALO - 2, HALO + 1)))

    @pl.when(lax.axis_index("au") == lax.axis_size("au") - 1)
    def _():
        mirror(((HALO + OWN, HALO + OWN - 1), (HALO + OWN + 1, HALO + OWN - 2)))

    lane = lanes_of((WINDOW, LANES))
    even_lane = lanes_of((HALF, LANES)) % 2 == 0

    def slab_of(source, slab):
        result = jnp.zeros((WINDOW, LANES), F32)
        for tile, start, first, count in reversed(PIECES[slab]):
            result = jnp.where(lane < first + count, turn(packed[source * 5 + tile], first - start), result)
        return result

    for source in range(8):
        logs = []
        for row in range(4):
            at = source * 4 + row + 1
            speed = slab_of(source, row)
            layer[at] = jnp.broadcast_to(speed[16:24, SPAN - 1 : SPAN], (8, LANES))
            vel[at, TOP : TOP + WINDOW, :] = speed
            logs.append(slab_of(source, 4 + row))
            g[at, TOP : TOP + WINDOW, :] = jnp.exp(0.5 * logs[-1])
        for pair in range(2):
            at = 2 * source + pair
            total = pair_sum(logs[2 * pair] + logs[2 * pair + 1], spare.at[at], even_lane)
            gc[at + 1, TOP : TOP + HALF, :] = jnp.exp(0.0625 * total)
    layer[0] = layer[1]
    layer[LAYERS + 1] = layer[LAYERS]
    g[0] = g[1]
    g[LAYERS + 1] = g[LAYERS]
    gc[0] = gc[1]
    gc[LAYERS // 2 + 1] = gc[LAYERS // 2]

    for at in range(LAYERS // 2):
        centre, total = around(gc, at + 1, HALF, 2)
        per = jnp.where(coarse_domain, DAMPING / total, 0.0)
        cc[at] = centre * per
        kc[at] = (0.125 / COARSE_FACTOR) * per
        ginv[at] = 1.0 / centre

    plate = packed[TILES]
    one[1, TOP : TOP + WINDOW, :] = plate
    beside = [plate + other for other in four(one, 1)[1:]]
    across_layers = None
    for at in range(LAYERS):
        g_mid, *g_four = four(g, at + 1)
        v_mid, *v_four = four(vel, at + 1)
        depth = depth_at(at)
        level = layer[at + 1]
        depth_tall, twice = tall(depth), tall(2.0 * level)
        total_g = (g_four[0] + g_four[1]) + (g_four[2] + g_four[3])
        total_g = total_g + (middle(g, at) + middle(g, at + 2))
        total = jnp.zeros((WINDOW, LANES), F32)
        for g_n, v_n, s_n in zip(g_four, v_four, beside):
            total = total + g_n * (depth_tall * s_n + twice) * (v_mid - v_n)
        total = g_mid * total
        for other in (at, at + 2):
            place = min(max(other - 1, 0), LAYERS - 1)
            if other == at and at > 0:
                total = total - across_layers
                continue
            scale = tall(depth + depth_at(place)) * plate + tall(level + layer[other])
            across_layers = (g_mid * middle(g, other)) * scale * (v_mid - middle(vel, other))
            total = total + across_layers
        per = jnp.where(domain, DAMPING / total_g, 0.0)
        c[at] = g_mid * per
        big[at] = total_g * (1.0 / DAMPING)
        f[at + 1, TOP : TOP + WINDOW, :] = -0.5 * total * per
    vcycle(f, one, two, zf, za, zb, spare, g, c, big, cc, kc, ginv)

    own_lane = lanes_of((OWN, LANES))
    sent = []
    for at in range(LAYERS):
        ratio = 1.0 / g[at + 1, TOP + HALO : TOP + HALO + OWN, :]
        x = one[at + 1, TOP + HALO : TOP + HALO + OWN, :] * ratio
        x_own[at] = x
        nxt = -(x * (c[at, HALO : HALO + OWN, :] * ratio))
        f_own[at] = nxt
        sent.append(nxt)
    for index in range(16):
        both = jnp.where(own_lane < 64, turn(sent[2 * index], -8), turn(sent[2 * index + 1], 56))
        start = 4 * (index % 2)
        f_up[index] = both[8:16]
        f_down[index] = both[0:8]
        f_up[16 + index // 2, start : start + 4, :] = both[4:8]
        f_down[16 + index // 2, start : start + 4, :] = both[8:12]


def side_kernel(x_own, label_window, inc, ones):
    slot = lanes_of((OWN, LANES)) // PART
    for part in range(8):
        tile = turn(x_own[4 * part], -MARGIN)
        for row in range(1, 4):
            tile = jnp.where(slot == row, turn(x_own[4 * part + row], PART * row - MARGIN), tile)
        inc[part] = tile
    low = label_window[...] & 127
    place = lax.broadcasted_iota(jnp.int32, (LANES, LANES), 0)
    for at in range(OWN):
        hit = jnp.where(low[at : at + 1, :] == place, 1.0, 0.0)
        ones[:, at * LANES : (at + 1) * LANES] = hit.astype(jnp.bfloat16)


INNER = 24
SKIP = 8


def second_kernel(
    g, c, big, cc, kc, ginv, vel, f_own, from_low, from_high, inc, label_window, ones,
    send,
    f, one, two, zf, za, zb, spare, layers,
):
    _, lane, _, _, _, _, domain = places()
    clear_edges((f, one, two))
    clear_edges((zf, za, zb), HALF)
    for index in range(16):
        start = 4 * (index % 2)
        spare[index, 0:4, :] = from_low[16 + index // 2, start : start + 4, :]
        spare[index, 4:12, :] = from_low[index]
        spare[index, 28:36, :] = from_high[index]
        spare[index, 36:40, :] = from_high[16 + index // 2, start : start + 4, :]
        for row, shift in ((0, 8), (1, 72)):
            at = 2 * index + row
            if row == 0:
                spare[index, HALO : HALO + OWN, :] = turn(f_own[at], -8)
            else:
                spare[index, HALO : HALO + OWN, :] = turn(f_own[at], 56)
            f[at + 1, TOP : TOP + WINDOW, :] = jnp.where(domain, turn(spare[index], shift), 0.0)
    vcycle(f, one, two, zf, za, zb, spare, g, c, big, cc, kc, ginv)

    top = TOP + SKIP
    for at in range(LAYERS):
        two[at + 1, top : top + INNER, :] = middle(one, at + 1, INNER, top) / middle(g, at + 1, INNER, top)
    row_at = SKIP + lax.broadcasted_iota(jnp.int32, (INNER, LANES), 0)
    lane = lanes_of((INNER, LANES))
    across = row_at + (lax.axis_index("au") * OWN - HALO)
    along = lane + (lax.axis_index("vert") * (8 * PART) + lax.axis_index("row") * PART - MARGIN)
    own = (row_at >= HALO) & (row_at < HALO + OWN) & (lane >= MARGIN) & (lane < MARGIN + PART)
    shares = [
        jnp.where(edge, 1.0, 0.5)
        for edge in (
            across == 0,
            across == lax.axis_size("au") * OWN - 1,
            along == 0,
            along == lax.axis_size("vert") * 8 * PART - 1,
        )
    ]
    column = jnp.zeros((INNER, LANES), F32)
    for at in range(LAYERS):
        g_mid, *g_four = four(g, at + 1, INNER, 1, top)
        v_mid, *v_four = four(vel, at + 1, INNER, 1, top)
        x_mid, *x_four = four(two, at + 1, INNER, 1, top)
        total = jnp.zeros((INNER, LANES), F32)
        for share, g_n, v_n, x_n in zip(shares, g_four, v_four, x_four):
            total = total + (share * g_n) * ((x_n - x_mid) * (v_n - v_mid))
        for other, end in ((at, 0), (at + 2, LAYERS + 1)):
            share = 1.0 if other == end else 0.5
            x_n, v_n = middle(two, other, INNER, top), middle(vel, other, INNER, top)
            total = total + (share * middle(g, other, INNER, top)) * ((x_n - x_mid) * (v_n - v_mid))
        total = jnp.where(own, g_mid * total, 0.0)
        column = column + tall(depth_at(at), INNER) * total
        folded = jnp.sum(total.reshape(INNER // 8, 8, LANES), axis=0)
        layers[at : at + 1, :] = jnp.sum(folded, axis=0, keepdims=True)

    high = label_window[...] >> 7
    sums = column[HALO - SKIP : HALO - SKIP + OWN, :]
    kind = lax.broadcasted_iota(jnp.int32, (4, LANES), 0)
    left = []
    for at in range(OWN):
        value = jnp.where(high[at : at + 1, :] == kind, sums[at : at + 1, :], 0.0)
        first = value.astype(jnp.bfloat16).astype(F32)
        rest = value - first
        then = rest.astype(jnp.bfloat16).astype(F32)
        left.append(jnp.concatenate([first, then, rest - then, jnp.zeros_like(first)], axis=0).astype(jnp.bfloat16))
    product = lax.dot_general(
        jnp.concatenate(left, axis=1), ones[...], (((1,), (1,)), ((), ())), preferred_element_type=F32
    )
    segments = (product[0:4] + product[4:8]) + product[8:12]

    slot = lanes_of((OWN, LANES)) // PART
    for part in range(8):
        tile = turn(two[4 * part + 1, TOP + HALO : TOP + HALO + OWN, :], -MARGIN)
        for row in range(1, 4):
            x = two[4 * part + row + 1, TOP + HALO : TOP + HALO + OWN, :]
            tile = jnp.where(slot == row, turn(x, PART * row - MARGIN), tile)
        send[part, 0:16, :] = inc[part]
        send[part, 16:32, :] = tile
        send[part, 32:36, :] = segments
        send[part, 36:40, :] = layers[4 * part : 4 * part + 4, :]


def place_kernel(got, inc, adj, spread):
    lane = lanes_of((OWN, LANES))
    slot = lane // PART
    for out, start in ((inc, 0), (adj, 16)):
        for row in range(4):
            for half in range(2):
                tile = jnp.zeros((OWN, LANES), F32)
                for source in range(4):
                    piece = got[4 * half + source, start : start + 16, :]
                    tile = jnp.where(slot == source, turn(piece, PART * (source - row)), tile)
                out[row, :, half * LANES : (half + 1) * LANES] = tile
    total = got[0, 32:40, :]
    for source in range(1, 8):
        total = total + got[source, 32:40, :]
    level = jnp.zeros((1, LANES), F32)
    lane = lanes_of((1, LANES))
    for row in range(4):
        level = jnp.where(lane == row, jnp.sum(total[4 + row : 5 + row, :], axis=1, keepdims=True), level)
    pieces = [total[row : row + 1, :] for row in range(4)] + [level]
    line = jnp.concatenate(pieces, axis=1)
    for other in range(spread.shape[0]):
        spread[other] = line


def total_kernel(parts, segments, layers):
    cells = LAYERS * lax.axis_size("au") * OWN * lax.axis_size("vert") * 8 * PART
    total = jnp.sum(parts[...], axis=0)
    for row in range(4):
        segments[row : row + 1, :] = total[:, row * LANES : (row + 1) * LANES] * (1.0 / (cells / NSEG) ** 0.5)
    layers[...] = total[:, 4 * LANES : 4 * LANES + 4] * (1.0 / (cells / LAYERS) ** 0.5)


def shards(velocity, log_visc, labels, seg_dir, layer_dir):
    vert = lax.axis_size("vert")
    across = lax.axis_size("au")
    ahead = [(i, (i + 1) % vert) for i in range(vert)]
    back = [((i + 1) % vert, i) for i in range(vert)]
    upward = [(i, i + 1) for i in range(across - 1)]
    downward = [(i + 1, i) for i in range(across - 1)]
    vmem = pl.BlockSpec(memory_space=pltpu.VMEM)
    hbm = pl.BlockSpec(memory_space=pltpu.HBM)
    labels_like = jax.ShapeDtypeStruct((OWN, 2 * LANES), jnp.int32)
    label_tile = jax.ShapeDtypeStruct((OWN, LANES), jnp.int32)
    edges, field = sds(3, OWN, LANES), sds(4, OWN, 2 * LANES)

    left, right, plate, vel, log, lab = call(
        edge_kernel,
        (edges, edges, sds(OWN, 2 * LANES), field, field, labels_like),
        [pltpu.VMEM((4, LANES), F32), pltpu.SemaphoreType.DMA((4,))],
        in_specs=[hbm] * 4,
    )(velocity, log_visc, labels, seg_dir.reshape(4, LANES))
    from_left = lax.ppermute(right, "vert", ahead)
    from_right = lax.ppermute(left, "vert", back)
    send = call(
        window_kernel,
        sds(8, 5, OWN, LANES),
        in_specs=[vmem, vmem, pl.BlockSpec(memory_space=pltpu.SMEM)],
    )(vel, log, layer_dir)
    send, plate_window, label_window = call(
        patch_kernel, (sds(8, 5, OWN, LANES), sds(OWN, LANES), label_tile)
    )(send, plate, lab, left, right, from_left, from_right)
    got = lax.all_to_all(send, "row", 0, 0, tiled=True)
    up, down = call(rows_kernel, (sds(62, 8, LANES), sds(62, 8, LANES)))(got, plate_window)
    from_low = lax.ppermute(up, "au", upward)
    from_high = lax.ppermute(down, "au", downward)
    fine = sds(LAYERS, WINDOW, LANES)
    fine_padded = sds(LAYERS + 2, PAD_ROWS, LANES)
    coarse = sds(LAYERS // 2, HALF, LANES)
    own = sds(LAYERS, OWN, LANES)
    fine_scratch = pltpu.VMEM((LAYERS + 2, PAD_ROWS, LANES), F32)
    coarse_scratch = pltpu.VMEM((LAYERS // 2 + 2, HALF_ROWS, LANES), F32)
    spare = pltpu.VMEM((LAYERS // 2, WINDOW, LANES), F32)
    *factors, x_own, f_own, f_up, f_down = call(
        first_kernel,
        (fine_padded, fine, fine, coarse, coarse, coarse, fine_padded)
        + (own, own, sds(24, 8, LANES), sds(24, 8, LANES)),
        [pltpu.VMEM((TILES + 1, WINDOW, LANES), F32)]
        + [fine_scratch] * 3
        + [coarse_scratch] * 3
        + [spare, pltpu.VMEM((LAYERS + 2, 8, LANES), F32), coarse_scratch],
    )(got, plate_window, from_low, from_high)
    from_low = lax.ppermute(f_up, "au", upward)
    from_high = lax.ppermute(f_down, "au", downward)
    inc, ones = call(
        side_kernel, (sds(8, OWN, LANES), jax.ShapeDtypeStruct((LANES, OWN * LANES), jnp.bfloat16))
    )(x_own, label_window)
    send = call(
        second_kernel,
        sds(8, 40, LANES),
        [fine_scratch] * 3 + [coarse_scratch] * 3 + [spare, pltpu.VMEM((LAYERS, LANES), F32)],
    )(*factors, f_own, from_low, from_high, inc, label_window, ones)
    got = lax.all_to_all(send, "row", 0, 0, tiled=True)
    increment, adjoint, spread = call(place_kernel, (field, field, sds(across * vert, 1, 5 * LANES)))(got)
    parts = lax.all_to_all(spread, ("au", "vert"), 0, 0, tiled=True)
    hv_segments, hv_layers = call(total_kernel, (sds(4, LANES), sds(1, 4)))(parts)
    return increment, adjoint, hv_segments.reshape(NSEG), hv_layers.reshape(4)


def solution(mesh):
    in_specs = (P("row", "au", "vert"), P("row", "au", "vert"), P("au", "vert"), P(), P("row"))
    out_specs = (P("row", "au", "vert"), P("row", "au", "vert"), P(), P("row"))
    return jax.shard_map(shards, mesh=mesh, in_specs=in_specs, out_specs=out_specs, check_vma=False)
```

time: 132 us -> 104 us (0.79)
  Pallas kernels: 39 us -> 15 us
  starting transfers between devices: 21.2 us -> 16.2 us
  waiting for transfers between devices: 7.72 us -> 10.5 us
  blocking collectives: 58.7 us -> 57.2 us
    pallas_call x1, Pallas kernels: 19.6 us -> 5.86 us  [shards(): call(first_kernel, (fine_padded, fine, fine, coarse, coarse, coarse, fine...]
    pallas_call x1, Pallas kernels: 15.8 us -> 6.08 us  [shards(): call(second_kernel, sds(8, 40, LANES), [fine_scratch] * 3 + [coarse_scrat...]
    all_to_all x2, blocking collectives: 31.7 us -> 26.7 us  [shards(): got = lax.all_to_all(send, 'row', 0, 0, tiled=True)]
    all_to_all x1, blocking collectives: 26.9 us -> 30.5 us  [shards(): parts = lax.all_to_all(spread, ('au', 'vert'), 0, 0, tiled=True)]
    ppermute x1, waiting for transfers between devices: 0.89 us -> 3.83 us  [shards(): from_high = lax.ppermute(down, 'au', downward)]
    ppermute x1, starting transfers between devices: 4.02 us -> 1.29 us  [shards(): from_high = lax.ppermute(f_down, 'au', downward)]
    ppermute x1, starting transfers between devices: 3.81 us -> 1.29 us  [shards(): from_high = lax.ppermute(down, 'au', downward)]
    ppermute x1, waiting for transfers between devices: 2.51 us -> 4.64 us  [shards(): from_high = lax.ppermute(f_down, 'au', downward)]
  transfers between devices with their start and end apart: 6 -> 6, of which waited for: 6 -> 4; matrix products, arithmetic and copies ran while one was open for 0% -> 0% of each run, Pallas kernels for 0% -> 1%
where the time goes in v2:
time: 104 us; the launch traced here: 103 us
  blocking collectives  57.2 us (55%)
  starting transfers between devices  16.2 us (16%)
  Pallas kernels  15 us (14%)
  waiting for transfers between devices  10.5 us (10%)
  local copies, waits for them, and re-layouts  3.72 us (4%)
    all_to_all x1, blocking collectives, shards(): parts = lax.all_to_all(spread, ('au', 'vert'), 0, 0, tiled=True)  30.5 us
    all_to_all x2, blocking collectives, shards(): got = lax.all_to_all(send, 'row', 0, 0, tiled=True)  26.7 us
    ppermute x1, starting transfers between devices, shards(): from_right = lax.ppermute(left, 'vert', back)  6.89 us
    pallas_call x1, Pallas kernels, shards(): call(second_kernel, sds(8, 40, LANES), [fine_scratch] * 3 + [coarse_scrat...  6.08 us
    pallas_call x1, Pallas kernels, shards(): call(first_kernel, (fine_padded, fine, fine, coarse, coarse, coarse, fine...  5.86 us
    ppermute x1, waiting for transfers between devices, shards(): from_high = lax.ppermute(f_down, 'au', downward)  4.64 us
    ppermute x1, waiting for transfers between devices, shards(): from_high = lax.ppermute(down, 'au', downward)  3.83 us
    unnamed x10, local copies, waits for them, and re-layouts  3.72 us
  transfers between devices with their start and end apart: 6, of which 4 were waited for; matrix products, arithmetic and copies ran while one was open for 0% of the time, Pallas kernels for 1%

profile of v2, /device:TPU:1, one launch (start us, length us, event | category | flops | bytes accessed | tf_op | source)
XLA Modules:
  0.0 103.3 jit_solution(17118532264218961064)
XLA Ops:
  0.6 0.0 copy-start
  0.6 0.8 copy-done
  1.5 0.0 copy-start.1
  1.5 0.8 copy-done.1
  2.3 0.0 copy-start.2
  2.3 0.7 copy-done.2
  3.0 0.0 copy-start.3
  3.0 0.7 copy-done.3
  3.7 0.3 shard_map.84
  4.1 6.9 %collective-permute-start.1 = (f32[3,16,128]{2,1,0:T(8,128)S(1)}, f32[3,16,128]{2,1,0:T(8,128)S(1)}, u32[]{:S(2)}, u32[]{:S(2)}) collective-permute-start(f32[3,16,128]{2,1,0:T(8,128)S(1)} %get-tuple-element.37.left), channel_id=1, source_target_pairs={{1,0},{2,1},{3,2},{4,3},{5,4},{6,5},{7,6},{0,7},{9,8},{10,9},{11,1... | collective-permute-start | bytes 73736 | tf_op jit(solution)/shard_map/ppermute | solution.py:573
  11.0 0.0 collective-permute-start
  11.0 0.0 copy-start.4
  11.0 0.7 copy-done.4
  11.6 0.8 shard_map.85.sent
  12.4 0.0 collective-permute-done.1.from_right
  12.4 0.0 collective-permute-done.from_left
  12.4 0.2 shard_map.86
  12.6 16.0 %all_to_all.15.got = f32[8,5,16,128]{3,2,1,0:T(8,128)S(1)} all-to-all(f32[8,5,16,128]{3,2,1,0:T(8,128)S(1)} %get-tuple-element.39), channel_id=1, replica_groups=mesh['row'=8,'au'=8,'vert'=8] {'row'}, dimensions={0} | all-to-all | bytes 655360 | tf_op jit(solution)/shard_map/all_to_all | solution.py:582
  28.7 3.2 %collective-permute-start.2 = (f32[62,8,128]{2,1,0:T(8,128)S(1)}, f32[62,8,128]{2,1,0:T(8,128)S(1)}, u32[]{:S(2)}, u32[]{:S(2)}) collective-permute-start(f32[62,8,128]{2,1,0:T(8,128)S(1)} %get-tuple-element.41), channel_id=1, source_target_pairs={{0,8},{8,16},{16,24},{24,32},{32,40},{40,48},{48,56},{1,9},{9,17},... | collective-permute-start | bytes 761864 | tf_op jit(solution)/shard_map/ppermute | solution.py:584
  31.9 1.3 %collective-permute-start.3 = (f32[62,8,128]{2,1,0:T(8,128)S(1)}, f32[62,8,128]{2,1,0:T(8,128)S(1)}, u32[]{:S(2)}, u32[]{:S(2)}) collective-permute-start(f32[62,8,128]{2,1,0:T(8,128)S(1)} %get-tuple-element.42), channel_id=1, source_target_pairs={{8,0},{16,8},{24,16},{32,24},{40,32},{48,40},{56,48},{9,1},{17,9},... | collective-permute-start | bytes 761864 | tf_op jit(solution)/shard_map/ppermute | solution.py:585
  33.2 1.9 %collective-permute-done.2.from_low = f32[62,8,128]{2,1,0:T(8,128)S(1)} collective-permute-done((f32[62,8,128]{2,1,0:T(8,128)S(1)}, f32[62,8,128]{2,1,0:T(8,128)S(1)}, u32[]{:S(2)}, u32[]{:S(2)}) %collective-permute-start.2) | collective-permute-done | bytes 253984 | tf_op jit(solution)/shard_map/ppermute | solution.py:584
  35.1 3.8 %collective-permute-done.3.from_high = f32[62,8,128]{2,1,0:T(8,128)S(1)} collective-permute-done((f32[62,8,128]{2,1,0:T(8,128)S(1)}, f32[62,8,128]{2,1,0:T(8,128)S(1)}, u32[]{:S(2)}, u32[]{:S(2)}) %collective-permute-start.3) | collective-permute-done | bytes 253984 | tf_op jit(solution)/shard_map/ppermute | solution.py:585
  38.9 5.9 %shard_map.88 = (f32[34,56,128]{2,1,0:T(8,128)S(1)}, f32[32,40,128]{2,1,0:T(8,128)S(1)}, f32[32,40,128]{2,1,0:T(8,128)S(1)}, f32[16,20,128]{2,1,0:T(8,128)S(1)},...) custom-call(f32[8,5,16,128]{3,2,1,0:T(8,128)S(1)} %all_to_all.15.got, ...), custom_call_target="tpu_custom_call" | custom-call | tf_op jit(solution)/shard_map/pallas_call | solution.py:593
  44.8 3.5 %collective-permute-start.4 = (f32[24,8,128]{2,1,0:T(8,128)S(1)}, f32[24,8,128]{2,1,0:T(8,128)S(1)}, u32[]{:S(2)}, u32[]{:S(2)}) collective-permute-start(f32[24,8,128]{2,1,0:T(8,128)S(1)} %get-tuple-element.51), channel_id=1, source_target_pairs={{0,8},{8,16},{16,24},{24,32},{32,40},{40,48},{48,56},{1,9},{9,17},... | collective-permute-start | bytes 294920 | tf_op jit(solution)/shard_map/ppermute | solution.py:602
  48.3 1.3 %collective-permute-start.5 = (f32[24,8,128]{2,1,0:T(8,128)S(1)}, f32[24,8,128]{2,1,0:T(8,128)S(1)}, u32[]{:S(2)}, u32[]{:S(2)}) collective-permute-start(f32[24,8,128]{2,1,0:T(8,128)S(1)} %get-tuple-element.52), channel_id=1, source_target_pairs={{8,0},{16,8},{24,16},{32,24},{40,32},{48,40},{56,48},{9,1},{17,9},... | collective-permute-start | bytes 294920 | tf_op jit(solution)/shard_map/ppermute | solution.py:603
  49.6 0.2 shard_map.89
  49.7 0.2 collective-permute-done.4.from_low
  49.9 4.6 %collective-permute-done.5.from_high = f32[24,8,128]{2,1,0:T(8,128)S(1)} collective-permute-done((f32[24,8,128]{2,1,0:T(8,128)S(1)}, f32[24,8,128]{2,1,0:T(8,128)S(1)}, u32[]{:S(2)}, u32[]{:S(2)}) %collective-permute-start.5) | collective-permute-done | bytes 98336 | tf_op jit(solution)/shard_map/ppermute | solution.py:603
  54.5 6.1 %shard_map.90 = f32[8,40,128]{2,1,0:T(8,128)S(1)} custom-call(f32[34,56,128]{2,1,0:T(8,128)S(1)} %get-tuple-element.43.g, f32[32,40,128]{2,1,0:T(8,128)S(1)} %get-tuple-element.44.c, f32[32,40,128]{2,1,0:T(8,128)S(1)} %get-tuple-element.45.big, f32[16,20,128]{2,1,0:T(8,128)S(1)} %get-tuple-element.46.cc, f32[16,20,128]{2,1,0:T(8,128)S(1)} %get-tuple-element.47.kc, ...), custom_call_target="tpu_custom_call" | custom-call | tf_op jit(solution)/shard_map/pallas_call | solution.py:607
  60.6 10.7 %all_to_all.16.got = f32[8,40,128]{2,1,0:T(8,128)S(1)} all-to-all(f32[8,40,128]{2,1,0:T(8,128)S(1)} %shard_map.90), channel_id=1, replica_groups=mesh['row'=8,'au'=8,'vert'=8] {'row'}, dimensions={0} | all-to-all | bytes 327680 | tf_op jit(solution)/shard_map/all_to_all | solution.py:612
  71.3 0.8 shard_map.91
  72.1 30.5 %all_to_all.17.parts = f32[64,1,640]{2,1,0:T(1,128)S(1)} all-to-all(f32[64,1,640]{2,1,0:T(1,128)S(1)} %get-tuple-element.59), channel_id=1, replica_groups=mesh['row'=8,'au'=8,'vert'=8] {'au','vert'}, dimensions={0} | all-to-all | bytes 327680 | tf_op jit(solution)/shard_map/all_to_all | solution.py:614
  102.6 0.7 shard_map.92
  (1 shorter events, 0.0 us)
Async XLA Ops:
  0.6 0.8 copy-start
  1.5 0.8 copy-start.1
  2.3 0.7 copy-start.2
  3.0 0.7 copy-start.3
  4.1 8.3 %collective-permute-start.1 = (f32[3,16,128]{2,1,0:T(8,128)S(1)}, f32[3,16,128]{2,1,0:T(8,128)S(1)}, u32[]{:S(2)}, u32[]{:S(2)}) collective-permute-start(f32[3,16,128]{2,1,0:T(8,128)S(1)} %get-tuple-element.37.left), channel_id=1, source_target_pairs={{1,0},{2,1},{3,2},{4,3},{5,4},{6,5},{7,6},{0,7},{9,8},{10,9},{11,1... | collective-permute-start | bytes 73736 | tf_op jit(solution)/shard_map/ppermute | solution.py:573
  11.0 1.5 %collective-permute-start = (f32[3,16,128]{2,1,0:T(8,128)S(1)}, f32[3,16,128]{2,1,0:T(8,128)S(1)}, u32[]{:S(2)}, u32[]{:S(2)}) collective-permute-start(f32[3,16,128]{2,1,0:T(8,128)S(1)} %get-tuple-element.38.right), channel_id=1, source_target_pairs={{0,1},{1,2},{2,3},{3,4},{4,5},{5,6},{6,7},{7,0},{8,9},{9,10},{10,1... | collective-permute-start | bytes 73736 | tf_op jit(solution)/shard_map/ppermute | solution.py:572
  11.0 0.7 copy-start.4
  28.7 6.4 %collective-permute-start.2 = (f32[62,8,128]{2,1,0:T(8,128)S(1)}, f32[62,8,128]{2,1,0:T(8,128)S(1)}, u32[]{:S(2)}, u32[]{:S(2)}) collective-permute-start(f32[62,8,128]{2,1,0:T(8,128)S(1)} %get-tuple-element.41), channel_id=1, source_target_pairs={{0,8},{8,16},{16,24},{24,32},{32,40},{40,48},{48,56},{1,9},{9,17},... | collective-permute-start | bytes 761864 | tf_op jit(solution)/shard_map/ppermute | solution.py:584
  31.9 7.0 %collective-permute-start.3 = (f32[62,8,128]{2,1,0:T(8,128)S(1)}, f32[62,8,128]{2,1,0:T(8,128)S(1)}, u32[]{:S(2)}, u32[]{:S(2)}) collective-permute-start(f32[62,8,128]{2,1,0:T(8,128)S(1)} %get-tuple-element.42), channel_id=1, source_target_pairs={{8,0},{16,8},{24,16},{32,24},{40,32},{48,40},{56,48},{9,1},{17,9},... | collective-permute-start | bytes 761864 | tf_op jit(solution)/shard_map/ppermute | solution.py:585
  44.8 5.1 %collective-permute-start.4 = (f32[24,8,128]{2,1,0:T(8,128)S(1)}, f32[24,8,128]{2,1,0:T(8,128)S(1)}, u32[]{:S(2)}, u32[]{:S(2)}) collective-permute-start(f32[24,8,128]{2,1,0:T(8,128)S(1)} %get-tuple-element.51), channel_id=1, source_target_pairs={{0,8},{8,16},{16,24},{24,32},{32,40},{40,48},{48,56},{1,9},{9,17},... | collective-permute-start | bytes 294920 | tf_op jit(solution)/shard_map/ppermute | solution.py:602
  48.3 6.3 %collective-permute-start.5 = (f32[24,8,128]{2,1,0:T(8,128)S(1)}, f32[24,8,128]{2,1,0:T(8,128)S(1)}, u32[]{:S(2)}, u32[]{:S(2)}) collective-permute-start(f32[24,8,128]{2,1,0:T(8,128)S(1)} %get-tuple-element.52), channel_id=1, source_target_pairs={{8,0},{16,8},{24,16},{32,24},{40,32},{48,40},{56,48},{9,1},{17,9},... | collective-permute-start | bytes 294920 | tf_op jit(solution)/shard_map/ppermute | solution.py:603

commit v3 on v2

--- a/solution.py
+++ b/solution.py
@@ -25,6 +25,7 @@
 TILES = 40
 F32 = jnp.float32
 VMEM_LIMIT = 48 * 1024 * 1024
+EDGE_LIMIT = 56290000
 
 
 def lanes_of(shape):
@@ -35,13 +36,13 @@
     return pltpu.roll(values, amount % LANES, values.ndim - 1)
 
 
-def call(kernel, outs, scratch=(), **more):
+def call(kernel, outs, scratch=(), limit=VMEM_LIMIT, **more):
     return pl.pallas_call(
         kernel,
         out_shape=outs,
         **more,
         scratch_shapes=list(scratch),
-        compiler_params=pltpu.CompilerParams(vmem_limit_bytes=VMEM_LIMIT),
+        compiler_params=pltpu.CompilerParams(vmem_limit_bytes=limit),
     )
 
 
@@ -235,8 +236,7 @@
     return centre, total + (middle(ref, at - 1, rows) + middle(ref, at + 1, rows))
 
 
-def pair_sum(values, spare, even_lane):
-    spare[...] = values
+def pair_sum(spare, even_lane):
     total = spare[pl.ds(0, HALF, 2), :] + spare[pl.ds(1, HALF, 2), :]
     return total + jnp.where(even_lane, turn(total, -1), turn(total, 1))
 
@@ -273,8 +273,9 @@
         return big[at] * ((middle(f, at + 1) - DAMPING * centre) + c[at] * total)
 
     for at in range(LAYERS // 2):
-        total = leftover(2 * at) + leftover(2 * at + 1)
-        zf[at + 1, TOP : TOP + HALF, :] = kc[at] * pair_sum(total, spare.at[at], even_lane)
+        spare[at] = leftover(2 * at) + leftover(2 * at + 1)
+    for at in range(LAYERS // 2):
+        zf[at + 1, TOP : TOP + HALF, :] = kc[at] * pair_sum(spare.at[at], even_lane)
     smooth(za, zf, None, cc, *coarse)
     smooth(zb, za, zf, cc, *coarse)
     smooth(za, zb, zf, cc, *coarse)
@@ -282,6 +283,7 @@
         value = middle(za, at + 1, HALF) * ginv[at]
         spare[at, pl.ds(0, HALF, 2), :] = value
         spare[at, pl.ds(1, HALF, 2), :] = value
+    for at in range(LAYERS // 2):
         value = spare[at]
         for row in (2 * at + 1, 2 * at + 2):
             one[row, TOP : TOP + WINDOW, :] = middle(two, row) + middle(g, row) * value
@@ -351,9 +353,9 @@
             logs.append(slab_of(source, 4 + row))
             g[at, TOP : TOP + WINDOW, :] = jnp.exp(0.5 * logs[-1])
         for pair in range(2):
-            at = 2 * source + pair
-            total = pair_sum(logs[2 * pair] + logs[2 * pair + 1], spare.at[at], even_lane)
-            gc[at + 1, TOP : TOP + HALF, :] = jnp.exp(0.0625 * total)
+            spare[2 * source + pair] = logs[2 * pair] + logs[2 * pair + 1]
+    for at in range(LAYERS // 2):
+        gc[at + 1, TOP : TOP + HALF, :] = jnp.exp(0.0625 * pair_sum(spare.at[at], even_lane))
     layer[0] = layer[1]
     layer[LAYERS + 1] = layer[LAYERS]
     g[0] = g[1]
@@ -404,12 +406,11 @@
         ratio = 1.0 / g[at + 1, TOP + HALO : TOP + HALO + OWN, :]
         x = one[at + 1, TOP + HALO : TOP + HALO + OWN, :] * ratio
         x_own[at] = x
-        nxt = -(x * (c[at, HALO : HALO + OWN, :] * ratio))
-        f_own[at] = nxt
-        sent.append(nxt)
+        sent.append(-(x * (c[at, HALO : HALO + OWN, :] * ratio)))
     for index in range(16):
         both = jnp.where(own_lane < 64, turn(sent[2 * index], -8), turn(sent[2 * index + 1], 56))
         start = 4 * (index % 2)
+        f_own[index] = both
         f_up[index] = both[8:16]
         f_down[index] = both[0:8]
         f_up[16 + index // 2, start : start + 4, :] = both[4:8]
@@ -448,13 +449,11 @@
         spare[index, 4:12, :] = from_low[index]
         spare[index, 28:36, :] = from_high[index]
         spare[index, 36:40, :] = from_high[16 + index // 2, start : start + 4, :]
+        spare[index, HALO : HALO + OWN, :] = f_own[index]
+    for index in range(16):
+        both = spare[index]
         for row, shift in ((0, 8), (1, 72)):
-            at = 2 * index + row
-            if row == 0:
-                spare[index, HALO : HALO + OWN, :] = turn(f_own[at], -8)
-            else:
-                spare[index, HALO : HALO + OWN, :] = turn(f_own[at], 56)
-            f[at + 1, TOP : TOP + WINDOW, :] = jnp.where(domain, turn(spare[index], shift), 0.0)
+            f[2 * index + row + 1, TOP : TOP + WINDOW, :] = jnp.where(domain, turn(both, shift), 0.0)
     vcycle(f, one, two, zf, za, zb, spare, g, c, big, cc, kc, ginv)
 
     top = TOP + SKIP
@@ -488,8 +487,8 @@
             total = total + (share * middle(g, other, INNER, top)) * ((x_n - x_mid) * (v_n - v_mid))
         total = jnp.where(own, g_mid * total, 0.0)
         column = column + tall(depth_at(at), INNER) * total
-        folded = jnp.sum(total.reshape(INNER // 8, 8, LANES), axis=0)
-        layers[at : at + 1, :] = jnp.sum(folded, axis=0, keepdims=True)
+        layers[at] = jnp.sum(total.reshape(INNER // 8, 8, LANES), axis=0)
+    level = jnp.sum(layers[...], axis=1)
 
     high = label_window[...] >> 7
     sums = column[HALO - SKIP : HALO - SKIP + OWN, :]
@@ -515,7 +514,7 @@
         send[part, 0:16, :] = inc[part]
         send[part, 16:32, :] = tile
         send[part, 32:36, :] = segments
-        send[part, 36:40, :] = layers[4 * part : 4 * part + 4, :]
+        send[part, 36:40, :] = level[4 * part : 4 * part + 4, :]
 
 
 def place_kernel(got, inc, adj, spread):
@@ -568,6 +567,7 @@
         (edges, edges, sds(OWN, 2 * LANES), field, field, labels_like),
         [pltpu.VMEM((4, LANES), F32), pltpu.SemaphoreType.DMA((4,))],
         in_specs=[hbm] * 4,
+        limit=EDGE_LIMIT,
     )(velocity, log_visc, labels, seg_dir.reshape(4, LANES))
     from_left = lax.ppermute(right, "vert", ahead)
     from_right = lax.ppermute(left, "vert", back)
@@ -593,7 +593,7 @@
     *factors, x_own, f_own, f_up, f_down = call(
         first_kernel,
         (fine_padded, fine, fine, coarse, coarse, coarse, fine_padded)
-        + (own, own, sds(24, 8, LANES), sds(24, 8, LANES)),
+        + (own, sds(LAYERS // 2, OWN, LANES), sds(24, 8, LANES), sds(24, 8, LANES)),
         [pltpu.VMEM((TILES + 1, WINDOW, LANES), F32)]
         + [fine_scratch] * 3
         + [coarse_scratch] * 3
@@ -607,7 +607,7 @@
     send = call(
         second_kernel,
         sds(8, 40, LANES),
-        [fine_scratch] * 3 + [coarse_scratch] * 3 + [spare, pltpu.VMEM((LAYERS, LANES), F32)],
+        [fine_scratch] * 3 + [coarse_scratch] * 3 + [spare, pltpu.VMEM((LAYERS, 8, LANES), F32)],
     )(*factors, f_own, from_low, from_high, inc, label_window, ones)
     got = lax.all_to_all(send, "row", 0, 0, tiled=True)
     increment, adjoint, spread = call(place_kernel, (field, field, sds(across * vert, 1, 5 * LANES)))(got)

time: 104 us -> 98.2 us (0.944)
  Pallas kernels: 15 us -> 11.1 us
  local copies, waits for them, and re-layouts: 3.72 us -> 2.05 us
    pallas_call x1, Pallas kernels: 6.08 us -> 3.29 us  [shards(): call(second_kernel, sds(8, 40, LANES), [fine_scratch] * 3 + [coarse_scrat...]
    pallas_call x1, Pallas kernels: 5.86 us -> 4.05 us  [shards(): call(first_kernel, (fine_padded, fine, fine, coarse, coarse, coarse, fine...]
    unnamed x10 -> x6, local copies, waits for them, and re-layouts: 3.72 us -> 2.05 us
where the time goes in v3:
time: 98.2 us; the launch traced here: 97.8 us
  blocking collectives  57.2 us (58%)
  starting transfers between devices  16.2 us (16%)
  Pallas kernels  11.1 us (11%)
  waiting for transfers between devices  10.5 us (11%)
  local copies, waits for them, and re-layouts  2.05 us (2%)
    all_to_all x1, blocking collectives, shards(): parts = lax.all_to_all(spread, ('au', 'vert'), 0, 0, tiled=True)  30.5 us
    all_to_all x2, blocking collectives, shards(): got = lax.all_to_all(send, 'row', 0, 0, tiled=True)  26.7 us
    ppermute x1, starting transfers between devices, shards(): from_right = lax.ppermute(left, 'vert', back)  6.89 us
    ppermute x1, waiting for transfers between devices, shards(): from_high = lax.ppermute(f_down, 'au', downward)  4.64 us
    pallas_call x1, Pallas kernels, shards(): call(first_kernel, (fine_padded, fine, fine, coarse, coarse, coarse, fine...  4.05 us
    ppermute x1, waiting for transfers between devices, shards(): from_high = lax.ppermute(down, 'au', downward)  3.83 us
    ppermute x1, starting transfers between devices, shards(): from_low = lax.ppermute(f_up, 'au', upward)  3.46 us
    pallas_call x1, Pallas kernels, shards(): call(second_kernel, sds(8, 40, LANES), [fine_scratch] * 3 + [coarse_scrat...  3.29 us
  transfers between devices with their start and end apart: 6, of which 4 were waited for; matrix products, arithmetic and copies ran while one was open for 0% of the time, Pallas kernels for 1%

profile of v3, /device:TPU:1, one launch (start us, length us, event | category | flops | bytes accessed | tf_op | source)
XLA Modules:
  0.0 97.8 jit_solution(2633511633511622812)
XLA Ops:
  0.6 0.0 copy-start
  0.6 0.7 copy-done
  1.4 0.0 copy-start.1
  1.4 0.7 copy-done.1
  2.0 1.1 %shard_map.84 = (f32[3,16,128]{2,1,0:T(8,128)S(1)}, f32[3,16,128]{2,1,0:T(8,128)S(1)}, f32[16,256]{1,0:T(8,128)S(1)}, f32[4,16,256]{2,1,0:T(8,128)S(1)}, f32[4,1...) custom-call(f32[4,16,256]{2,1,0:T(8,128)} %vel_in.1, f32[4,16,256]{2,1,0:T(8,128)} %log_in.1, s32[16,256]{1,0:T(8,128)S(1)} %copy-done, ...), custom_call_target="tpu_custom_call" | custom-call | tf_op jit(solution)/shard_map/pallas_call | solution.py:565
  3.1 6.9 %collective-permute-start.1 = (f32[3,16,128]{2,1,0:T(8,128)S(1)}, f32[3,16,128]{2,1,0:T(8,128)S(1)}, u32[]{:S(2)}, u32[]{:S(2)}) collective-permute-start(f32[3,16,128]{2,1,0:T(8,128)S(1)} %get-tuple-element.37.left), channel_id=1, source_target_pairs={{1,0},{2,1},{3,2},{4,3},{5,4},{6,5},{7,6},{0,7},{9,8},{10,9},{11,1... | collective-permute-start | bytes 73736 | tf_op jit(solution)/shard_map/ppermute | solution.py:573
  10.0 0.0 collective-permute-start
  10.0 0.0 copy-start.2
  10.0 0.7 copy-done.2
  10.6 0.8 shard_map.85.sent
  11.4 0.0 collective-permute-done.1.from_right
  11.5 0.0 collective-permute-done.from_left
  11.5 0.2 shard_map.86
  11.7 16.0 %all_to_all.15.got = f32[8,5,16,128]{3,2,1,0:T(8,128)S(1)} all-to-all(f32[8,5,16,128]{3,2,1,0:T(8,128)S(1)} %get-tuple-element.39), channel_id=1, replica_groups=mesh['row'=8,'au'=8,'vert'=8] {'row'}, dimensions={0} | all-to-all | bytes 655360 | tf_op jit(solution)/shard_map/all_to_all | solution.py:582
  27.7 3.2 %collective-permute-start.2 = (f32[62,8,128]{2,1,0:T(8,128)S(1)}, f32[62,8,128]{2,1,0:T(8,128)S(1)}, u32[]{:S(2)}, u32[]{:S(2)}) collective-permute-start(f32[62,8,128]{2,1,0:T(8,128)S(1)} %get-tuple-element.41), channel_id=1, source_target_pairs={{0,8},{8,16},{16,24},{24,32},{32,40},{40,48},{48,56},{1,9},{9,17},... | collective-permute-start | bytes 761864 | tf_op jit(solution)/shard_map/ppermute | solution.py:584
  30.9 1.3 %collective-permute-start.3 = (f32[62,8,128]{2,1,0:T(8,128)S(1)}, f32[62,8,128]{2,1,0:T(8,128)S(1)}, u32[]{:S(2)}, u32[]{:S(2)}) collective-permute-start(f32[62,8,128]{2,1,0:T(8,128)S(1)} %get-tuple-element.42), channel_id=1, source_target_pairs={{8,0},{16,8},{24,16},{32,24},{40,32},{48,40},{56,48},{9,1},{17,9},... | collective-permute-start | bytes 761864 | tf_op jit(solution)/shard_map/ppermute | solution.py:585
  32.2 1.9 %collective-permute-done.2.from_low = f32[62,8,128]{2,1,0:T(8,128)S(1)} collective-permute-done((f32[62,8,128]{2,1,0:T(8,128)S(1)}, f32[62,8,128]{2,1,0:T(8,128)S(1)}, u32[]{:S(2)}, u32[]{:S(2)}) %collective-permute-start.2) | collective-permute-done | bytes 253984 | tf_op jit(solution)/shard_map/ppermute | solution.py:584
  34.1 3.8 %collective-permute-done.3.from_high = f32[62,8,128]{2,1,0:T(8,128)S(1)} collective-permute-done((f32[62,8,128]{2,1,0:T(8,128)S(1)}, f32[62,8,128]{2,1,0:T(8,128)S(1)}, u32[]{:S(2)}, u32[]{:S(2)}) %collective-permute-start.3) | collective-permute-done | bytes 253984 | tf_op jit(solution)/shard_map/ppermute | solution.py:585
  38.0 4.1 %shard_map.88 = (f32[34,56,128]{2,1,0:T(8,128)S(1)}, f32[32,40,128]{2,1,0:T(8,128)S(1)}, f32[32,40,128]{2,1,0:T(8,128)S(1)}, f32[16,20,128]{2,1,0:T(8,128)S(1)},...) custom-call(f32[8,5,16,128]{3,2,1,0:T(8,128)S(1)} %all_to_all.15.got, ...), custom_call_target="tpu_custom_call" | custom-call | tf_op jit(solution)/shard_map/pallas_call | solution.py:593
  42.0 3.5 %collective-permute-start.4 = (f32[24,8,128]{2,1,0:T(8,128)S(1)}, f32[24,8,128]{2,1,0:T(8,128)S(1)}, u32[]{:S(2)}, u32[]{:S(2)}) collective-permute-start(f32[24,8,128]{2,1,0:T(8,128)S(1)} %get-tuple-element.51), channel_id=1, source_target_pairs={{0,8},{8,16},{16,24},{24,32},{32,40},{40,48},{48,56},{1,9},{9,17},... | collective-permute-start | bytes 294920 | tf_op jit(solution)/shard_map/ppermute | solution.py:602
  45.5 1.3 %collective-permute-start.5 = (f32[24,8,128]{2,1,0:T(8,128)S(1)}, f32[24,8,128]{2,1,0:T(8,128)S(1)}, u32[]{:S(2)}, u32[]{:S(2)}) collective-permute-start(f32[24,8,128]{2,1,0:T(8,128)S(1)} %get-tuple-element.52), channel_id=1, source_target_pairs={{8,0},{16,8},{24,16},{32,24},{40,32},{48,40},{56,48},{9,1},{17,9},... | collective-permute-start | bytes 294920 | tf_op jit(solution)/shard_map/ppermute | solution.py:603
  46.8 0.2 shard_map.89
  47.0 0.2 collective-permute-done.4.from_low
  47.1 4.6 %collective-permute-done.5.from_high = f32[24,8,128]{2,1,0:T(8,128)S(1)} collective-permute-done((f32[24,8,128]{2,1,0:T(8,128)S(1)}, f32[24,8,128]{2,1,0:T(8,128)S(1)}, u32[]{:S(2)}, u32[]{:S(2)}) %collective-permute-start.5) | collective-permute-done | bytes 98336 | tf_op jit(solution)/shard_map/ppermute | solution.py:603
  51.8 3.3 %shard_map.90 = f32[8,40,128]{2,1,0:T(8,128)S(1)} custom-call(f32[34,56,128]{2,1,0:T(8,128)S(1)} %get-tuple-element.43.g, f32[32,40,128]{2,1,0:T(8,128)S(1)} %get-tuple-element.44.c, f32[32,40,128]{2,1,0:T(8,128)S(1)} %get-tuple-element.45.big, f32[16,20,128]{2,1,0:T(8,128)S(1)} %get-tuple-element.46.cc, f32[16,20,128]{2,1,0:T(8,128)S(1)} %get-tuple-element.47.kc, ...), custom_call_target="tpu_custom_call" | custom-call | tf_op jit(solution)/shard_map/pallas_call | solution.py:607
  55.1 10.7 %all_to_all.16.got = f32[8,40,128]{2,1,0:T(8,128)S(1)} all-to-all(f32[8,40,128]{2,1,0:T(8,128)S(1)} %shard_map.90), channel_id=1, replica_groups=mesh['row'=8,'au'=8,'vert'=8] {'row'}, dimensions={0} | all-to-all | bytes 327680 | tf_op jit(solution)/shard_map/all_to_all | solution.py:612
  65.7 0.8 shard_map.91
  66.5 30.5 %all_to_all.17.parts = f32[64,1,640]{2,1,0:T(1,128)S(1)} all-to-all(f32[64,1,640]{2,1,0:T(1,128)S(1)} %get-tuple-element.59), channel_id=1, replica_groups=mesh['row'=8,'au'=8,'vert'=8] {'au','vert'}, dimensions={0} | all-to-all | bytes 327680 | tf_op jit(solution)/shard_map/all_to_all | solution.py:614
  97.1 0.7 shard_map.92
  (1 shorter events, 0.0 us)
Async XLA Ops:
  0.6 0.7 copy-start
  1.4 0.7 copy-start.1
  3.1 8.3 %collective-permute-start.1 = (f32[3,16,128]{2,1,0:T(8,128)S(1)}, f32[3,16,128]{2,1,0:T(8,128)S(1)}, u32[]{:S(2)}, u32[]{:S(2)}) collective-permute-start(f32[3,16,128]{2,1,0:T(8,128)S(1)} %get-tuple-element.37.left), channel_id=1, source_target_pairs={{1,0},{2,1},{3,2},{4,3},{5,4},{6,5},{7,6},{0,7},{9,8},{10,9},{11,1... | collective-permute-start | bytes 73736 | tf_op jit(solution)/shard_map/ppermute | solution.py:573
  10.0 1.5 %collective-permute-start = (f32[3,16,128]{2,1,0:T(8,128)S(1)}, f32[3,16,128]{2,1,0:T(8,128)S(1)}, u32[]{:S(2)}, u32[]{:S(2)}) collective-permute-start(f32[3,16,128]{2,1,0:T(8,128)S(1)} %get-tuple-element.38.right), channel_id=1, source_target_pairs={{0,1},{1,2},{2,3},{3,4},{4,5},{5,6},{6,7},{7,0},{8,9},{9,10},{10,1... | collective-permute-start | bytes 73736 | tf_op jit(solution)/shard_map/ppermute | solution.py:572
  10.0 0.7 copy-start.2
  27.7 6.4 %collective-permute-start.2 = (f32[62,8,128]{2,1,0:T(8,128)S(1)}, f32[62,8,128]{2,1,0:T(8,128)S(1)}, u32[]{:S(2)}, u32[]{:S(2)}) collective-permute-start(f32[62,8,128]{2,1,0:T(8,128)S(1)} %get-tuple-element.41), channel_id=1, source_target_pairs={{0,8},{8,16},{16,24},{24,32},{32,40},{40,48},{48,56},{1,9},{9,17},... | collective-permute-start | bytes 761864 | tf_op jit(solution)/shard_map/ppermute | solution.py:584
  30.9 7.0 %collective-permute-start.3 = (f32[62,8,128]{2,1,0:T(8,128)S(1)}, f32[62,8,128]{2,1,0:T(8,128)S(1)}, u32[]{:S(2)}, u32[]{:S(2)}) collective-permute-start(f32[62,8,128]{2,1,0:T(8,128)S(1)} %get-tuple-element.42), channel_id=1, source_target_pairs={{8,0},{16,8},{24,16},{32,24},{40,32},{48,40},{56,48},{9,1},{17,9},... | collective-permute-start | bytes 761864 | tf_op jit(solution)/shard_map/ppermute | solution.py:585
  42.0 5.1 %collective-permute-start.4 = (f32[24,8,128]{2,1,0:T(8,128)S(1)}, f32[24,8,128]{2,1,0:T(8,128)S(1)}, u32[]{:S(2)}, u32[]{:S(2)}) collective-permute-start(f32[24,8,128]{2,1,0:T(8,128)S(1)} %get-tuple-element.51), channel_id=1, source_target_pairs={{0,8},{8,16},{16,24},{24,32},{32,40},{40,48},{48,56},{1,9},{9,17},... | collective-permute-start | bytes 294920 | tf_op jit(solution)/shard_map/ppermute | solution.py:602
  45.5 6.3 %collective-permute-start.5 = (f32[24,8,128]{2,1,0:T(8,128)S(1)}, f32[24,8,128]{2,1,0:T(8,128)S(1)}, u32[]{:S(2)}, u32[]{:S(2)}) collective-permute-start(f32[24,8,128]{2,1,0:T(8,128)S(1)} %get-tuple-element.52), channel_id=1, source_target_pairs={{8,0},{16,8},{24,16},{32,24},{40,32},{48,40},{56,48},{9,1},{17,9},... | collective-permute-start | bytes 294920 | tf_op jit(solution)/shard_map/ppermute | solution.py:603

commit v4 on v3

--- a/solution.py
+++ b/solution.py
@@ -21,11 +21,14 @@
 TOP = 8
 HALF = WINDOW // 2
 HALF_ROWS = 40
+INNER = 24
+SKIP = 8
+NARROW = 8
 PAD_ROWS = WINDOW + 2 * TOP
 TILES = 40
 F32 = jnp.float32
-VMEM_LIMIT = 48 * 1024 * 1024
-EDGE_LIMIT = 56290000
+VMEM_LIMIT = 24 * 1024 * 1024
+EDGE_LIMIT = 56360000
 
 
 def lanes_of(shape):
@@ -50,15 +53,27 @@
     return jax.ShapeDtypeStruct(shape, F32)
 
 
-def edge_kernel(vel_in, log_in, lab_in, seg_in, left, right, plate, vel, log, lab, seg, sems):
+def edge_kernel(vel_in, log_in, left, right, vel, log, sems):
     copies = [
         pltpu.make_async_copy(source, target, sems.at[number])
-        for number, (source, target) in enumerate(((vel_in, vel), (log_in, log), (lab_in, lab), (seg_in, seg)))
+        for number, (source, target) in enumerate(((vel_in, vel), (log_in, log)))
     ]
     for copy in copies:
         copy.start()
     for copy in copies:
         copy.wait()
+    slot = lanes_of((OWN, LANES)) // PART
+    for group, field in enumerate((vel, log)):
+        first = field[0, :, 0:LANES]
+        last = turn(field[0, :, LANES : 2 * LANES], MARGIN)
+        for row in range(1, 4):
+            first = jnp.where(slot == row, turn(field[row, :, 0:LANES], PART * row), first)
+            last = jnp.where(slot == row, turn(field[row, :, LANES : 2 * LANES], PART * row + MARGIN), last)
+        left[group] = first
+        right[group] = last
+
+
+def plate_kernel(lab, seg, plate, left, right, label_window):
     for top in (0, 8):
         for half in range(2):
             labels = lab[top : top + 8, half * LANES : (half + 1) * LANES]
@@ -70,17 +85,11 @@
                 got = jnp.take_along_axis(table, low, axis=1, mode="promise_in_bounds")
                 value = jnp.where(high == part, got, value)
             plate[top : top + 8, half * LANES : (half + 1) * LANES] = value
-    slot = lanes_of((OWN, LANES)) // PART
-    for group, field in enumerate((vel, log)):
-        first = field[0, :, 0:LANES]
-        last = turn(field[0, :, LANES : 2 * LANES], MARGIN)
-        for row in range(1, 4):
-            first = jnp.where(slot == row, turn(field[row, :, 0:LANES], PART * row), first)
-            last = jnp.where(slot == row, turn(field[row, :, LANES : 2 * LANES], PART * row + MARGIN), last)
-        left[group] = first
-        right[group] = last
-    left[2] = plate[:, 0:LANES]
-    right[2] = turn(plate[:, LANES : 2 * LANES], MARGIN)
+    left[...] = plate[:, 0:LANES]
+    right[...] = turn(plate[:, LANES : 2 * LANES], MARGIN)
+    part = lax.axis_index("row")
+    labels = jnp.where(part >= 4, lab[:, LANES : 2 * LANES], lab[:, 0:LANES])
+    label_window[...] = pltpu.roll(labels, (LANES + MARGIN - NARROW - PART * (part % 4)) % LANES, 1)
 
 
 PIECES = (
@@ -129,24 +138,25 @@
             send[part, tile] = tiles[tile]
 
 
-def patch_kernel(sent, plate, lab, left, right, from_left, from_right, send, plate_window, label_window):
+def inner(edge, own, group, low):
+    place = lanes_of((OWN, LANES)) % PART
+    near, next_one = (MARGIN - 1, MARGIN - 2) if low else (0, 1)
+    if group == 0:
+        return jnp.where((place == near) | (place == next_one), 0.0, edge)
+    sign = 1 if low else -1
+    edge = jnp.where(place == near, turn(own, sign * (MARGIN - 1)), edge)
+    return jnp.where(place == next_one, turn(own, sign * (MARGIN - 3)), edge)
+
+
+def patch_kernel(sent, left, right, from_left, from_right, send):
     lane = lanes_of((OWN, LANES))
-    place = lane % PART
     first = lax.axis_index("vert") == 0
     last = lax.axis_index("vert") == lax.axis_size("vert") - 1
     before, after = [], []
-    for group in range(3):
+    for group in range(2):
         low, high = from_left[group], from_right[group]
-        if group == 0:
-            low_inner = jnp.where(place >= MARGIN - 2, 0.0, low)
-            high_inner = jnp.where(place < 2, 0.0, high)
-        else:
-            low_inner = jnp.where(place == MARGIN - 1, turn(left[group], MARGIN - 1), low)
-            low_inner = jnp.where(place == MARGIN - 2, turn(left[group], MARGIN - 3), low_inner)
-            high_inner = jnp.where(place == 0, turn(right[group], 1 - MARGIN), high)
-            high_inner = jnp.where(place == 1, turn(right[group], 3 - MARGIN), high_inner)
-        before.append(jnp.where(first, low_inner, low))
-        after.append(jnp.where(last, high_inner, high))
+        before.append(jnp.where(first, inner(low, left[group], group, True), low))
+        after.append(jnp.where(last, inner(high, right[group], group, False), high))
     for part in range(1, 7):
         send[part] = sent[part]
     for part, edges, begin, stop in ((0, before, 0, MARGIN), (7, after, SPAN - MARGIN, SPAN)):
@@ -163,32 +173,27 @@
                 tiles[tile] = jnp.where((lane >= low + shift) & (lane < high + shift), moved, tiles[tile])
         for tile in range(5):
             send[part, tile] = tiles[tile]
+
+
+def rows_kernel(got, plate, left, right, from_left, from_right, up, down, plate_window):
+    lane = lanes_of((OWN, LANES))
+    first = lax.axis_index("vert") == 0
+    last = lax.axis_index("vert") == lax.axis_size("vert") - 1
+    before = jnp.where(first, inner(from_left[...], left[...], 1, True), from_left[...])
+    after = jnp.where(last, inner(from_right[...], right[...], 1, False), from_right[...])
     part = lax.axis_index("row")
     shift = PART * (part % 4)
     one, two = turn(plate[:, 0:LANES], MARGIN), turn(plate[:, LANES : 2 * LANES], MARGIN)
     head = lane < MARGIN
-    tiles = (
-        jnp.where(head, before[2], one),
-        jnp.where(head, one, two),
-        jnp.where(head, two, turn(after[2], MARGIN)),
-    )
+    tiles = (jnp.where(head, before, one), jnp.where(head, one, two), jnp.where(head, two, turn(after, MARGIN)))
     late = part >= 4
     here = jnp.where(late, tiles[1], tiles[0])
     there = jnp.where(late, tiles[2], tiles[1])
     back = (LANES - shift) % LANES
-    plate_window[...] = jnp.where(lane < LANES - shift, pltpu.roll(here, back, 1), pltpu.roll(there, back, 1))
-    labels = jnp.where(late, lab[:, LANES : 2 * LANES], lab[:, 0:LANES])
-    label_window[...] = pltpu.roll(labels, (LANES + MARGIN - shift) % LANES, 1)
-
-
-def rows_kernel(got, plate_window, up, down):
-    def tile(index):
-        if index < TILES:
-            return got[index // 5, index % 5]
-        return plate_window[...]
-
+    window = jnp.where(lane < LANES - shift, pltpu.roll(here, back, 1), pltpu.roll(there, back, 1))
+    plate_window[...] = window
     for index in range(TILES + 1):
-        values = tile(index)
+        values = got[index // 5, index % 5] if index < TILES else window
         at = TILES + 1 + index // 2
         half = 4 * (index % 2)
         up[index] = values[8:16]
@@ -230,10 +235,10 @@
     )
 
 
-def around(ref, at, rows=WINDOW, reach=1):
-    centre, low, high, left, right = four(ref, at, rows, reach)
+def around(ref, at, rows=WINDOW, reach=1, top=TOP):
+    centre, low, high, left, right = four(ref, at, rows, reach, top)
     total = (low + high) + (left + right)
-    return centre, total + (middle(ref, at - 1, rows) + middle(ref, at + 1, rows))
+    return centre, total + (middle(ref, at - 1, rows, top) + middle(ref, at + 1, rows, top))
 
 
 def pair_sum(spare, even_lane):
@@ -241,58 +246,82 @@
     return total + jnp.where(even_lane, turn(total, -1), turn(total, 1))
 
 
-def clear_edges(refs, rows=WINDOW):
+def clear_edges(refs, rows=WINDOW, skip=0):
     row = jnp.zeros((1, LANES), F32)
     slab = jnp.zeros((rows, LANES), F32)
+    top = TOP + skip
     for ref in refs:
         last = ref.shape[0] - 1
         for at in range(1, last):
-            ref[at, TOP - 1 : TOP, :] = row
-            ref[at, TOP + rows : TOP + rows + 1, :] = row
-        ref[0, TOP : TOP + rows, :] = slab
-        ref[last, TOP : TOP + rows, :] = slab
-
-
-def smooth(out, values, source, factor, count, rows=WINDOW, reach=1):
-    for at in range(count):
-        centre, total = around(values, at + 1, rows, reach)
+            ref[at, top - 1 : top, :] = row
+            ref[at, top + rows : top + rows + 1, :] = row
+        ref[0, top : top + rows, :] = slab
+        ref[last, top : top + rows, :] = slab
+
+
+def join(ref, rows=WINDOW, skip=0):
+    top = TOP + skip
+    last = ref.shape[0] - 2
+    low = lanes_of((rows, LANES)) < 64
+    ref[0, top : top + rows, :] = jnp.where(low, 0.0, turn(middle(ref, last, rows, top), 64))
+    ref[last + 1, top : top + rows, :] = jnp.where(low, turn(middle(ref, 1, rows, top), 64), 0.0)
+
+
+def smooth(out, values, source, factor, rows=WINDOW, reach=1, skip=0):
+    top = TOP + skip
+    for at in range(out.shape[0] - 2):
+        centre, total = around(values, at + 1, rows, reach, top)
         if source is None:
-            result = (1.0 + KEEP) * centre + factor[at] * total
+            result = (1.0 + KEEP) * centre
         else:
-            result = (KEEP * centre + middle(source, at + 1, rows)) + factor[at] * total
-        out[at + 1, TOP : TOP + rows, :] = result
-
-
-def vcycle(f, one, two, zf, za, zb, spare, g, c, big, cc, kc, ginv):
+            result = KEEP * centre + middle(source, at + 1, rows, top)
+        out[at + 1, top : top + rows, :] = result + factor[at, skip : skip + rows, :] * total
+
+
+def vcycle(f, one, two, zf, za, zb, spare, g, g_top, c, big, cc, kc, ginv, joined):
     even_lane = lanes_of((HALF, LANES)) % 2 == 0
-    coarse = (LAYERS // 2, HALF, 2)
-    smooth(two, f, None, c, LAYERS)
+    count = zf.shape[0] - 2
+
+    def close(ref, rows=WINDOW, skip=0):
+        if joined:
+            join(ref, rows, skip)
+
+    smooth(two, f, None, c)
+    close(two)
 
     def leftover(at):
         centre, total = around(two, at + 1)
         return big[at] * ((middle(f, at + 1) - DAMPING * centre) + c[at] * total)
 
-    for at in range(LAYERS // 2):
+    for at in range(count):
         spare[at] = leftover(2 * at) + leftover(2 * at + 1)
-    for at in range(LAYERS // 2):
+    for at in range(count):
         zf[at + 1, TOP : TOP + HALF, :] = kc[at] * pair_sum(spare.at[at], even_lane)
-    smooth(za, zf, None, cc, *coarse)
-    smooth(zb, za, zf, cc, *coarse)
-    smooth(za, zb, zf, cc, *coarse)
-    for at in range(LAYERS // 2):
-        value = middle(za, at + 1, HALF) * ginv[at]
-        spare[at, pl.ds(0, HALF, 2), :] = value
-        spare[at, pl.ds(1, HALF, 2), :] = value
-    for at in range(LAYERS // 2):
-        value = spare[at]
+    close(zf, HALF)
+    smooth(za, zf, None, cc, HALF, 2)
+    close(za, HALF)
+    smooth(zb, za, zf, cc, HALF, 2)
+    close(zb, HALF)
+    smooth(za, zb, zf, cc, 16, 2)
+    for at in range(count):
+        value = middle(za, at + 1, 16) * ginv[at, 0:16, :]
+        spare[at, pl.ds(0, 16, 2), :] = value
+        spare[at, pl.ds(1, 16, 2), :] = value
+    top = TOP + SKIP
+    for at in range(count):
+        value = spare[at, SKIP : SKIP + INNER, :]
         for row in (2 * at + 1, 2 * at + 2):
-            one[row, TOP : TOP + WINDOW, :] = middle(two, row) + middle(g, row) * value
-    smooth(two, one, f, c, LAYERS)
-    smooth(one, two, f, c, LAYERS)
+            one[row, top : top + INNER, :] = (
+                middle(two, row, INNER, top) + middle(g, row, INNER, g_top + SKIP) * value
+            )
+    close(one, INNER, SKIP)
+    smooth(two, one, f, c, INNER, 1, SKIP)
+    close(two, INNER, SKIP)
+    smooth(one, two, f, c, INNER, 1, SKIP)
 
 
 def depth_at(at):
-    place = jnp.full((8, LANES), at, jnp.int32)
+    place = jnp.zeros((8, LANES), jnp.int32) + at
     return jnp.exp(-(LAYERS - 1 - place).astype(F32) / (LAYERS / 4.0))
 
 
@@ -307,7 +336,8 @@
 ):
     domain = places()[-1]
     coarse_domain = places(HALF)[-1]
-    clear_edges((f, one, two, vel, g))
+    clear_edges((f, two, vel, g))
+    clear_edges((one,), INNER, SKIP)
     clear_edges((zf, za, zb, gc), HALF)
     for index in range(TILES + 1):
         a, b, d, e = rows_of(index, from_low, from_high, TILES + 1)
@@ -371,8 +401,8 @@
         ginv[at] = 1.0 / centre
 
     plate = packed[TILES]
-    one[1, TOP : TOP + WINDOW, :] = plate
-    beside = [plate + other for other in four(one, 1)[1:]]
+    two[1, TOP : TOP + WINDOW, :] = plate
+    beside = [plate + other for other in four(two, 1)[1:]]
     across_layers = None
     for at in range(LAYERS):
         g_mid, *g_four = four(g, at + 1)
@@ -398,7 +428,7 @@
         c[at] = g_mid * per
         big[at] = total_g * (1.0 / DAMPING)
         f[at + 1, TOP : TOP + WINDOW, :] = -0.5 * total * per
-    vcycle(f, one, two, zf, za, zb, spare, g, c, big, cc, kc, ginv)
+    vcycle(f, one, two, zf, za, zb, spare, g, TOP, c, big, cc, kc, ginv, False)
 
     own_lane = lanes_of((OWN, LANES))
     sent = []
@@ -408,7 +438,7 @@
         x_own[at] = x
         sent.append(-(x * (c[at, HALO : HALO + OWN, :] * ratio)))
     for index in range(16):
-        both = jnp.where(own_lane < 64, turn(sent[2 * index], -8), turn(sent[2 * index + 1], 56))
+        both = jnp.where(own_lane < 64, turn(sent[index], -NARROW), turn(sent[index + 16], 64 - NARROW))
         start = 4 * (index % 2)
         f_own[index] = both
         f_up[index] = both[8:16]
@@ -417,7 +447,10 @@
         f_down[16 + index // 2, start : start + 4, :] = both[8:12]
 
 
-def side_kernel(x_own, label_window, inc, ones):
+def side_kernel(
+    g, c, big, cc, kc, ginv, vel, x_own, label_window,
+    inc, ones, g_two, c_two, big_two, cc_two, kc_two, ginv_two, vel_two,
+):
     slot = lanes_of((OWN, LANES)) // PART
     for part in range(8):
         tile = turn(x_own[4 * part], -MARGIN)
@@ -429,10 +462,15 @@
     for at in range(OWN):
         hit = jnp.where(low[at : at + 1, :] == place, 1.0, 0.0)
         ones[:, at * LANES : (at + 1) * LANES] = hit.astype(jnp.bfloat16)
-
-
-INNER = 24
-SKIP = 8
+    for source, target in ((g, g_two), (vel, vel_two), (c, c_two), (big, big_two), (cc, cc_two), (kc, kc_two), (ginv, ginv_two)):
+        rows = target.shape[1]
+        top = TOP if source.shape[1] == PAD_ROWS else 0
+        first = lanes_of((rows, LANES)) < 64
+        for at in range(target.shape[0]):
+            upper = at + (8 if rows == HALF else 16)
+            target[at] = jnp.where(
+                first, turn(middle(source, at, rows, top), -NARROW), turn(middle(source, upper, rows, top), 64 - NARROW)
+            )
 
 
 def second_kernel(
@@ -440,30 +478,32 @@
     send,
     f, one, two, zf, za, zb, spare, layers,
 ):
-    _, lane, _, _, _, _, domain = places()
-    clear_edges((f, one, two))
+    count = LAYERS // 2
+    clear_edges((f, two))
+    clear_edges((one,), INNER, SKIP)
     clear_edges((zf, za, zb), HALF)
-    for index in range(16):
+    for index in range(count):
         start = 4 * (index % 2)
-        spare[index, 0:4, :] = from_low[16 + index // 2, start : start + 4, :]
-        spare[index, 4:12, :] = from_low[index]
-        spare[index, 28:36, :] = from_high[index]
-        spare[index, 36:40, :] = from_high[16 + index // 2, start : start + 4, :]
-        spare[index, HALO : HALO + OWN, :] = f_own[index]
-    for index in range(16):
-        both = spare[index]
-        for row, shift in ((0, 8), (1, 72)):
-            f[2 * index + row + 1, TOP : TOP + WINDOW, :] = jnp.where(domain, turn(both, shift), 0.0)
-    vcycle(f, one, two, zf, za, zb, spare, g, c, big, cc, kc, ginv)
+        at = index + 1
+        f[at, TOP : TOP + 4, :] = from_low[16 + index // 2, start : start + 4, :]
+        f[at, TOP + 4 : TOP + 12, :] = from_low[index]
+        f[at, TOP + HALO : TOP + HALO + OWN, :] = f_own[index]
+        f[at, TOP + 28 : TOP + 36, :] = from_high[index]
+        f[at, TOP + 36 : TOP + 40, :] = from_high[16 + index // 2, start : start + 4, :]
+    join(f)
+    vcycle(f, one, two, zf, za, zb, spare, g, 0, c, big, cc, kc, ginv, True)
 
     top = TOP + SKIP
-    for at in range(LAYERS):
-        two[at + 1, top : top + INNER, :] = middle(one, at + 1, INNER, top) / middle(g, at + 1, INNER, top)
+    for at in range(count):
+        two[at + 1, top : top + INNER, :] = middle(one, at + 1, INNER, top) / middle(g, at + 1, INNER, SKIP)
+    join(two, INNER, SKIP)
     row_at = SKIP + lax.broadcasted_iota(jnp.int32, (INNER, LANES), 0)
     lane = lanes_of((INNER, LANES))
+    low = lane < 64
+    place = lane % 64 + NARROW
     across = row_at + (lax.axis_index("au") * OWN - HALO)
-    along = lane + (lax.axis_index("vert") * (8 * PART) + lax.axis_index("row") * PART - MARGIN)
-    own = (row_at >= HALO) & (row_at < HALO + OWN) & (lane >= MARGIN) & (lane < MARGIN + PART)
+    along = place + (lax.axis_index("vert") * (8 * PART) + lax.axis_index("row") * PART - MARGIN)
+    own = (row_at >= HALO) & (row_at < HALO + OWN) & (place >= MARGIN) & (place < MARGIN + PART)
     shares = [
         jnp.where(edge, 1.0, 0.5)
         for edge in (
@@ -474,23 +514,29 @@
         )
     ]
     column = jnp.zeros((INNER, LANES), F32)
-    for at in range(LAYERS):
-        g_mid, *g_four = four(g, at + 1, INNER, 1, top)
-        v_mid, *v_four = four(vel, at + 1, INNER, 1, top)
+    upper = (lanes_of((8, LANES)) >= 64).astype(jnp.int32) * count
+    for at in range(count):
+        g_mid, *g_four = four(g, at + 1, INNER, 1, SKIP)
+        v_mid, *v_four = four(vel, at + 1, INNER, 1, SKIP)
         x_mid, *x_four = four(two, at + 1, INNER, 1, top)
         total = jnp.zeros((INNER, LANES), F32)
         for share, g_n, v_n, x_n in zip(shares, g_four, v_four, x_four):
             total = total + (share * g_n) * ((x_n - x_mid) * (v_n - v_mid))
-        for other, end in ((at, 0), (at + 2, LAYERS + 1)):
-            share = 1.0 if other == end else 0.5
-            x_n, v_n = middle(two, other, INNER, top), middle(vel, other, INNER, top)
-            total = total + (share * middle(g, other, INNER, top)) * ((x_n - x_mid) * (v_n - v_mid))
+        for other in (at, at + 2):
+            share = 0.5
+            if other == 0:
+                share = jnp.where(low, 1.0, 0.5)
+            if other == count + 1:
+                share = jnp.where(low, 0.5, 1.0)
+            x_n, v_n = middle(two, other, INNER, top), middle(vel, other, INNER, SKIP)
+            total = total + (share * middle(g, other, INNER, SKIP)) * ((x_n - x_mid) * (v_n - v_mid))
         total = jnp.where(own, g_mid * total, 0.0)
-        column = column + tall(depth_at(at), INNER) * total
+        column = column + tall(depth_at(upper + at), INNER) * total
         layers[at] = jnp.sum(total.reshape(INNER // 8, 8, LANES), axis=0)
     level = jnp.sum(layers[...], axis=1)
 
     high = label_window[...] >> 7
+    column = jnp.where(low, column + turn(column, 64), 0.0)
     sums = column[HALO - SKIP : HALO - SKIP + OWN, :]
     kind = lax.broadcasted_iota(jnp.int32, (4, LANES), 0)
     left = []
@@ -506,28 +552,22 @@
     segments = (product[0:4] + product[4:8]) + product[8:12]
 
     slot = lanes_of((OWN, LANES)) // PART
+    lower = lanes_of((4, LANES)) < 64
     for part in range(8):
-        tile = turn(two[4 * part + 1, TOP + HALO : TOP + HALO + OWN, :], -MARGIN)
-        for row in range(1, 4):
-            x = two[4 * part + row + 1, TOP + HALO : TOP + HALO + OWN, :]
-            tile = jnp.where(slot == row, turn(x, PART * row - MARGIN), tile)
+        half, at = part // 4, 4 * (part % 4)
+        tile = None
+        for row in range(4):
+            x = two[at + row + 1, TOP + HALO : TOP + HALO + OWN, :]
+            x = turn(x, PART * row - (MARGIN - NARROW) - 64 * half)
+            tile = x if tile is None else jnp.where(slot == row, x, tile)
         send[part, 0:16, :] = inc[part]
         send[part, 16:32, :] = tile
         send[part, 32:36, :] = segments
-        send[part, 36:40, :] = level[4 * part : 4 * part + 4, :]
-
-
-def place_kernel(got, inc, adj, spread):
-    lane = lanes_of((OWN, LANES))
-    slot = lane // PART
-    for out, start in ((inc, 0), (adj, 16)):
-        for row in range(4):
-            for half in range(2):
-                tile = jnp.zeros((OWN, LANES), F32)
-                for source in range(4):
-                    piece = got[4 * half + source, start : start + 16, :]
-                    tile = jnp.where(slot == source, turn(piece, PART * (source - row)), tile)
-                out[row, :, half * LANES : (half + 1) * LANES] = tile
+        here = level[at : at + 4, :]
+        send[part, 36:40, :] = jnp.where(lower, 0.0, here) if half else jnp.where(lower, here, 0.0)
+
+
+def sum_kernel(got, spread):
     total = got[0, 32:40, :]
     for source in range(1, 8):
         total = total + got[source, 32:40, :]
@@ -541,7 +581,17 @@
         spread[other] = line
 
 
-def total_kernel(parts, segments, layers):
+def place_kernel(got, parts, inc, adj, segments, layers):
+    lane = lanes_of((OWN, LANES))
+    slot = lane // PART
+    for out, start in ((inc, 0), (adj, 16)):
+        for row in range(4):
+            for half in range(2):
+                tile = jnp.zeros((OWN, LANES), F32)
+                for source in range(4):
+                    piece = got[4 * half + source, start : start + 16, :]
+                    tile = jnp.where(slot == source, turn(piece, PART * (source - row)), tile)
+                out[row, :, half * LANES : (half + 1) * LANES] = tile
     cells = LAYERS * lax.axis_size("au") * OWN * lax.axis_size("vert") * 8 * PART
     total = jnp.sum(parts[...], axis=0)
     for row in range(4):
@@ -558,61 +608,73 @@
     downward = [(i + 1, i) for i in range(across - 1)]
     vmem = pl.BlockSpec(memory_space=pltpu.VMEM)
     hbm = pl.BlockSpec(memory_space=pltpu.HBM)
-    labels_like = jax.ShapeDtypeStruct((OWN, 2 * LANES), jnp.int32)
     label_tile = jax.ShapeDtypeStruct((OWN, LANES), jnp.int32)
-    edges, field = sds(3, OWN, LANES), sds(4, OWN, 2 * LANES)
-
-    left, right, plate, vel, log, lab = call(
+    tile, pair, field = sds(OWN, LANES), sds(2, OWN, LANES), sds(4, OWN, 2 * LANES)
+
+    left, right, vel, log = call(
         edge_kernel,
-        (edges, edges, sds(OWN, 2 * LANES), field, field, labels_like),
-        [pltpu.VMEM((4, LANES), F32), pltpu.SemaphoreType.DMA((4,))],
-        in_specs=[hbm] * 4,
+        (pair, pair, field, field),
+        [pltpu.SemaphoreType.DMA((2,))],
+        in_specs=[hbm] * 2,
         limit=EDGE_LIMIT,
-    )(velocity, log_visc, labels, seg_dir.reshape(4, LANES))
+    )(velocity, log_visc)
     from_left = lax.ppermute(right, "vert", ahead)
     from_right = lax.ppermute(left, "vert", back)
+    plate, plate_left, plate_right, label_window = call(
+        plate_kernel, (sds(OWN, 2 * LANES), tile, tile, label_tile)
+    )(labels, seg_dir.reshape(4, LANES))
+    plate_before = lax.ppermute(plate_right, "vert", ahead)
+    plate_after = lax.ppermute(plate_left, "vert", back)
     send = call(
         window_kernel,
         sds(8, 5, OWN, LANES),
         in_specs=[vmem, vmem, pl.BlockSpec(memory_space=pltpu.SMEM)],
     )(vel, log, layer_dir)
-    send, plate_window, label_window = call(
-        patch_kernel, (sds(8, 5, OWN, LANES), sds(OWN, LANES), label_tile)
-    )(send, plate, lab, left, right, from_left, from_right)
+    send = call(patch_kernel, sds(8, 5, OWN, LANES))(send, left, right, from_left, from_right)
     got = lax.all_to_all(send, "row", 0, 0, tiled=True)
-    up, down = call(rows_kernel, (sds(62, 8, LANES), sds(62, 8, LANES)))(got, plate_window)
+    up, down, plate_window = call(rows_kernel, (sds(62, 8, LANES), sds(62, 8, LANES), tile))(
+        got, plate, plate_left, plate_right, plate_before, plate_after
+    )
     from_low = lax.ppermute(up, "au", upward)
     from_high = lax.ppermute(down, "au", downward)
     fine = sds(LAYERS, WINDOW, LANES)
     fine_padded = sds(LAYERS + 2, PAD_ROWS, LANES)
     coarse = sds(LAYERS // 2, HALF, LANES)
-    own = sds(LAYERS, OWN, LANES)
-    fine_scratch = pltpu.VMEM((LAYERS + 2, PAD_ROWS, LANES), F32)
-    coarse_scratch = pltpu.VMEM((LAYERS // 2 + 2, HALF_ROWS, LANES), F32)
-    spare = pltpu.VMEM((LAYERS // 2, WINDOW, LANES), F32)
+
+    def scratch(layers):
+        return (
+            [pltpu.VMEM((layers + 2, PAD_ROWS, LANES), F32)] * 3
+            + [pltpu.VMEM((layers // 2 + 2, HALF_ROWS, LANES), F32)] * 3
+            + [pltpu.VMEM((layers // 2, WINDOW, LANES), F32)]
+        )
+
     *factors, x_own, f_own, f_up, f_down = call(
         first_kernel,
         (fine_padded, fine, fine, coarse, coarse, coarse, fine_padded)
-        + (own, sds(LAYERS // 2, OWN, LANES), sds(24, 8, LANES), sds(24, 8, LANES)),
+        + (sds(LAYERS, OWN, LANES), sds(LAYERS // 2, OWN, LANES), sds(24, 8, LANES), sds(24, 8, LANES)),
         [pltpu.VMEM((TILES + 1, WINDOW, LANES), F32)]
-        + [fine_scratch] * 3
-        + [coarse_scratch] * 3
-        + [spare, pltpu.VMEM((LAYERS + 2, 8, LANES), F32), coarse_scratch],
+        + scratch(LAYERS)
+        + [pltpu.VMEM((LAYERS + 2, 8, LANES), F32), pltpu.VMEM((LAYERS // 2 + 2, HALF_ROWS, LANES), F32)],
     )(got, plate_window, from_low, from_high)
     from_low = lax.ppermute(f_up, "au", upward)
     from_high = lax.ppermute(f_down, "au", downward)
-    inc, ones = call(
-        side_kernel, (sds(8, OWN, LANES), jax.ShapeDtypeStruct((LANES, OWN * LANES), jnp.bfloat16))
-    )(x_own, label_window)
-    send = call(
-        second_kernel,
-        sds(8, 40, LANES),
-        [fine_scratch] * 3 + [coarse_scratch] * 3 + [spare, pltpu.VMEM((LAYERS, 8, LANES), F32)],
-    )(*factors, f_own, from_low, from_high, inc, label_window, ones)
+    fine = sds(LAYERS // 2, WINDOW, LANES)
+    fine_closed = sds(LAYERS // 2 + 2, WINDOW, LANES)
+    coarse = sds(LAYERS // 4, HALF, LANES)
+    inc, ones, *factors = call(
+        side_kernel,
+        (sds(8, OWN, LANES), jax.ShapeDtypeStruct((LANES, OWN * LANES), jnp.bfloat16))
+        + (fine_closed, fine, fine, coarse, coarse, coarse, fine_closed),
+    )(*factors, x_own, label_window)
+    send = call(second_kernel, sds(8, 40, LANES), scratch(LAYERS // 2) + [pltpu.VMEM((LAYERS // 2, 8, LANES), F32)])(
+        *factors, f_own, from_low, from_high, inc, label_window, ones
+    )
     got = lax.all_to_all(send, "row", 0, 0, tiled=True)
-    increment, adjoint, spread = call(place_kernel, (field, field, sds(across * vert, 1, 5 * LANES)))(got)
+    spread = call(sum_kernel, sds(across * vert, 1, 5 * LANES))(got)
     parts = lax.all_to_all(spread, ("au", "vert"), 0, 0, tiled=True)
-    hv_segments, hv_layers = call(total_kernel, (sds(4, LANES), sds(1, 4)))(parts)
+    increment, adjoint, hv_segments, hv_layers = call(place_kernel, (field, field, sds(4, LANES), sds(1, 4)))(
+        got, parts
+    )
     return increment, adjoint, hv_segments.reshape(NSEG), hv_layers.reshape(4)
 
 

time: 98.2 us -> 95.8 us (0.976)
  blocking collectives: 57.2 us -> 41.2 us
  starting transfers between devices: 16.2 us -> 26.3 us
  waiting for transfers between devices: 10.5 us -> 15.6 us
  local copies, waits for them, and re-layouts: 2.05 us -> 0.66 us
    all_to_all x2 -> x1, blocking collectives: 26.7 us -> 10.7 us  [shards(): got = lax.all_to_all(send, 'row', 0, 0, tiled=True)]
    all_to_all x0 -> x1, starting transfers between devices: none -> 6.19 us  [shards(): got = lax.all_to_all(send, 'row', 0, 0, tiled=True)]
    all_to_all x0 -> x1, waiting for transfers between devices: none -> 4.81 us  [shards(): got = lax.all_to_all(send, 'row', 0, 0, tiled=True)]
    ppermute x0 -> x2, starting transfers between devices: none -> 3.99 us  [the longest x1 3.99 us: shards(): plate_after = lax.ppermute(plate_left, 'vert', back)]
    unnamed x6, local copies, waits for them, and re-layouts: 2.05 us -> 0.66 us
    ppermute x0 -> x2, waiting for transfers between devices: none -> 1.17 us  [the longest x1 0.83 us: shards(): plate_after = lax.ppermute(plate_left, 'vert', back)]
    pallas_call x6 -> x7, Pallas kernels: 6.13 us -> 5.26 us  [the longest x1 2.14 us: shards(): call(second_kernel, sds(8, 40, LANES), scratch(LAYERS // 2) + [pltpu.VMEM...]
  transfers between devices with their start and end apart: 6 -> 9, of which waited for: 4 -> 6; matrix products, arithmetic and copies ran while one was open for 0% -> 0% of each run, Pallas kernels for 1% -> 2%
where the time goes in v4:
time: 95.8 us; the launch traced here: 95.3 us
  blocking collectives  41.2 us (43%)
  starting transfers between devices  26.3 us (27%)
  waiting for transfers between devices  15.6 us (16%)
  Pallas kernels  10.8 us (11%)
    all_to_all x1, blocking collectives, shards(): parts = lax.all_to_all(spread, ('au', 'vert'), 0, 0, tiled=True)  30.5 us
    all_to_all x1, blocking collectives, shards(): got = lax.all_to_all(send, 'row', 0, 0, tiled=True)  10.7 us
    ppermute x1, starting transfers between devices, shards(): from_right = lax.ppermute(left, 'vert', back)  6.89 us
    all_to_all x1, starting transfers between devices, shards(): got = lax.all_to_all(send, 'row', 0, 0, tiled=True)  6.19 us
    all_to_all x1, waiting for transfers between devices, shards(): got = lax.all_to_all(send, 'row', 0, 0, tiled=True)  4.81 us
    ppermute x1, starting transfers between devices, shards(): plate_after = lax.ppermute(plate_left, 'vert', back)  3.99 us
    ppermute x1, waiting for transfers between devices, shards(): from_high = lax.ppermute(f_down, 'au', downward)  3.89 us
    ppermute x1, waiting for transfers between devices, shards(): from_high = lax.ppermute(down, 'au', downward)  3.83 us
  transfers between devices with their start and end apart: 9, of which 6 were waited for; matrix products, arithmetic and copies ran while one was open for 0% of the time, Pallas kernels for 2%

profile of v4, /device:TPU:1, one launch (start us, length us, event | category | flops | bytes accessed | tf_op | source)
XLA Modules:
  0.0 95.3 jit_solution(5527159114735412978)
XLA Ops:
  0.6 1.0 %shard_map.84 = (f32[2,16,128]{2,1,0:T(8,128)S(1)}, f32[2,16,128]{2,1,0:T(8,128)S(1)}, f32[4,16,256]{2,1,0:T(8,128)S(1)}, f32[4,16,256]{2,1,0:T(8,128)S(1)}) custom-call(f32[4,16,256]{2,1,0:T(8,128)} %vel_in.1, f32[4,16,256]{2,1,0:T(8,128)} %log_in.1), custom_call_target="tpu_custom_call" | custom-call | tf_op jit(solution)/shard_map/pallas_call | solution.py:614
  1.6 6.9 %collective-permute-start.1 = (f32[2,16,128]{2,1,0:T(8,128)S(1)}, f32[2,16,128]{2,1,0:T(8,128)S(1)}, u32[]{:S(2)}, u32[]{:S(2)}) collective-permute-start(f32[2,16,128]{2,1,0:T(8,128)S(1)} %get-tuple-element.41.left), channel_id=1, source_target_pairs={{1,0},{2,1},{3,2},{4,3},{5,4},{6,5},{7,6},{0,7},{9,8},{10,9},{11,1... | collective-permute-start | bytes 49160 | tf_op jit(solution)/shard_map/ppermute | solution.py:622
  8.5 0.0 collective-permute-start
  8.5 0.0 copy-start.2
  8.5 0.7 copy-done.2
  9.2 0.8 shard_map.85.sent
  10.0 0.0 collective-permute-done.1.from_right
  10.0 0.0 collective-permute-done.from_left
  10.0 0.9 shard_map.86
  10.9 0.0 copy-start
  10.9 0.0 copy-start.1
  10.9 6.2 %all-to-all-start = ((f32[8,5,16,128]{3,2,1,0:T(8,128)}), f32[8,5,16,128]{3,2,1,0:T(8,128)S(1)}, u32[]{:S(2)}, u32[]{:S(2)}) async-start(f32[8,5,16,128]{3,2,1,0:T(8,128)} %shard_map.86), calls=%async_computation | async-start | bytes 655360 | tf_op jit(solution)/shard_map/all_to_all | solution.py:634
  17.1 0.0 copy-done
  17.1 0.0 copy-done.1
  17.1 0.1 shard_map.87
  17.2 4.0 %collective-permute-start.3 = (f32[16,128]{1,0:T(8,128)S(1)}, f32[16,128]{1,0:T(8,128)S(1)}, u32[]{:S(2)}, u32[]{:S(2)}) collective-permute-start(f32[16,128]{1,0:T(8,128)S(1)} %get-tuple-element.44.left), channel_id=1, source_target_pairs={{1,0},{2,1},{3,2},{4,3},{5,4},{6,5},{7,6},{0,7},{9,8},{10,9},{11,1... | collective-permute-start | bytes 24584 | tf_op jit(solution)/shard_map/ppermute | solution.py:627
  21.2 0.0 collective-permute-start.2
  21.2 0.8 collective-permute-done.3.from_right
  22.0 0.3 collective-permute-done.2.from_left
  22.4 4.8 %all-to-all-done.got = f32[8,5,16,128]{3,2,1,0:T(8,128)S(1)} async-done(((f32[8,5,16,128]{3,2,1,0:T(8,128)}), f32[8,5,16,128]{3,2,1,0:T(8,128)S(1)}, u32[]{:S(2)}, u32[]{:S(2)}) %all-to-all-start) | async-done | bytes 327712 | tf_op jit(solution)/shard_map/all_to_all | solution.py:634
  27.2 0.2 shard_map.88
  27.4 3.2 %collective-permute-start.4 = (f32[62,8,128]{2,1,0:T(8,128)S(1)}, f32[62,8,128]{2,1,0:T(8,128)S(1)}, u32[]{:S(2)}, u32[]{:S(2)}) collective-permute-start(f32[62,8,128]{2,1,0:T(8,128)S(1)} %get-tuple-element.47), channel_id=1, source_target_pairs={{0,8},{8,16},{16,24},{24,32},{32,40},{40,48},{48,56},{1,9},{9,17},... | collective-permute-start | bytes 761864 | tf_op jit(solution)/shard_map/ppermute | solution.py:638
  30.6 1.3 %collective-permute-start.5 = (f32[62,8,128]{2,1,0:T(8,128)S(1)}, f32[62,8,128]{2,1,0:T(8,128)S(1)}, u32[]{:S(2)}, u32[]{:S(2)}) collective-permute-start(f32[62,8,128]{2,1,0:T(8,128)S(1)} %get-tuple-element.48), channel_id=1, source_target_pairs={{8,0},{16,8},{24,16},{32,24},{40,32},{48,40},{56,48},{9,1},{17,9},... | collective-permute-start | bytes 761864 | tf_op jit(solution)/shard_map/ppermute | solution.py:639
  31.9 1.9 %collective-permute-done.4.from_low = f32[62,8,128]{2,1,0:T(8,128)S(1)} collective-permute-done((f32[62,8,128]{2,1,0:T(8,128)S(1)}, f32[62,8,128]{2,1,0:T(8,128)S(1)}, u32[]{:S(2)}, u32[]{:S(2)}) %collective-permute-start.4) | collective-permute-done | bytes 253984 | tf_op jit(solution)/shard_map/ppermute | solution.py:638
  33.8 3.8 %collective-permute-done.5.from_high = f32[62,8,128]{2,1,0:T(8,128)S(1)} collective-permute-done((f32[62,8,128]{2,1,0:T(8,128)S(1)}, f32[62,8,128]{2,1,0:T(8,128)S(1)}, u32[]{:S(2)}, u32[]{:S(2)}) %collective-permute-start.5) | collective-permute-done | bytes 253984 | tf_op jit(solution)/shard_map/ppermute | solution.py:639
  37.7 3.7 %shard_map.89 = (f32[34,56,128]{2,1,0:T(8,128)S(1)}, f32[32,40,128]{2,1,0:T(8,128)S(1)}, f32[32,40,128]{2,1,0:T(8,128)S(1)}, f32[16,20,128]{2,1,0:T(8,128)S(1)},...) custom-call(f32[8,5,16,128]{3,2,1,0:T(8,128)S(1)} %all-to-all-done.g, ...), custom_call_target="tpu_custom_call" | custom-call | tf_op jit(solution)/shard_map/pallas_call | solution.py:651
  41.3 3.5 %collective-permute-start.6 = (f32[24,8,128]{2,1,0:T(8,128)S(1)}, f32[24,8,128]{2,1,0:T(8,128)S(1)}, u32[]{:S(2)}, u32[]{:S(2)}) collective-permute-start(f32[24,8,128]{2,1,0:T(8,128)S(1)} %get-tuple-element.66), channel_id=1, source_target_pairs={{0,8},{8,16},{16,24},{24,32},{32,40},{40,48},{48,56},{1,9},{9,17},... | collective-permute-start | bytes 294920 | tf_op jit(solution)/shard_map/ppermute | solution.py:659
  44.8 1.3 %collective-permute-start.7 = (f32[24,8,128]{2,1,0:T(8,128)S(1)}, f32[24,8,128]{2,1,0:T(8,128)S(1)}, u32[]{:S(2)}, u32[]{:S(2)}) collective-permute-start(f32[24,8,128]{2,1,0:T(8,128)S(1)} %get-tuple-element.67), channel_id=1, source_target_pairs={{8,0},{16,8},{24,16},{32,24},{40,32},{48,40},{56,48},{9,1},{17,9},... | collective-permute-start | bytes 294920 | tf_op jit(solution)/shard_map/ppermute | solution.py:660
  46.1 1.1 %shard_map.90 = (f32[8,16,128]{2,1,0:T(8,128)S(1)}, bf16[128,2048]{1,0:T(8,128)(2,1)S(1)}, f32[18,40,128]{2,1,0:T(8,128)S(1)}, f32[16,40,128]{2,1,0:T(8,128)S(1)...) custom-call(f32[34,56,128]{2,1,0:T(8,128)S(1)} %get-tuple-element.49, ...), custom_call_target="tpu_custom_call" | custom-call | tf_op jit(solution)/shard_map/pallas_call | solution.py:664
  47.2 0.0 collective-permute-done.6.from_low
  47.2 3.9 %collective-permute-done.7.from_high = f32[24,8,128]{2,1,0:T(8,128)S(1)} collective-permute-done((f32[24,8,128]{2,1,0:T(8,128)S(1)}, f32[24,8,128]{2,1,0:T(8,128)S(1)}, u32[]{:S(2)}, u32[]{:S(2)}) %collective-permute-start.7) | collective-permute-done | bytes 98336 | tf_op jit(solution)/shard_map/ppermute | solution.py:660
  51.1 2.1 %shard_map.91 = f32[8,40,128]{2,1,0:T(8,128)S(1)} custom-call(f32[18,40,128]{2,1,0:T(8,128)S(1)} %get-tuple-element.58.g, f32[16,40,128]{2,1,0:T(8,128)S(1)} %get-tuple-element.59.c, f32[16,40,128]{2,1,0:T(8,128)S(1)} %get-tuple-element.60.big, f32[8,20,128]{2,1,0:T(8,128)S(1)} %get-tuple-element.61.cc, f32[8,20,128]{2,1,0:T(8,128)S(1)} %get-tuple-element.62.kc, ...), custom_call_target="tpu_custom_call" | custom-call | tf_op jit(solution)/shard_map/pallas_call | solution.py:669
  53.2 10.7 %all_to_all.15.got = f32[8,40,128]{2,1,0:T(8,128)S(1)} all-to-all(f32[8,40,128]{2,1,0:T(8,128)S(1)} %shard_map.91), channel_id=1, replica_groups=mesh['row'=8,'au'=8,'vert'=8] {'row'}, dimensions={0} | all-to-all | bytes 327680 | tf_op jit(solution)/shard_map/all_to_all | solution.py:672
  63.9 0.1 shard_map.92
  64.0 30.5 %all_to_all.16.parts = f32[64,1,640]{2,1,0:T(1,128)S(1)} all-to-all(f32[64,1,640]{2,1,0:T(1,128)S(1)} %shard_map.92), channel_id=1, replica_groups=mesh['row'=8,'au'=8,'vert'=8] {'au','vert'}, dimensions={0} | all-to-all | bytes 327680 | tf_op jit(solution)/shard_map/all_to_all | solution.py:674
  94.5 0.8 shard_map.93
Async XLA Ops:
  1.6 8.3 %collective-permute-start.1 = (f32[2,16,128]{2,1,0:T(8,128)S(1)}, f32[2,16,128]{2,1,0:T(8,128)S(1)}, u32[]{:S(2)}, u32[]{:S(2)}) collective-permute-start(f32[2,16,128]{2,1,0:T(8,128)S(1)} %get-tuple-element.41.left), channel_id=1, source_target_pairs={{1,0},{2,1},{3,2},{4,3},{5,4},{6,5},{7,6},{0,7},{9,8},{10,9},{11,1... | collective-permute-start | bytes 49160 | tf_op jit(solution)/shard_map/ppermute | solution.py:622
  8.5 1.5 %collective-permute-start = (f32[2,16,128]{2,1,0:T(8,128)S(1)}, f32[2,16,128]{2,1,0:T(8,128)S(1)}, u32[]{:S(2)}, u32[]{:S(2)}) collective-permute-start(f32[2,16,128]{2,1,0:T(8,128)S(1)} %get-tuple-element.42.right), channel_id=1, source_target_pairs={{0,1},{1,2},{2,3},{3,4},{4,5},{5,6},{6,7},{7,0},{8,9},{9,10},{10,1... | collective-permute-start | bytes 49160 | tf_op jit(solution)/shard_map/ppermute | solution.py:621
  8.5 0.7 copy-start.2
  10.9 6.2 %copy-start = (s32[16,256]{1,0:T(8,128)S(1)}, s32[16,256]{1,0:T(8,128)}, u32[]{:S(2)}) copy-start(s32[16,256]{1,0:T(8,128)} %lab.1) | copy-start | bytes 49156
  10.9 6.2 %copy-start.1 = (f32[512]{0:T(512)S(1)}, f32[512]{0:T(512)}, u32[]{:S(2)}) copy-start(f32[512]{0:T(512)} %param.8) | copy-start | bytes 6148
  10.9 16.3 %all-to-all-start = ((f32[8,5,16,128]{3,2,1,0:T(8,128)}), f32[8,5,16,128]{3,2,1,0:T(8,128)S(1)}, u32[]{:S(2)}, u32[]{:S(2)}) async-start(f32[8,5,16,128]{3,2,1,0:T(8,128)} %shard_map.86), calls=%async_computation | async-start | bytes 655360 | tf_op jit(solution)/shard_map/all_to_all | solution.py:634
  17.2 4.8 %collective-permute-start.3 = (f32[16,128]{1,0:T(8,128)S(1)}, f32[16,128]{1,0:T(8,128)S(1)}, u32[]{:S(2)}, u32[]{:S(2)}) collective-permute-start(f32[16,128]{1,0:T(8,128)S(1)} %get-tuple-element.44.left), channel_id=1, source_target_pairs={{1,0},{2,1},{3,2},{4,3},{5,4},{6,5},{7,6},{0,7},{9,8},{10,9},{11,1... | collective-permute-start | bytes 24584 | tf_op jit(solution)/shard_map/ppermute | solution.py:627
  21.2 1.2 %collective-permute-start.2 = (f32[16,128]{1,0:T(8,128)S(1)}, f32[16,128]{1,0:T(8,128)S(1)}, u32[]{:S(2)}, u32[]{:S(2)}) collective-permute-start(f32[16,128]{1,0:T(8,128)S(1)} %get-tuple-element.45.right), channel_id=1, source_target_pairs={{0,1},{1,2},{2,3},{3,4},{4,5},{5,6},{6,7},{7,0},{8,9},{9,10},{10,1... | collective-permute-start | bytes 24584 | tf_op jit(solution)/shard_map/ppermute | solution.py:626
  27.4 6.4 %collective-permute-start.4 = (f32[62,8,128]{2,1,0:T(8,128)S(1)}, f32[62,8,128]{2,1,0:T(8,128)S(1)}, u32[]{:S(2)}, u32[]{:S(2)}) collective-permute-start(f32[62,8,128]{2,1,0:T(8,128)S(1)} %get-tuple-element.47), channel_id=1, source_target_pairs={{0,8},{8,16},{16,24},{24,32},{32,40},{40,48},{48,56},{1,9},{9,17},... | collective-permute-start | bytes 761864 | tf_op jit(solution)/shard_map/ppermute | solution.py:638
  30.6 7.0 %collective-permute-start.5 = (f32[62,8,128]{2,1,0:T(8,128)S(1)}, f32[62,8,128]{2,1,0:T(8,128)S(1)}, u32[]{:S(2)}, u32[]{:S(2)}) collective-permute-start(f32[62,8,128]{2,1,0:T(8,128)S(1)} %get-tuple-element.48), channel_id=1, source_target_pairs={{8,0},{16,8},{24,16},{32,24},{40,32},{48,40},{56,48},{9,1},{17,9},... | collective-permute-start | bytes 761864 | tf_op jit(solution)/shard_map/ppermute | solution.py:639
  41.3 5.8 %collective-permute-start.6 = (f32[24,8,128]{2,1,0:T(8,128)S(1)}, f32[24,8,128]{2,1,0:T(8,128)S(1)}, u32[]{:S(2)}, u32[]{:S(2)}) collective-permute-start(f32[24,8,128]{2,1,0:T(8,128)S(1)} %get-tuple-element.66), channel_id=1, source_target_pairs={{0,8},{8,16},{16,24},{24,32},{32,40},{40,48},{48,56},{1,9},{9,17},... | collective-permute-start | bytes 294920 | tf_op jit(solution)/shard_map/ppermute | solution.py:659
  44.8 6.3 %collective-permute-start.7 = (f32[24,8,128]{2,1,0:T(8,128)S(1)}, f32[24,8,128]{2,1,0:T(8,128)S(1)}, u32[]{:S(2)}, u32[]{:S(2)}) collective-permute-start(f32[24,8,128]{2,1,0:T(8,128)S(1)} %get-tuple-element.67), channel_id=1, source_target_pairs={{8,0},{16,8},{24,16},{32,24},{40,32},{48,40},{56,48},{9,1},{17,9},... | collective-permute-start | bytes 294920 | tf_op jit(solution)/shard_map/ppermute | solution.py:660

commit v5 on v4

--- a/solution.py
+++ b/solution.py
@@ -21,6 +21,7 @@
 TOP = 8
 HALF = WINDOW // 2
 HALF_ROWS = 40
+HALF_TALL = 24
 INNER = 24
 SKIP = 8
 NARROW = 8
@@ -74,6 +75,7 @@
 
 
 def plate_kernel(lab, seg, plate, left, right, label_window):
+    tables = seg[...]
     for top in (0, 8):
         for half in range(2):
             labels = lab[top : top + 8, half * LANES : (half + 1) * LANES]
@@ -81,7 +83,7 @@
             high = labels >> 7
             value = jnp.zeros((8, LANES), F32)
             for part in range(4):
-                table = jnp.broadcast_to(seg[part : part + 1, :], (8, LANES))
+                table = jnp.broadcast_to(tables[part : part + 1, :], (8, LANES))
                 got = jnp.take_along_axis(table, low, axis=1, mode="promise_in_bounds")
                 value = jnp.where(high == part, got, value)
             plate[top : top + 8, half * LANES : (half + 1) * LANES] = value
@@ -224,21 +226,29 @@
     return ref[at, top : top + rows, :]
 
 
-def four(ref, at, rows=WINDOW, reach=1, top=TOP):
-    centre = middle(ref, at, rows, top)
-    return (
-        centre,
-        ref[at, top - 1 : top - 1 + rows, :],
-        ref[at, top + 1 : top + 1 + rows, :],
-        turn(centre, reach),
-        turn(centre, -reach),
-    )
-
-
-def around(ref, at, rows=WINDOW, reach=1, top=TOP):
-    centre, low, high, left, right = four(ref, at, rows, reach, top)
-    total = (low + high) + (left + right)
-    return centre, total + (middle(ref, at - 1, rows, top) + middle(ref, at + 1, rows, top))
+def four(ref, at):
+    centre = middle(ref, at)
+    low, high = ref[at, TOP - 1 : TOP - 1 + WINDOW, :], ref[at, TOP + 1 : TOP + 1 + WINDOW, :]
+    return low, high, turn(centre, 1), turn(centre, -1)
+
+
+def slabs(ref, rows=WINDOW, reach=1, top=TOP):
+    before, centre = middle(ref, 0, rows, top), middle(ref, 1, rows, top)
+    for at in range(ref.shape[0] - 2):
+        after = middle(ref, at + 2, rows, top)
+        beside = (
+            ref[at + 1, top - 1 : top - 1 + rows, :],
+            ref[at + 1, top + 1 : top + 1 + rows, :],
+            turn(centre, reach),
+            turn(centre, -reach),
+        )
+        yield at, centre, beside, (before, after)
+        before, centre = centre, after
+
+
+def around(ref, rows=WINDOW, reach=1, top=TOP):
+    for at, centre, (low, high, left, right), (before, after) in slabs(ref, rows, reach, top):
+        yield at, centre, ((low + high) + (left + right)) + (before + after)
 
 
 def pair_sum(spare, even_lane):
@@ -269,8 +279,7 @@
 
 def smooth(out, values, source, factor, rows=WINDOW, reach=1, skip=0):
     top = TOP + skip
-    for at in range(out.shape[0] - 2):
-        centre, total = around(values, at + 1, rows, reach, top)
+    for at, centre, total in around(values, rows, reach, top):
         if source is None:
             result = (1.0 + KEEP) * centre
         else:
@@ -289,14 +298,14 @@
     smooth(two, f, None, c)
     close(two)
 
-    def leftover(at):
-        centre, total = around(two, at + 1)
-        return big[at] * ((middle(f, at + 1) - DAMPING * centre) + c[at] * total)
-
+    first = None
+    for at, centre, total in around(two):
+        leftover = big[at] * ((middle(f, at + 1) - DAMPING * centre) + c[at] * total)
+        if at % 2:
+            spare[at // 2] = first + leftover
+        first = leftover
     for at in range(count):
-        spare[at] = leftover(2 * at) + leftover(2 * at + 1)
-    for at in range(count):
-        zf[at + 1, TOP : TOP + HALF, :] = kc[at] * pair_sum(spare.at[at], even_lane)
+        zf[at + 1, TOP : TOP + HALF, :] = kc[at, 0:HALF, :] * pair_sum(spare.at[at], even_lane)
     close(zf, HALF)
     smooth(za, zf, None, cc, HALF, 2)
     close(za, HALF)
@@ -393,36 +402,33 @@
     gc[0] = gc[1]
     gc[LAYERS // 2 + 1] = gc[LAYERS // 2]
 
-    for at in range(LAYERS // 2):
-        centre, total = around(gc, at + 1, HALF, 2)
+    for at, centre, total in around(gc, HALF, 2):
         per = jnp.where(coarse_domain, DAMPING / total, 0.0)
-        cc[at] = centre * per
-        kc[at] = (0.125 / COARSE_FACTOR) * per
-        ginv[at] = 1.0 / centre
+        for ref, value in ((cc, centre * per), (kc, (0.125 / COARSE_FACTOR) * per), (ginv, 1.0 / centre)):
+            ref[at, 0:HALF, :] = value
+            ref[at, HALF:HALF_TALL, :] = jnp.zeros((HALF_TALL - HALF, LANES), F32)
 
     plate = packed[TILES]
     two[1, TOP : TOP + WINDOW, :] = plate
-    beside = [plate + other for other in four(two, 1)[1:]]
+    beside = [plate + other for other in four(two, 1)]
     across_layers = None
-    for at in range(LAYERS):
-        g_mid, *g_four = four(g, at + 1)
-        v_mid, *v_four = four(vel, at + 1)
+    for (at, g_mid, g_four, g_two), (_, v_mid, v_four, v_two) in zip(slabs(g), slabs(vel)):
         depth = depth_at(at)
         level = layer[at + 1]
         depth_tall, twice = tall(depth), tall(2.0 * level)
         total_g = (g_four[0] + g_four[1]) + (g_four[2] + g_four[3])
-        total_g = total_g + (middle(g, at) + middle(g, at + 2))
+        total_g = total_g + (g_two[0] + g_two[1])
         total = jnp.zeros((WINDOW, LANES), F32)
         for g_n, v_n, s_n in zip(g_four, v_four, beside):
             total = total + g_n * (depth_tall * s_n + twice) * (v_mid - v_n)
         total = g_mid * total
-        for other in (at, at + 2):
+        for other, g_n, v_n in zip((at, at + 2), g_two, v_two):
             place = min(max(other - 1, 0), LAYERS - 1)
             if other == at and at > 0:
                 total = total - across_layers
                 continue
             scale = tall(depth + depth_at(place)) * plate + tall(level + layer[other])
-            across_layers = (g_mid * middle(g, other)) * scale * (v_mid - middle(vel, other))
+            across_layers = (g_mid * g_n) * scale * (v_mid - v_n)
             total = total + across_layers
         per = jnp.where(domain, DAMPING / total_g, 0.0)
         c[at] = g_mid * per
@@ -467,7 +473,7 @@
         top = TOP if source.shape[1] == PAD_ROWS else 0
         first = lanes_of((rows, LANES)) < 64
         for at in range(target.shape[0]):
-            upper = at + (8 if rows == HALF else 16)
+            upper = at + (8 if rows == HALF_TALL else 16)
             target[at] = jnp.where(
                 first, turn(middle(source, at, rows, top), -NARROW), turn(middle(source, upper, rows, top), 64 - NARROW)
             )
@@ -515,21 +521,18 @@
     ]
     column = jnp.zeros((INNER, LANES), F32)
     upper = (lanes_of((8, LANES)) >= 64).astype(jnp.int32) * count
-    for at in range(count):
-        g_mid, *g_four = four(g, at + 1, INNER, 1, SKIP)
-        v_mid, *v_four = four(vel, at + 1, INNER, 1, SKIP)
-        x_mid, *x_four = four(two, at + 1, INNER, 1, top)
+    walk = zip(slabs(g, INNER, 1, SKIP), slabs(vel, INNER, 1, SKIP), slabs(two, INNER, 1, top))
+    for (at, g_mid, g_four, g_two), (_, v_mid, v_four, v_two), (_, x_mid, x_four, x_two) in walk:
         total = jnp.zeros((INNER, LANES), F32)
         for share, g_n, v_n, x_n in zip(shares, g_four, v_four, x_four):
             total = total + (share * g_n) * ((x_n - x_mid) * (v_n - v_mid))
-        for other in (at, at + 2):
+        for other, g_n, v_n, x_n in zip((at, at + 2), g_two, v_two, x_two):
             share = 0.5
             if other == 0:
                 share = jnp.where(low, 1.0, 0.5)
             if other == count + 1:
                 share = jnp.where(low, 0.5, 1.0)
-            x_n, v_n = middle(two, other, INNER, top), middle(vel, other, INNER, SKIP)
-            total = total + (share * middle(g, other, INNER, SKIP)) * ((x_n - x_mid) * (v_n - v_mid))
+            total = total + (share * g_n) * ((x_n - x_mid) * (v_n - v_mid))
         total = jnp.where(own, g_mid * total, 0.0)
         column = column + tall(depth_at(upper + at), INNER) * total
         layers[at] = jnp.sum(total.reshape(INNER // 8, 8, LANES), axis=0)
@@ -562,9 +565,9 @@
             tile = x if tile is None else jnp.where(slot == row, x, tile)
         send[part, 0:16, :] = inc[part]
         send[part, 16:32, :] = tile
-        send[part, 32:36, :] = segments
         here = level[at : at + 4, :]
-        send[part, 36:40, :] = jnp.where(lower, 0.0, here) if half else jnp.where(lower, here, 0.0)
+        here = jnp.where(lower, 0.0, here) if half else jnp.where(lower, here, 0.0)
+        send[part, 32:40, :] = jnp.concatenate([segments, here], axis=0)
 
 
 def sum_kernel(got, spread):
@@ -594,8 +597,8 @@
                 out[row, :, half * LANES : (half + 1) * LANES] = tile
     cells = LAYERS * lax.axis_size("au") * OWN * lax.axis_size("vert") * 8 * PART
     total = jnp.sum(parts[...], axis=0)
-    for row in range(4):
-        segments[row : row + 1, :] = total[:, row * LANES : (row + 1) * LANES] * (1.0 / (cells / NSEG) ** 0.5)
+    lines = [total[:, row * LANES : (row + 1) * LANES] for row in range(4)]
+    segments[...] = jnp.concatenate(lines, axis=0) * (1.0 / (cells / NSEG) ** 0.5)
     layers[...] = total[:, 4 * LANES : 4 * LANES + 4] * (1.0 / (cells / LAYERS) ** 0.5)
 
 
@@ -639,20 +642,20 @@
     from_high = lax.ppermute(down, "au", downward)
     fine = sds(LAYERS, WINDOW, LANES)
     fine_padded = sds(LAYERS + 2, PAD_ROWS, LANES)
-    coarse = sds(LAYERS // 2, HALF, LANES)
+    coarse = sds(LAYERS // 2, HALF_TALL, LANES)
 
     def scratch(layers):
         return (
             [pltpu.VMEM((layers + 2, PAD_ROWS, LANES), F32)] * 3
             + [pltpu.VMEM((layers // 2 + 2, HALF_ROWS, LANES), F32)] * 3
-            + [pltpu.VMEM((layers // 2, WINDOW, LANES), F32)]
+            + [pltpu.VMEM((layers // 2 + 1, WINDOW, LANES), F32)]
         )
 
     *factors, x_own, f_own, f_up, f_down = call(
         first_kernel,
         (fine_padded, fine, fine, coarse, coarse, coarse, fine_padded)
-        + (sds(LAYERS, OWN, LANES), sds(LAYERS // 2, OWN, LANES), sds(24, 8, LANES), sds(24, 8, LANES)),
-        [pltpu.VMEM((TILES + 1, WINDOW, LANES), F32)]
+        + (sds(LAYERS, OWN, LANES), sds(LAYERS // 2, OWN, LANES), sds(25, 8, LANES), sds(25, 8, LANES)),
+        [pltpu.VMEM((TILES + 2, WINDOW, LANES), F32)]
         + scratch(LAYERS)
         + [pltpu.VMEM((LAYERS + 2, 8, LANES), F32), pltpu.VMEM((LAYERS // 2 + 2, HALF_ROWS, LANES), F32)],
     )(got, plate_window, from_low, from_high)
@@ -660,7 +663,7 @@
     from_high = lax.ppermute(f_down, "au", downward)
     fine = sds(LAYERS // 2, WINDOW, LANES)
     fine_closed = sds(LAYERS // 2 + 2, WINDOW, LANES)
-    coarse = sds(LAYERS // 4, HALF, LANES)
+    coarse = sds(LAYERS // 4, HALF_TALL, LANES)
     inc, ones, *factors = call(
         side_kernel,
         (sds(8, OWN, LANES), jax.ShapeDtypeStruct((LANES, OWN * LANES), jnp.bfloat16))

time: 95.8 us -> 95.8 us (level)
  no operation moved by 1% of the time
where the time goes in v5:
time: 95.8 us; the launch traced here: 95.4 us
  blocking collectives  41.2 us (43%)
  starting transfers between devices  26.3 us (27%)
  waiting for transfers between devices  15.6 us (16%)
  Pallas kernels  10.8 us (11%)
    all_to_all x1, blocking collectives, shards(): parts = lax.all_to_all(spread, ('au', 'vert'), 0, 0, tiled=True)  30.5 us
    all_to_all x1, blocking collectives, shards(): got = lax.all_to_all(send, 'row', 0, 0, tiled=True)  10.7 us
    ppermute x1, starting transfers between devices, shards(): from_right = lax.ppermute(left, 'vert', back)  6.89 us
    all_to_all x1, starting transfers between devices, shards(): got = lax.all_to_all(send, 'row', 0, 0, tiled=True)  6.19 us
    all_to_all x1, waiting for transfers between devices, shards(): got = lax.all_to_all(send, 'row', 0, 0, tiled=True)  4.81 us
    ppermute x1, starting transfers between devices, shards(): plate_after = lax.ppermute(plate_left, 'vert', back)  3.99 us
    ppermute x1, waiting for transfers between devices, shards(): from_high = lax.ppermute(f_down, 'au', downward)  3.93 us
    ppermute x1, waiting for transfers between devices, shards(): from_high = lax.ppermute(down, 'au', downward)  3.83 us
  transfers between devices with their start and end apart: 9, of which 6 were waited for; matrix products, arithmetic and copies ran while one was open for 0% of the time, Pallas kernels for 2%

profile of v5, /device:TPU:1, one launch (start us, length us, event | category | flops | bytes accessed | tf_op | source)
XLA Modules:
  0.0 95.4 jit_solution(11121645111461516916)
XLA Ops:
  0.6 1.0 %shard_map.84 = (f32[2,16,128]{2,1,0:T(8,128)S(1)}, f32[2,16,128]{2,1,0:T(8,128)S(1)}, f32[4,16,256]{2,1,0:T(8,128)S(1)}, f32[4,16,256]{2,1,0:T(8,128)S(1)}) custom-call(f32[4,16,256]{2,1,0:T(8,128)} %vel_in.1, f32[4,16,256]{2,1,0:T(8,128)} %log_in.1), custom_call_target="tpu_custom_call" | custom-call | tf_op jit(solution)/shard_map/pallas_call | solution.py:617
  1.6 6.9 %collective-permute-start.1 = (f32[2,16,128]{2,1,0:T(8,128)S(1)}, f32[2,16,128]{2,1,0:T(8,128)S(1)}, u32[]{:S(2)}, u32[]{:S(2)}) collective-permute-start(f32[2,16,128]{2,1,0:T(8,128)S(1)} %get-tuple-element.41.left), channel_id=1, source_target_pairs={{1,0},{2,1},{3,2},{4,3},{5,4},{6,5},{7,6},{0,7},{9,8},{10,9},{11,1... | collective-permute-start | bytes 49160 | tf_op jit(solution)/shard_map/ppermute | solution.py:625
  8.5 0.0 collective-permute-start
  8.5 0.0 copy-start.2
  8.5 0.7 copy-done.2
  9.2 0.8 shard_map.85.sent
  10.0 0.0 collective-permute-done.1.from_right
  10.0 0.0 collective-permute-done.from_left
  10.0 0.9 shard_map.86
  10.9 0.0 copy-start
  10.9 0.0 copy-start.1
  10.9 6.2 %all-to-all-start = ((f32[8,5,16,128]{3,2,1,0:T(8,128)}), f32[8,5,16,128]{3,2,1,0:T(8,128)S(1)}, u32[]{:S(2)}, u32[]{:S(2)}) async-start(f32[8,5,16,128]{3,2,1,0:T(8,128)} %shard_map.86), calls=%async_computation | async-start | bytes 655360 | tf_op jit(solution)/shard_map/all_to_all | solution.py:637
  17.1 0.0 copy-done
  17.1 0.0 copy-done.1
  17.1 0.1 shard_map.87
  17.2 4.0 %collective-permute-start.3 = (f32[16,128]{1,0:T(8,128)S(1)}, f32[16,128]{1,0:T(8,128)S(1)}, u32[]{:S(2)}, u32[]{:S(2)}) collective-permute-start(f32[16,128]{1,0:T(8,128)S(1)} %get-tuple-element.44.left), channel_id=1, source_target_pairs={{1,0},{2,1},{3,2},{4,3},{5,4},{6,5},{7,6},{0,7},{9,8},{10,9},{11,1... | collective-permute-start | bytes 24584 | tf_op jit(solution)/shard_map/ppermute | solution.py:630
  21.2 0.0 collective-permute-start.2
  21.2 0.8 collective-permute-done.3.from_right
  22.0 0.3 collective-permute-done.2.from_left
  22.4 4.8 %all-to-all-done.got = f32[8,5,16,128]{3,2,1,0:T(8,128)S(1)} async-done(((f32[8,5,16,128]{3,2,1,0:T(8,128)}), f32[8,5,16,128]{3,2,1,0:T(8,128)S(1)}, u32[]{:S(2)}, u32[]{:S(2)}) %all-to-all-start) | async-done | bytes 327712 | tf_op jit(solution)/shard_map/all_to_all | solution.py:637
  27.2 0.2 shard_map.88
  27.4 3.2 %collective-permute-start.4 = (f32[62,8,128]{2,1,0:T(8,128)S(1)}, f32[62,8,128]{2,1,0:T(8,128)S(1)}, u32[]{:S(2)}, u32[]{:S(2)}) collective-permute-start(f32[62,8,128]{2,1,0:T(8,128)S(1)} %get-tuple-element.47), channel_id=1, source_target_pairs={{0,8},{8,16},{16,24},{24,32},{32,40},{40,48},{48,56},{1,9},{9,17},... | collective-permute-start | bytes 761864 | tf_op jit(solution)/shard_map/ppermute | solution.py:641
  30.6 1.3 %collective-permute-start.5 = (f32[62,8,128]{2,1,0:T(8,128)S(1)}, f32[62,8,128]{2,1,0:T(8,128)S(1)}, u32[]{:S(2)}, u32[]{:S(2)}) collective-permute-start(f32[62,8,128]{2,1,0:T(8,128)S(1)} %get-tuple-element.48), channel_id=1, source_target_pairs={{8,0},{16,8},{24,16},{32,24},{40,32},{48,40},{56,48},{9,1},{17,9},... | collective-permute-start | bytes 761864 | tf_op jit(solution)/shard_map/ppermute | solution.py:642
  31.9 1.9 %collective-permute-done.4.from_low = f32[62,8,128]{2,1,0:T(8,128)S(1)} collective-permute-done((f32[62,8,128]{2,1,0:T(8,128)S(1)}, f32[62,8,128]{2,1,0:T(8,128)S(1)}, u32[]{:S(2)}, u32[]{:S(2)}) %collective-permute-start.4) | collective-permute-done | bytes 253984 | tf_op jit(solution)/shard_map/ppermute | solution.py:641
  33.8 3.8 %collective-permute-done.5.from_high = f32[62,8,128]{2,1,0:T(8,128)S(1)} collective-permute-done((f32[62,8,128]{2,1,0:T(8,128)S(1)}, f32[62,8,128]{2,1,0:T(8,128)S(1)}, u32[]{:S(2)}, u32[]{:S(2)}) %collective-permute-start.5) | collective-permute-done | bytes 253984 | tf_op jit(solution)/shard_map/ppermute | solution.py:642
  37.7 3.7 %shard_map.89 = (f32[34,56,128]{2,1,0:T(8,128)S(1)}, f32[32,40,128]{2,1,0:T(8,128)S(1)}, f32[32,40,128]{2,1,0:T(8,128)S(1)}, f32[16,24,128]{2,1,0:T(8,128)S(1)},...) custom-call(f32[8,5,16,128]{3,2,1,0:T(8,128)S(1)} %all-to-all-done.g, ...), custom_call_target="tpu_custom_call" | custom-call | tf_op jit(solution)/shard_map/pallas_call | solution.py:654
  41.4 3.5 %collective-permute-start.6 = (f32[25,8,128]{2,1,0:T(8,128)S(1)}, f32[25,8,128]{2,1,0:T(8,128)S(1)}, u32[]{:S(2)}, u32[]{:S(2)}) collective-permute-start(f32[25,8,128]{2,1,0:T(8,128)S(1)} %get-tuple-element.66), channel_id=1, source_target_pairs={{0,8},{8,16},{16,24},{24,32},{32,40},{40,48},{48,56},{1,9},{9,17},... | collective-permute-start | bytes 307208 | tf_op jit(solution)/shard_map/ppermute | solution.py:662
  44.8 1.3 %collective-permute-start.7 = (f32[25,8,128]{2,1,0:T(8,128)S(1)}, f32[25,8,128]{2,1,0:T(8,128)S(1)}, u32[]{:S(2)}, u32[]{:S(2)}) collective-permute-start(f32[25,8,128]{2,1,0:T(8,128)S(1)} %get-tuple-element.67), channel_id=1, source_target_pairs={{8,0},{16,8},{24,16},{32,24},{40,32},{48,40},{56,48},{9,1},{17,9},... | collective-permute-start | bytes 307208 | tf_op jit(solution)/shard_map/ppermute | solution.py:663
  46.1 1.1 %shard_map.90 = (f32[8,16,128]{2,1,0:T(8,128)S(1)}, bf16[128,2048]{1,0:T(8,128)(2,1)S(1)}, f32[18,40,128]{2,1,0:T(8,128)S(1)}, f32[16,40,128]{2,1,0:T(8,128)S(1)...) custom-call(f32[34,56,128]{2,1,0:T(8,128)S(1)} %get-tuple-element.49, ...), custom_call_target="tpu_custom_call" | custom-call | tf_op jit(solution)/shard_map/pallas_call | solution.py:667
  47.2 0.0 collective-permute-done.6.from_low
  47.2 3.9 %collective-permute-done.7.from_high = f32[25,8,128]{2,1,0:T(8,128)S(1)} collective-permute-done((f32[25,8,128]{2,1,0:T(8,128)S(1)}, f32[25,8,128]{2,1,0:T(8,128)S(1)}, u32[]{:S(2)}, u32[]{:S(2)}) %collective-permute-start.7) | collective-permute-done | bytes 102432 | tf_op jit(solution)/shard_map/ppermute | solution.py:663
  51.1 2.1 %shard_map.91 = f32[8,40,128]{2,1,0:T(8,128)S(1)} custom-call(f32[18,40,128]{2,1,0:T(8,128)S(1)} %get-tuple-element.58.g, f32[16,40,128]{2,1,0:T(8,128)S(1)} %get-tuple-element.59.c, f32[16,40,128]{2,1,0:T(8,128)S(1)} %get-tuple-element.60.big, f32[8,24,128]{2,1,0:T(8,128)S(1)} %get-tuple-element.61.cc, f32[8,24,128]{2,1,0:T(8,128)S(1)} %get-tuple-element.62.kc, ...), custom_call_target="tpu_custom_call" | custom-call | tf_op jit(solution)/shard_map/pallas_call | solution.py:672
  53.2 10.7 %all_to_all.15.got = f32[8,40,128]{2,1,0:T(8,128)S(1)} all-to-all(f32[8,40,128]{2,1,0:T(8,128)S(1)} %shard_map.91), channel_id=1, replica_groups=mesh['row'=8,'au'=8,'vert'=8] {'row'}, dimensions={0} | all-to-all | bytes 327680 | tf_op jit(solution)/shard_map/all_to_all | solution.py:675
  63.9 0.1 shard_map.92
  64.0 30.5 %all_to_all.16.parts = f32[64,1,640]{2,1,0:T(1,128)S(1)} all-to-all(f32[64,1,640]{2,1,0:T(1,128)S(1)} %shard_map.92), channel_id=1, replica_groups=mesh['row'=8,'au'=8,'vert'=8] {'au','vert'}, dimensions={0} | all-to-all | bytes 327680 | tf_op jit(solution)/shard_map/all_to_all | solution.py:677
  94.6 0.8 shard_map.93
Async XLA Ops:
  1.6 8.3 %collective-permute-start.1 = (f32[2,16,128]{2,1,0:T(8,128)S(1)}, f32[2,16,128]{2,1,0:T(8,128)S(1)}, u32[]{:S(2)}, u32[]{:S(2)}) collective-permute-start(f32[2,16,128]{2,1,0:T(8,128)S(1)} %get-tuple-element.41.left), channel_id=1, source_target_pairs={{1,0},{2,1},{3,2},{4,3},{5,4},{6,5},{7,6},{0,7},{9,8},{10,9},{11,1... | collective-permute-start | bytes 49160 | tf_op jit(solution)/shard_map/ppermute | solution.py:625
  8.5 1.5 %collective-permute-start = (f32[2,16,128]{2,1,0:T(8,128)S(1)}, f32[2,16,128]{2,1,0:T(8,128)S(1)}, u32[]{:S(2)}, u32[]{:S(2)}) collective-permute-start(f32[2,16,128]{2,1,0:T(8,128)S(1)} %get-tuple-element.42.right), channel_id=1, source_target_pairs={{0,1},{1,2},{2,3},{3,4},{4,5},{5,6},{6,7},{7,0},{8,9},{9,10},{10,1... | collective-permute-start | bytes 49160 | tf_op jit(solution)/shard_map/ppermute | solution.py:624
  8.5 0.7 copy-start.2
  10.9 6.2 %copy-start = (s32[16,256]{1,0:T(8,128)S(1)}, s32[16,256]{1,0:T(8,128)}, u32[]{:S(2)}) copy-start(s32[16,256]{1,0:T(8,128)} %lab.1) | copy-start | bytes 49156
  10.9 6.2 %copy-start.1 = (f32[512]{0:T(512)S(1)}, f32[512]{0:T(512)}, u32[]{:S(2)}) copy-start(f32[512]{0:T(512)} %param.8) | copy-start | bytes 6148
  10.9 16.3 %all-to-all-start = ((f32[8,5,16,128]{3,2,1,0:T(8,128)}), f32[8,5,16,128]{3,2,1,0:T(8,128)S(1)}, u32[]{:S(2)}, u32[]{:S(2)}) async-start(f32[8,5,16,128]{3,2,1,0:T(8,128)} %shard_map.86), calls=%async_computation | async-start | bytes 655360 | tf_op jit(solution)/shard_map/all_to_all | solution.py:637
  17.2 4.8 %collective-permute-start.3 = (f32[16,128]{1,0:T(8,128)S(1)}, f32[16,128]{1,0:T(8,128)S(1)}, u32[]{:S(2)}, u32[]{:S(2)}) collective-permute-start(f32[16,128]{1,0:T(8,128)S(1)} %get-tuple-element.44.left), channel_id=1, source_target_pairs={{1,0},{2,1},{3,2},{4,3},{5,4},{6,5},{7,6},{0,7},{9,8},{10,9},{11,1... | collective-permute-start | bytes 24584 | tf_op jit(solution)/shard_map/ppermute | solution.py:630
  21.2 1.2 %collective-permute-start.2 = (f32[16,128]{1,0:T(8,128)S(1)}, f32[16,128]{1,0:T(8,128)S(1)}, u32[]{:S(2)}, u32[]{:S(2)}) collective-permute-start(f32[16,128]{1,0:T(8,128)S(1)} %get-tuple-element.45.right), channel_id=1, source_target_pairs={{0,1},{1,2},{2,3},{3,4},{4,5},{5,6},{6,7},{7,0},{8,9},{9,10},{10,1... | collective-permute-start | bytes 24584 | tf_op jit(solution)/shard_map/ppermute | solution.py:629
  27.4 6.4 %collective-permute-start.4 = (f32[62,8,128]{2,1,0:T(8,128)S(1)}, f32[62,8,128]{2,1,0:T(8,128)S(1)}, u32[]{:S(2)}, u32[]{:S(2)}) collective-permute-start(f32[62,8,128]{2,1,0:T(8,128)S(1)} %get-tuple-element.47), channel_id=1, source_target_pairs={{0,8},{8,16},{16,24},{24,32},{32,40},{40,48},{48,56},{1,9},{9,17},... | collective-permute-start | bytes 761864 | tf_op jit(solution)/shard_map/ppermute | solution.py:641
  30.6 7.0 %collective-permute-start.5 = (f32[62,8,128]{2,1,0:T(8,128)S(1)}, f32[62,8,128]{2,1,0:T(8,128)S(1)}, u32[]{:S(2)}, u32[]{:S(2)}) collective-permute-start(f32[62,8,128]{2,1,0:T(8,128)S(1)} %get-tuple-element.48), channel_id=1, source_target_pairs={{8,0},{16,8},{24,16},{32,24},{40,32},{48,40},{56,48},{9,1},{17,9},... | collective-permute-start | bytes 761864 | tf_op jit(solution)/shard_map/ppermute | solution.py:642
  41.4 5.8 %collective-permute-start.6 = (f32[25,8,128]{2,1,0:T(8,128)S(1)}, f32[25,8,128]{2,1,0:T(8,128)S(1)}, u32[]{:S(2)}, u32[]{:S(2)}) collective-permute-start(f32[25,8,128]{2,1,0:T(8,128)S(1)} %get-tuple-element.66), channel_id=1, source_target_pairs={{0,8},{8,16},{16,24},{24,32},{32,40},{40,48},{48,56},{1,9},{9,17},... | collective-permute-start | bytes 307208 | tf_op jit(solution)/shard_map/ppermute | solution.py:662
  44.8 6.3 %collective-permute-start.7 = (f32[25,8,128]{2,1,0:T(8,128)S(1)}, f32[25,8,128]{2,1,0:T(8,128)S(1)}, u32[]{:S(2)}, u32[]{:S(2)}) collective-permute-start(f32[25,8,128]{2,1,0:T(8,128)S(1)} %get-tuple-element.67), channel_id=1, source_target_pairs={{8,0},{16,8},{24,16},{32,24},{40,32},{48,40},{56,48},{9,1},{17,9},... | collective-permute-start | bytes 307208 | tf_op jit(solution)/shard_map/ppermute | solution.py:663

commit v6 on v5

--- a/solution.py
+++ b/solution.py
@@ -177,7 +177,7 @@
             send[part, tile] = tiles[tile]
 
 
-def rows_kernel(got, plate, left, right, from_left, from_right, up, down, plate_window):
+def plate_window_kernel(plate, left, right, from_left, from_right, plate_window):
     lane = lanes_of((OWN, LANES))
     first = lax.axis_index("vert") == 0
     last = lax.axis_index("vert") == lax.axis_size("vert") - 1
@@ -192,8 +192,11 @@
     here = jnp.where(late, tiles[1], tiles[0])
     there = jnp.where(late, tiles[2], tiles[1])
     back = (LANES - shift) % LANES
-    window = jnp.where(lane < LANES - shift, pltpu.roll(here, back, 1), pltpu.roll(there, back, 1))
-    plate_window[...] = window
+    plate_window[...] = jnp.where(lane < LANES - shift, pltpu.roll(here, back, 1), pltpu.roll(there, back, 1))
+
+
+def rows_kernel(got, plate_window, up, down):
+    window = plate_window[...]
     for index in range(TILES + 1):
         values = got[index // 5, index % 5] if index < TILES else window
         at = TILES + 1 + index // 2
@@ -635,9 +638,8 @@
     )(vel, log, layer_dir)
     send = call(patch_kernel, sds(8, 5, OWN, LANES))(send, left, right, from_left, from_right)
     got = lax.all_to_all(send, "row", 0, 0, tiled=True)
-    up, down, plate_window = call(rows_kernel, (sds(62, 8, LANES), sds(62, 8, LANES), tile))(
-        got, plate, plate_left, plate_right, plate_before, plate_after
-    )
+    plate_window = call(plate_window_kernel, tile)(plate, plate_left, plate_right, plate_before, plate_after)
+    up, down = call(rows_kernel, (sds(62, 8, LANES), sds(62, 8, LANES)))(got, plate_window)
     from_low = lax.ppermute(up, "au", upward)
     from_high = lax.ppermute(down, "au", downward)
     fine = sds(LAYERS, WINDOW, LANES)

time: 95.8 us -> 95.7 us (level)
  no operation moved by 1% of the time
where the time goes in v6:
time: 95.7 us; the launch traced here: 95.2 us
  blocking collectives  41.2 us (43%)
  starting transfers between devices  26.3 us (27%)
  waiting for transfers between devices  15.4 us (16%)
  Pallas kernels  10.8 us (11%)
    all_to_all x1, blocking collectives, shards(): parts = lax.all_to_all(spread, ('au', 'vert'), 0, 0, tiled=True)  30.5 us
    all_to_all x1, blocking collectives, shards(): got = lax.all_to_all(send, 'row', 0, 0, tiled=True)  10.7 us
    ppermute x1, starting transfers between devices, shards(): from_right = lax.ppermute(left, 'vert', back)  6.89 us
    all_to_all x1, starting transfers between devices, shards(): got = lax.all_to_all(send, 'row', 0, 0, tiled=True)  6.19 us
    all_to_all x1, waiting for transfers between devices, shards(): got = lax.all_to_all(send, 'row', 0, 0, tiled=True)  4.61 us
    ppermute x1, starting transfers between devices, shards(): plate_after = lax.ppermute(plate_left, 'vert', back)  3.99 us
    ppermute x1, waiting for transfers between devices, shards(): from_high = lax.ppermute(f_down, 'au', downward)  3.93 us
    ppermute x1, waiting for transfers between devices, shards(): from_high = lax.ppermute(down, 'au', downward)  3.83 us
  transfers between devices with their start and end apart: 9, of which 6 were waited for; matrix products, arithmetic and copies ran while one was open for 0% of the time, Pallas kernels for 2%

profile of v6, /device:TPU:1, one launch (start us, length us, event | category | flops | bytes accessed | tf_op | source)
XLA Modules:
  0.0 95.2 jit_solution(16332180619678120096)
XLA Ops:
  0.6 1.0 %shard_map.84 = (f32[2,16,128]{2,1,0:T(8,128)S(1)}, f32[2,16,128]{2,1,0:T(8,128)S(1)}, f32[4,16,256]{2,1,0:T(8,128)S(1)}, f32[4,16,256]{2,1,0:T(8,128)S(1)}) custom-call(f32[4,16,256]{2,1,0:T(8,128)} %vel_in.1, f32[4,16,256]{2,1,0:T(8,128)} %log_in.1), custom_call_target="tpu_custom_call" | custom-call | tf_op jit(solution)/shard_map/pallas_call | solution.py:620
  1.6 6.9 %collective-permute-start.1 = (f32[2,16,128]{2,1,0:T(8,128)S(1)}, f32[2,16,128]{2,1,0:T(8,128)S(1)}, u32[]{:S(2)}, u32[]{:S(2)}) collective-permute-start(f32[2,16,128]{2,1,0:T(8,128)S(1)} %get-tuple-element.40.left), channel_id=1, source_target_pairs={{1,0},{2,1},{3,2},{4,3},{5,4},{6,5},{7,6},{0,7},{9,8},{10,9},{11,1... | collective-permute-start | bytes 49160 | tf_op jit(solution)/shard_map/ppermute | solution.py:628
  8.5 0.0 collective-permute-start
  8.5 0.0 copy-start.2
  8.5 0.7 copy-done.2
  9.2 0.8 shard_map.85.sent
  10.0 0.0 collective-permute-done.1.from_right
  10.0 0.0 collective-permute-done.from_left
  10.0 0.9 shard_map.86
  10.9 0.0 copy-start
  10.9 0.0 copy-start.1
  10.9 6.2 %all-to-all-start = ((f32[8,5,16,128]{3,2,1,0:T(8,128)}), f32[8,5,16,128]{3,2,1,0:T(8,128)S(1)}, u32[]{:S(2)}, u32[]{:S(2)}) async-start(f32[8,5,16,128]{3,2,1,0:T(8,128)} %shard_map.86), calls=%async_computation | async-start | bytes 655360 | tf_op jit(solution)/shard_map/all_to_all | solution.py:640
  17.1 0.0 copy-done
  17.1 0.0 copy-done.1
  17.1 0.1 shard_map.87
  17.2 4.0 %collective-permute-start.3 = (f32[16,128]{1,0:T(8,128)S(1)}, f32[16,128]{1,0:T(8,128)S(1)}, u32[]{:S(2)}, u32[]{:S(2)}) collective-permute-start(f32[16,128]{1,0:T(8,128)S(1)} %get-tuple-element.43.left), channel_id=1, source_target_pairs={{1,0},{2,1},{3,2},{4,3},{5,4},{6,5},{7,6},{0,7},{9,8},{10,9},{11,1... | collective-permute-start | bytes 24584 | tf_op jit(solution)/shard_map/ppermute | solution.py:633
  21.2 0.0 collective-permute-start.2
  21.2 0.8 collective-permute-done.3.from_right
  22.0 0.3 collective-permute-done.2.from_left
  22.4 0.2 shard_map.88.plate_window
  22.6 4.6 %all-to-all-done.got = f32[8,5,16,128]{3,2,1,0:T(8,128)S(1)} async-done(((f32[8,5,16,128]{3,2,1,0:T(8,128)}), f32[8,5,16,128]{3,2,1,0:T(8,128)S(1)}, u32[]{:S(2)}, u32[]{:S(2)}) %all-to-all-start) | async-done | bytes 327712 | tf_op jit(solution)/shard_map/all_to_all | solution.py:640
  27.2 3.2 %collective-permute-start.4 = (f32[62,8,128]{2,1,0:T(8,128)S(1)}, f32[62,8,128]{2,1,0:T(8,128)S(1)}, u32[]{:S(2)}, u32[]{:S(2)}) collective-permute-start(f32[62,8,128]{2,1,0:T(8,128)S(1)} %get-tuple-element.45), channel_id=1, source_target_pairs={{0,8},{8,16},{16,24},{24,32},{32,40},{40,48},{48,56},{1,9},{9,17},... | collective-permute-start | bytes 761864 | tf_op jit(solution)/shard_map/ppermute | solution.py:643
  30.5 1.3 %collective-permute-start.5 = (f32[62,8,128]{2,1,0:T(8,128)S(1)}, f32[62,8,128]{2,1,0:T(8,128)S(1)}, u32[]{:S(2)}, u32[]{:S(2)}) collective-permute-start(f32[62,8,128]{2,1,0:T(8,128)S(1)} %get-tuple-element.46), channel_id=1, source_target_pairs={{8,0},{16,8},{24,16},{32,24},{40,32},{48,40},{56,48},{9,1},{17,9},... | collective-permute-start | bytes 761864 | tf_op jit(solution)/shard_map/ppermute | solution.py:644
  31.8 1.9 %collective-permute-done.4.from_low = f32[62,8,128]{2,1,0:T(8,128)S(1)} collective-permute-done((f32[62,8,128]{2,1,0:T(8,128)S(1)}, f32[62,8,128]{2,1,0:T(8,128)S(1)}, u32[]{:S(2)}, u32[]{:S(2)}) %collective-permute-start.4) | collective-permute-done | bytes 253984 | tf_op jit(solution)/shard_map/ppermute | solution.py:643
  33.7 3.8 %collective-permute-done.5.from_high = f32[62,8,128]{2,1,0:T(8,128)S(1)} collective-permute-done((f32[62,8,128]{2,1,0:T(8,128)S(1)}, f32[62,8,128]{2,1,0:T(8,128)S(1)}, u32[]{:S(2)}, u32[]{:S(2)}) %collective-permute-start.5) | collective-permute-done | bytes 253984 | tf_op jit(solution)/shard_map/ppermute | solution.py:644
  37.5 3.7 %shard_map.90 = (f32[34,56,128]{2,1,0:T(8,128)S(1)}, f32[32,40,128]{2,1,0:T(8,128)S(1)}, f32[32,40,128]{2,1,0:T(8,128)S(1)}, f32[16,24,128]{2,1,0:T(8,128)S(1)},...) custom-call(f32[8,5,16,128]{3,2,1,0:T(8,128)S(1)} %all-to-all-done.g, ...), custom_call_target="tpu_custom_call" | custom-call | tf_op jit(solution)/shard_map/pallas_call | solution.py:656
  41.2 3.5 %collective-permute-start.6 = (f32[25,8,128]{2,1,0:T(8,128)S(1)}, f32[25,8,128]{2,1,0:T(8,128)S(1)}, u32[]{:S(2)}, u32[]{:S(2)}) collective-permute-start(f32[25,8,128]{2,1,0:T(8,128)S(1)} %get-tuple-element.64), channel_id=1, source_target_pairs={{0,8},{8,16},{16,24},{24,32},{32,40},{40,48},{48,56},{1,9},{9,17},... | collective-permute-start | bytes 307208 | tf_op jit(solution)/shard_map/ppermute | solution.py:664
  44.7 1.3 %collective-permute-start.7 = (f32[25,8,128]{2,1,0:T(8,128)S(1)}, f32[25,8,128]{2,1,0:T(8,128)S(1)}, u32[]{:S(2)}, u32[]{:S(2)}) collective-permute-start(f32[25,8,128]{2,1,0:T(8,128)S(1)} %get-tuple-element.65), channel_id=1, source_target_pairs={{8,0},{16,8},{24,16},{32,24},{40,32},{48,40},{56,48},{9,1},{17,9},... | collective-permute-start | bytes 307208 | tf_op jit(solution)/shard_map/ppermute | solution.py:665
  46.0 1.1 %shard_map.91 = (f32[8,16,128]{2,1,0:T(8,128)S(1)}, bf16[128,2048]{1,0:T(8,128)(2,1)S(1)}, f32[18,40,128]{2,1,0:T(8,128)S(1)}, f32[16,40,128]{2,1,0:T(8,128)S(1)...) custom-call(f32[34,56,128]{2,1,0:T(8,128)S(1)} %get-tuple-element.47, ...), custom_call_target="tpu_custom_call" | custom-call | tf_op jit(solution)/shard_map/pallas_call | solution.py:669
  47.0 0.0 collective-permute-done.6.from_low
  47.0 3.9 %collective-permute-done.7.from_high = f32[25,8,128]{2,1,0:T(8,128)S(1)} collective-permute-done((f32[25,8,128]{2,1,0:T(8,128)S(1)}, f32[25,8,128]{2,1,0:T(8,128)S(1)}, u32[]{:S(2)}, u32[]{:S(2)}) %collective-permute-start.7) | collective-permute-done | bytes 102432 | tf_op jit(solution)/shard_map/ppermute | solution.py:665
  51.0 2.1 %shard_map.92 = f32[8,40,128]{2,1,0:T(8,128)S(1)} custom-call(f32[18,40,128]{2,1,0:T(8,128)S(1)} %get-tuple-element.56.g, f32[16,40,128]{2,1,0:T(8,128)S(1)} %get-tuple-element.57.c, f32[16,40,128]{2,1,0:T(8,128)S(1)} %get-tuple-element.58.big, f32[8,24,128]{2,1,0:T(8,128)S(1)} %get-tuple-element.59.cc, f32[8,24,128]{2,1,0:T(8,128)S(1)} %get-tuple-element.60.kc, ...), custom_call_target="tpu_custom_call" | custom-call | tf_op jit(solution)/shard_map/pallas_call | solution.py:674
  53.1 10.7 %all_to_all.15.got = f32[8,40,128]{2,1,0:T(8,128)S(1)} all-to-all(f32[8,40,128]{2,1,0:T(8,128)S(1)} %shard_map.92), channel_id=1, replica_groups=mesh['row'=8,'au'=8,'vert'=8] {'row'}, dimensions={0} | all-to-all | bytes 327680 | tf_op jit(solution)/shard_map/all_to_all | solution.py:677
  63.7 0.1 shard_map.93
  63.9 30.5 %all_to_all.16.parts = f32[64,1,640]{2,1,0:T(1,128)S(1)} all-to-all(f32[64,1,640]{2,1,0:T(1,128)S(1)} %shard_map.93), channel_id=1, replica_groups=mesh['row'=8,'au'=8,'vert'=8] {'au','vert'}, dimensions={0} | all-to-all | bytes 327680 | tf_op jit(solution)/shard_map/all_to_all | solution.py:679
  94.4 0.8 shard_map.94
  (1 shorter events, 0.0 us)
Async XLA Ops:
  1.6 8.3 %collective-permute-start.1 = (f32[2,16,128]{2,1,0:T(8,128)S(1)}, f32[2,16,128]{2,1,0:T(8,128)S(1)}, u32[]{:S(2)}, u32[]{:S(2)}) collective-permute-start(f32[2,16,128]{2,1,0:T(8,128)S(1)} %get-tuple-element.40.left), channel_id=1, source_target_pairs={{1,0},{2,1},{3,2},{4,3},{5,4},{6,5},{7,6},{0,7},{9,8},{10,9},{11,1... | collective-permute-start | bytes 49160 | tf_op jit(solution)/shard_map/ppermute | solution.py:628
  8.5 1.5 %collective-permute-start = (f32[2,16,128]{2,1,0:T(8,128)S(1)}, f32[2,16,128]{2,1,0:T(8,128)S(1)}, u32[]{:S(2)}, u32[]{:S(2)}) collective-permute-start(f32[2,16,128]{2,1,0:T(8,128)S(1)} %get-tuple-element.41.right), channel_id=1, source_target_pairs={{0,1},{1,2},{2,3},{3,4},{4,5},{5,6},{6,7},{7,0},{8,9},{9,10},{10,1... | collective-permute-start | bytes 49160 | tf_op jit(solution)/shard_map/ppermute | solution.py:627
  8.5 0.7 copy-start.2
  10.9 6.2 %copy-start = (s32[16,256]{1,0:T(8,128)S(1)}, s32[16,256]{1,0:T(8,128)}, u32[]{:S(2)}) copy-start(s32[16,256]{1,0:T(8,128)} %lab.1) | copy-start | bytes 49156
  10.9 6.2 %copy-start.1 = (f32[512]{0:T(512)S(1)}, f32[512]{0:T(512)}, u32[]{:S(2)}) copy-start(f32[512]{0:T(512)} %param.8) | copy-start | bytes 6148
  10.9 16.3 %all-to-all-start = ((f32[8,5,16,128]{3,2,1,0:T(8,128)}), f32[8,5,16,128]{3,2,1,0:T(8,128)S(1)}, u32[]{:S(2)}, u32[]{:S(2)}) async-start(f32[8,5,16,128]{3,2,1,0:T(8,128)} %shard_map.86), calls=%async_computation | async-start | bytes 655360 | tf_op jit(solution)/shard_map/all_to_all | solution.py:640
  17.2 4.8 %collective-permute-start.3 = (f32[16,128]{1,0:T(8,128)S(1)}, f32[16,128]{1,0:T(8,128)S(1)}, u32[]{:S(2)}, u32[]{:S(2)}) collective-permute-start(f32[16,128]{1,0:T(8,128)S(1)} %get-tuple-element.43.left), channel_id=1, source_target_pairs={{1,0},{2,1},{3,2},{4,3},{5,4},{6,5},{7,6},{0,7},{9,8},{10,9},{11,1... | collective-permute-start | bytes 24584 | tf_op jit(solution)/shard_map/ppermute | solution.py:633
  21.2 1.2 %collective-permute-start.2 = (f32[16,128]{1,0:T(8,128)S(1)}, f32[16,128]{1,0:T(8,128)S(1)}, u32[]{:S(2)}, u32[]{:S(2)}) collective-permute-start(f32[16,128]{1,0:T(8,128)S(1)} %get-tuple-element.44.right), channel_id=1, source_target_pairs={{0,1},{1,2},{2,3},{3,4},{4,5},{5,6},{6,7},{7,0},{8,9},{9,10},{10,1... | collective-permute-start | bytes 24584 | tf_op jit(solution)/shard_map/ppermute | solution.py:632
  27.2 6.4 %collective-permute-start.4 = (f32[62,8,128]{2,1,0:T(8,128)S(1)}, f32[62,8,128]{2,1,0:T(8,128)S(1)}, u32[]{:S(2)}, u32[]{:S(2)}) collective-permute-start(f32[62,8,128]{2,1,0:T(8,128)S(1)} %get-tuple-element.45), channel_id=1, source_target_pairs={{0,8},{8,16},{16,24},{24,32},{32,40},{40,48},{48,56},{1,9},{9,17},... | collective-permute-start | bytes 761864 | tf_op jit(solution)/shard_map/ppermute | solution.py:643
  30.5 7.0 %collective-permute-start.5 = (f32[62,8,128]{2,1,0:T(8,128)S(1)}, f32[62,8,128]{2,1,0:T(8,128)S(1)}, u32[]{:S(2)}, u32[]{:S(2)}) collective-permute-start(f32[62,8,128]{2,1,0:T(8,128)S(1)} %get-tuple-element.46), channel_id=1, source_target_pairs={{8,0},{16,8},{24,16},{32,24},{40,32},{48,40},{56,48},{9,1},{17,9},... | collective-permute-start | bytes 761864 | tf_op jit(solution)/shard_map/ppermute | solution.py:644
  41.2 5.8 %collective-permute-start.6 = (f32[25,8,128]{2,1,0:T(8,128)S(1)}, f32[25,8,128]{2,1,0:T(8,128)S(1)}, u32[]{:S(2)}, u32[]{:S(2)}) collective-permute-start(f32[25,8,128]{2,1,0:T(8,128)S(1)} %get-tuple-element.64), channel_id=1, source_target_pairs={{0,8},{8,16},{16,24},{24,32},{32,40},{40,48},{48,56},{1,9},{9,17},... | collective-permute-start | bytes 307208 | tf_op jit(solution)/shard_map/ppermute | solution.py:664
  44.7 6.3 %collective-permute-start.7 = (f32[25,8,128]{2,1,0:T(8,128)S(1)}, f32[25,8,128]{2,1,0:T(8,128)S(1)}, u32[]{:S(2)}, u32[]{:S(2)}) collective-permute-start(f32[25,8,128]{2,1,0:T(8,128)S(1)} %get-tuple-element.65), channel_id=1, source_target_pairs={{8,0},{16,8},{24,16},{32,24},{40,32},{48,40},{56,48},{9,1},{17,9},... | collective-permute-start | bytes 307208 | tf_op jit(solution)/shard_map/ppermute | solution.py:665
